TPU v7x, 512 devices: a whole 4x8x8 slice. The times are simulated.
512 devices in a mesh: grp: 8 (over z_lo, core), seg: 64 (over y, z_hi, x).
Axes of the slice: x: 4, y: 8, z: 8 (z_hi: 2, z_lo: 4; z = z_hi * 4 + z_lo), core: 2. Of those that a mesh axis runs over, the one named last changes fastest.
Arguments:
- queries: bfloat16 [98304, 2048], P(('seg', 'grp')), may hold values from -8 to 8
- keys: bfloat16 [98304, 2048], P(('seg', 'grp')), may hold values from -8 to 8
- values: bfloat16 [98304, 2048], P(('seg', 'grp')), may hold values from -6 to 6
- offsets_two: int32 [32], replicated, may hold values from 0 to 7
- offsets_three: int32 [32], replicated, may hold values from 0 to 63
- w_out: bfloat16 [2048, 2048], P('seg'), may hold values from -0.125 to 0.125
Outputs:
- mixed: bfloat16 [98304, 2048], P(('seg', 'grp'))
All inputs are finite; a program needn't handle non-finite values.
Results may differ from a plain program's by a relative error of at most 0.0056.
Values may be sent and summed in bfloat16 or wider, within the bound.
No kernel may reach another device: no remote copies, remote signals or barrier semaphores. Data moves between devices by JAX's collectives and lax.ppermute only.
A program may use at most 128 MiB of HBM per device.

v0:
```python
import math

import jax
import jax.numpy as jnp
from jax import lax
from jax.sharding import PartitionSpec as P

H = 32
HD = 64
R2 = 8
R3 = 64
SPAN = 8


def partner(value, axis, bit):
    mask = 2**bit
    pairs = [(source, source ^ mask) for source in range(lax.axis_size(axis))]
    return lax.ppermute(value, axis, pairs)


def attend(query_heads, key_heads, value_heads):
    count = query_heads.shape[0]
    heads = query_heads.shape[1]
    block = math.gcd(count, 512)
    scale = HD ** (-0.5)

    def one_head(items):
        head_q, head_k, head_v = items

        def one_block(block_q):
            scores = jnp.dot(block_q, head_k.T, preferred_element_type=jnp.float32) * scale
            largest = jnp.max(scores, axis=-1)
            expo = jnp.exp(scores - largest[:, None])
            totals = jnp.sum(expo, axis=-1)
            outputs = (
                jnp.dot(expo.astype(jnp.bfloat16), head_v, preferred_element_type=jnp.float32)
                / totals[:, None]
            )
            return (largest, totals, outputs)

        return lax.map(one_block, head_q.reshape(count // block, block, head_q.shape[1]))

    largest, totals, outputs = lax.map(
        one_head,
        (
            jnp.moveaxis(query_heads, 1, 0),
            jnp.moveaxis(key_heads, 1, 0),
            jnp.moveaxis(value_heads, 1, 0),
        ),
    )
    return (
        largest.reshape(heads, count).T,
        totals.reshape(heads, count).T,
        jnp.moveaxis(outputs.reshape(heads, count, HD), 0, 1),
    )


def choose_rows(matrix, offsets, rate):
    heads = offsets.shape[0]
    count = matrix.shape[0] // rate
    shaped = matrix.reshape(count, rate, heads, HD)
    select = (lax.iota(jnp.int32, rate)[:, None] == offsets[None, :]).astype(jnp.bfloat16)
    picked = jnp.einsum("nrhe,rh->nhe", shaped, select, preferred_element_type=jnp.float32)
    return picked.astype(jnp.bfloat16).reshape(count, heads * HD)


def spread_level(level, offsets, rate):
    largest, totals, outputs = level
    count, heads = largest.shape
    row_count = count * rate
    big_largest = jnp.broadcast_to(largest[:, None], (count, rate, heads)).reshape(row_count, heads)
    big_totals = jnp.broadcast_to(totals[:, None], (count, rate, heads)).reshape(row_count, heads)
    big_outputs = jnp.broadcast_to(outputs[:, None], (count, rate, heads, HD)).reshape(
        row_count, heads, HD
    )
    cover = (lax.iota(jnp.int32, row_count) % rate)[:, None] == offsets[None, :]
    return (big_largest, big_totals, big_outputs, cover)


def combine(levels):
    peak = levels[0][0]
    for level in levels[1:]:
        peak = jnp.maximum(peak, jnp.where(level[3], level[0], peak))
    weight_sum = jnp.zeros_like(peak)
    summed = jnp.zeros_like(levels[0][2])
    for largest, totals, outputs, cover in levels:
        weight = jnp.where(cover, totals * jnp.exp(jnp.where(cover, largest, peak) - peak), 0.0)
        weight_sum = weight_sum + weight
        summed = summed + weight[..., None] * outputs
    return summed / weight_sum[..., None]


def heads_view(matrix):
    return matrix.reshape(matrix.shape[0], matrix.shape[1] // HD, HD)


def local(queries, keys, values, offsets_two, offsets_three, w_out):
    local_heads = H // lax.axis_size("grp")
    width = local_heads * HD
    head_q, head_k, head_v = (
        lax.all_to_all(queries, "grp", split_axis=1, concat_axis=0, tiled=True),
        lax.all_to_all(keys, "grp", split_axis=1, concat_axis=0, tiled=True),
        lax.all_to_all(values, "grp", split_axis=1, concat_axis=0, tiled=True),
    )
    rows = head_q.shape[0]
    first_head = lax.axis_index("grp") * local_heads
    own_two = lax.dynamic_slice_in_dim(offsets_two, first_head, local_heads)
    own_three = lax.dynamic_slice_in_dim(offsets_three, first_head, local_heads)
    first = attend(heads_view(head_q), heads_view(head_k), heads_view(head_v))
    level_one = (first[0], first[1], first[2], jnp.ones((rows, local_heads), jnp.bool_))
    query_two = choose_rows(head_q, own_two, R2)
    key_two = choose_rows(head_k, own_two, R2)
    value_two = choose_rows(head_v, own_two, R2)
    steps_count = SPAN.bit_length() - 1
    bit_list = list(range(steps_count))
    place = lax.axis_index("seg")
    for bit in bit_list:
        other_key, other_value = partner((key_two, value_two), "seg", bit)
        upper = place // 2**bit % 2 == 1
        key_two = jnp.where(
            upper,
            jnp.concatenate([other_key, key_two], 0),
            jnp.concatenate([key_two, other_key], 0),
        )
        value_two = jnp.where(
            upper,
            jnp.concatenate([other_value, value_two], 0),
            jnp.concatenate([value_two, other_value], 0),
        )
    second = attend(heads_view(query_two), heads_view(key_two), heads_view(value_two))
    level_two = spread_level(second, own_two, R2)
    query_three = choose_rows(head_q, own_three, R3)
    key_three = choose_rows(head_k, own_three, R3)
    value_three = choose_rows(head_v, own_three, R3)
    far_keys, far_values = (
        lax.all_gather(key_three, "seg", axis=0, tiled=True),
        lax.all_gather(value_three, "seg", axis=0, tiled=True),
    )
    third = attend(heads_view(query_three), heads_view(far_keys), heads_view(far_values))
    level_three = spread_level(third, own_three, R3)
    attention_heads = (
        combine([level_one, level_two, level_three]).reshape(rows, width).astype(jnp.bfloat16)
    )
    attention = lax.all_to_all(attention_heads, "grp", split_axis=0, concat_axis=1, tiled=True)
    mixed = jnp.dot(
        attention,
        lax.all_gather(w_out, "seg", axis=0, tiled=True),
        preferred_element_type=jnp.float32,
    )
    return mixed.astype(jnp.bfloat16)


def solution(mesh):
    placed = (
        P(("seg", "grp"), None),
        P(("seg", "grp"), None),
        P(("seg", "grp"), None),
        P(),
        P(),
        P("seg", None),
    )
    return jax.shard_map(
        local, mesh=mesh, in_specs=placed, out_specs=P(("seg", "grp"), None), check_vma=False
    )
```

profile of v0, /device:TPU:1, one launch (start us, length us, event | category | flops | bytes accessed | tf_op | source)
XLA Modules:
  0.0 756.3 jit_solution(2338546668515450154)
XLA Ops:
  8.7 10.3 %all-to-all-start.1 = ((bf16[192,8,256]{2,0,1:T(8,128)(2,1)}), bf16[192,8,256]{2,0,1:T(8,128)(2,1)S(1)}, u32[]{:S(2)}, u32[]{:S(2)}) async-start(bf16[192,8,256]{2,0,1:T(8,128)(2,1)} %bitcast.208), calls=%async_computation.1 | async-start | bytes 1572864 | tf_op jit(solution)/shard_map/all_to_all | solution.py:102
  20.0 19.2 %all-to-all-done.1 = bf16[192,8,256]{2,0,1:T(8,128)(2,1)S(1)} async-done(((bf16[192,8,256]{2,0,1:T(8,128)(2,1)}), bf16[192,8,256]{2,0,1:T(8,128)(2,1)S(1)}, u32[]{:S(2)}, u32[]{:S(2)}) %all-to-all-start.1) | async-done | bytes 786464 | tf_op jit(solution)/shard_map/all_to_all | solution.py:102
  39.1 4.3 all-to-all-start.2
  44.4 19.2 %all-to-all-done.2 = bf16[192,8,256]{2,0,1:T(8,128)(2,1)S(1)} async-done(((bf16[192,8,256]{2,0,1:T(8,128)(2,1)}), bf16[192,8,256]{2,0,1:T(8,128)(2,1)S(1)}, u32[]{:S(2)}, u32[]{:S(2)}) %all-to-all-start.2) | async-done | bytes 786464 | tf_op jit(solution)/shard_map/all_to_all | solution.py:103
  63.6 4.3 all-to-all-start
  75.4 12.7 %all-to-all-done = bf16[192,8,256]{2,0,1:T(8,128)(2,1)S(1)} async-done(((bf16[192,8,256]{2,0,1:T(8,128)(2,1)}), bf16[192,8,256]{2,0,1:T(8,128)(2,1)S(1)}, u32[]{:S(2)}, u32[]{:S(2)}) %all-to-all-start) | async-done | bytes 786464 | tf_op jit(solution)/shard_map/all_to_all | solution.py:101
  96.4 7.6 %multiply_reduce_fusion = (bf16[4,192,64]{2,0,1:T(4,128)(2,1)}, bf16[4,192,64]{2,0,1:T(4,128)(2,1)S(1)}, bf16[4,192,64]{2,0,1:T(4,128)(2,1)}) fusion(f32[4,8]{0,1:T(8,128)S(1)} %fusion.63, bf16[192,8,4,64]{3,2,1,0:T(4,128)(2,1)} %reshape.200, bf16[192,8,4,64]{3,2,1,0:T(4,128)(2,1)} %reshape.198, bf16[192,8,4,64]{3,2,1,0:T(4,128)(2,1)} %reshape.197), kind=kLoop, calls=%fused_computation.52 | loop fusion | flops 3391488 | bytes 2654336
  108.0 3.4 collective-permute-start
  111.8 211.6 %all_gather.9 = bf16[1536,256]{1,0:T(8,128)(2,1)} all-gather(bf16[24,256]{1,0:T(8,128)(2,1)S(1)} %reshape.206), channel_id=1, replica_groups=mesh['grp'=8,'seg'=64] {'seg'}, dimensions={0}, use_global_device_ids=true | all-gather | bytes 798720 | tf_op jit(solution)/shard_map/all_gather | solution.py:136
  323.9 199.7 %all_gather.10 = bf16[1536,256]{1,0:T(8,128)(2,1)} all-gather(bf16[24,256]{1,0:T(8,128)(2,1)S(1)} %reshape.209), channel_id=1, replica_groups=mesh['grp'=8,'seg'=64] {'seg'}, dimensions={0}, use_global_device_ids=true | all-gather | bytes 798720 | tf_op jit(solution)/shard_map/all_gather | solution.py:137
  529.0 44.7 %while.85 = (s32[]{:T(128)}, f32[4,3,512]{2,1,0:T(4,128)}, f32[4,3,512]{2,1,0:T(4,128)}, f32[4,3,512,64]{2,3,1,0:T(8,128)}, bf16[4,1536,64]{1,2,0:T(8,128)(2,1)}...) while((s32[]{:T(128)}, f32[4,3,512]{2,1,0:T(4,128)}, ...), condition=%wide.region_5.6_spmd, body=%wide.region_0.5_spmd.sunk | while | flops 206076928 | bytes 13679926 | solution.py:43
  532.7 6.2 while.90
  543.8 6.2 while.90
  554.9 6.2 while.90
  566.1 6.2 while.90
  579.2 14.8 %while.89 = (s32[]{:T(128)}, f32[4,3,8]{2,1,0:T(4,128)S(1)}, f32[4,3,8]{2,1,0:T(4,128)S(1)}, f32[4,3,8,64]{3,2,1,0:T(8,128)}, bf16[4,24,64]{2,1,0:T(8,128)(2,1)S...) while((s32[]{:T(128)}, f32[4,3,8]{2,1,0:T(4,128)S(1)}, ...), condition=%wide.region_17.18_spmd, body=%wide.region_12.17_spmd.sunk | while | flops 3219956 | bytes 2547738 | solution.py:43
  579.8 2.5 while.92
  583.5 2.5 while.92
  587.2 2.5 while.92
  590.9 2.5 while.92
  603.5 2.7 copy.110
  607.5 4.9 collective-permute-start.1
  617.2 7.5 collective-permute-start.2
  627.9 6.0 collective-permute-done.2
  634.1 16.4 %while.87 = (s32[]{:T(128)}, f32[4,3,64]{2,1,0:T(4,128)S(1)}, f32[4,3,64]{2,1,0:T(4,128)S(1)}, f32[4,3,64,64]{3,2,1,0:T(8,128)}, bf16[4,192,64]{2,1,0:T(8,128)(2...) while((s32[]{:T(128)}, f32[4,3,64]{2,1,0:T(4,128)S(1)}, ...), condition=%wide.region_11.12_spmd, body=%wide.region_6.11_spmd.sunk | while | flops 25759616 | bytes 3796538 | solution.py:43
  634.7 2.9 while.91
  638.8 2.9 while.91
  642.9 2.9 while.91
  647.0 2.9 while.91
  655.2 2.9 fusion.44
  660.0 83.2 %all_to_all.64 = bf16[8,192,256]{2,1,0:T(8,128)(2,1)S(1)} all-to-all(bf16[8,192,256]{2,1,0:T(8,128)(2,1)S(1)} %copy.69), channel_id=1, replica_groups=mesh['grp'=8,'seg'=64] {'grp'}, dimensions={0} | all-to-all | bytes 1572864 | tf_op jit(solution)/shard_map/all_to_all | solution.py:144
  743.4 6.1 convolution_convert_fusion
  (444 shorter events, 135.2 us)
Async XLA Ops:
  6.5 12.5 %copy-start.9 = (bf16[192,2048]{1,0:T(8,128)(2,1)S(1)}, bf16[192,2048]{1,0:T(8,128)(2,1)}, u32[]{:S(2)}) copy-start(bf16[192,2048]{1,0:T(8,128)(2,1)} %param.20) | copy-start | bytes 2359300
  8.7 30.5 %all-to-all-start.1 = ((bf16[192,8,256]{2,0,1:T(8,128)(2,1)}), bf16[192,8,256]{2,0,1:T(8,128)(2,1)S(1)}, u32[]{:S(2)}, u32[]{:S(2)}) async-start(bf16[192,8,256]{2,0,1:T(8,128)(2,1)} %bitcast.208), calls=%async_computation.1 | async-start | bytes 1572864 | tf_op jit(solution)/shard_map/all_to_all | solution.py:102
  19.0 24.5 %copy-start.10 = (bf16[192,2048]{1,0:T(8,128)(2,1)S(1)}, bf16[192,2048]{1,0:T(8,128)(2,1)}, u32[]{:S(2)}) copy-start(bf16[192,2048]{1,0:T(8,128)(2,1)} %param.18) | copy-start | bytes 2359300
  39.1 24.5 %all-to-all-start.2 = ((bf16[192,8,256]{2,0,1:T(8,128)(2,1)}), bf16[192,8,256]{2,0,1:T(8,128)(2,1)S(1)}, u32[]{:S(2)}, u32[]{:S(2)}) async-start(bf16[192,8,256]{2,0,1:T(8,128)(2,1)} %bitcast.207), calls=%async_computation.2 | async-start | bytes 1572864 | tf_op jit(solution)/shard_map/all_to_all | solution.py:103
  43.5 25.3 %copy-start.25 = (s32[32]{0:T(128)S(1)}, s32[32]{0:T(128)}, u32[]{:S(2)}) copy-start(s32[32]{0:T(128)} %param.21) | copy-start | bytes 388
  43.5 25.4 %copy-start.26 = (s32[32]{0:T(128)S(1)}, s32[32]{0:T(128)}, u32[]{:S(2)}) copy-start(s32[32]{0:T(128)} %param.22) | copy-start | bytes 388
  63.6 24.5 %all-to-all-start = ((bf16[192,8,256]{2,0,1:T(8,128)(2,1)}), bf16[192,8,256]{2,0,1:T(8,128)(2,1)S(1)}, u32[]{:S(2)}, u32[]{:S(2)}) async-start(bf16[192,8,256]{2,0,1:T(8,128)(2,1)} %bitcast.209), calls=%async_computation | async-start | bytes 1572864 | tf_op jit(solution)/shard_map/all_to_all | solution.py:101
  67.9 675.5 %all-gather.2.cloned.1.call-start = ((), (), s32[]{:S(2)}) async-start(), calls=%async_computation.4 | async-start | bytes 8519680 | tf_op jit(solution)/shard_map/all_gather | solution.py:147
  68.9 3.3 copy-start.21
  69.0 3.3 copy-start.23
  96.4 14.9 %copy-start.2 = (bf16[24,64,4,64]{3,2,1,0:T(4,128)(2,1)S(1)}, bf16[24,64,4,64]{3,2,1,0:T(4,128)(2,1)}, u32[]{:S(2)}) copy-start(bf16[24,64,4,64]{3,2,1,0:T(4,128)(2,1)} %reshape.205) | copy-start | bytes 2359300
  104.1 219.4 %copy-start.1 = (bf16[24,64,4,64]{3,2,1,0:T(4,128)(2,1)S(1)}, bf16[24,64,4,64]{3,2,1,0:T(4,128)(2,1)}, u32[]{:S(2)}) copy-start(bf16[24,64,4,64]{3,2,1,0:T(4,128)(2,1)} %reshape.208) | copy-start | bytes 2359300
  105.3 470.2 %collective-permute-start.3 = (bf16[192,256]{0,1:T(8,128)(2,1)S(1)}, bf16[192,256]{0,1:T(8,128)(2,1)}, u32[]{:S(2)}, u32[]{:S(2)}) collective-permute-start(bf16[192,256]{0,1:T(8,128)(2,1)S(1)} %bitcast.308), channel_id=1, source_target_pairs={{0,1},{1,0},{2,3},{3,2},{4,5},{5,4},{6,7},{7,6},{8,9},{9,8},{10,11... | collective-permute-start | bytes 294920 | tf_op jit(solution)/shard_map/ppermute | solution.py:18
  108.0 498.2 %collective-permute-start = (bf16[192,256]{0,1:T(8,128)(2,1)}, bf16[192,256]{0,1:T(8,128)(2,1)}, u32[]{:S(2)}, u32[]{:S(2)}) collective-permute-start(bf16[192,256]{0,1:T(8,128)(2,1)} %bitcast.45), channel_id=1, source_target_pairs={{0,1},{1,0},{2,3},{3,2},{4,5},{5,4},{6,7},{7,6},{8,9},{9,8},{10,11... | collective-permute-start | bytes 294920 | tf_op jit(solution)/shard_map/ppermute | solution.py:18
  111.8 411.8 %copy-start.3 = (bf16[8,192,256]{1,0,2:T(8,128)(2,1)S(1)}, bf16[8,192,256]{1,0,2:T(8,128)(2,1)}, u32[]{:S(2)}) copy-start(bf16[8,192,256]{1,0,2:T(8,128)(2,1)} %copy.52) | copy-start | bytes 2359300
  323.8 201.6 %copy-start.4 = (bf16[8,192,256]{1,0,2:T(8,128)(2,1)S(1)}, bf16[8,192,256]{1,0,2:T(8,128)(2,1)}, u32[]{:S(2)}) copy-start(bf16[8,192,256]{1,0,2:T(8,128)(2,1)} %copy.54) | copy-start | bytes 2359300
  529.0 44.7 %copy-start = (bf16[24,64,4,64]{3,2,1,0:T(4,128)(2,1)S(1)}, bf16[24,64,4,64]{3,2,1,0:T(4,128)(2,1)}, u32[]{:S(2)}) copy-start(bf16[24,64,4,64]{3,2,1,0:T(4,128)(2,1)} %reshape.204) | copy-start | bytes 2359300
  574.9 4.3 copy-start.18
  577.3 35.1 %collective-permute-start.4 = (bf16[384,256]{0,1:T(8,128)(2,1)}, bf16[384,256]{0,1:T(8,128)(2,1)}, u32[]{:S(2)}, u32[]{:S(2)}) collective-permute-start(bf16[384,256]{0,1:T(8,128)(2,1)} %maximum_select_fusion.8), channel_id=1, source_target_pairs={{0,2},{1,3},{2,0},{3,1},{4,6},{5,7},{6,4},{7,5},{8,10},{9,11},{10,... | collective-permute-start | bytes 589832 | tf_op jit(solution)/shard_map/ppermute | solution.py:18
  579.2 14.8 %copy-start.8 = (bf16[4,192,64]{2,0,1:T(4,128)(2,1)S(1)}, bf16[4,192,64]{2,0,1:T(4,128)(2,1)}, u32[]{:S(2)}) copy-start(bf16[4,192,64]{2,0,1:T(4,128)(2,1)} %get-tuple-element.313) | copy-start | bytes 294916
  607.5 9.7 %collective-permute-start.1 = (bf16[384,256]{0,1:T(8,128)(2,1)S(1)}, bf16[384,256]{0,1:T(8,128)(2,1)S(1)}, u32[]{:S(2)}, u32[]{:S(2)}) collective-permute-start(bf16[384,256]{0,1:T(8,128)(2,1)S(1)} %maximum_select_fusion.6), channel_id=1, source_target_pairs={{0,2},{1,3},{2,0},{3,1},{4,6},{5,7},{6,4},{7,5},{8,10},{9,11},{10,... | collective-permute-start | bytes 589832 | tf_op jit(solution)/shard_map/ppermute | solution.py:18
  613.7 14.0 %collective-permute-start.5 = (bf16[768,256]{0,1:T(8,128)(2,1)S(1)}, bf16[768,256]{0,1:T(8,128)(2,1)S(1)}, u32[]{:S(2)}, u32[]{:S(2)}) collective-permute-start(bf16[768,256]{0,1:T(8,128)(2,1)S(1)} %maximum_select_fusion.4), channel_id=1, source_target_pairs={{0,4},{1,5},{2,6},{3,7},{4,0},{5,1},{6,2},{7,3},{8,12},{9,13},{10,... | collective-permute-start | bytes 1179656 | tf_op jit(solution)/shard_map/ppermute | solution.py:18
  617.2 16.7 %collective-permute-start.2 = (bf16[768,256]{0,1:T(8,128)(2,1)S(1)}, bf16[768,256]{0,1:T(8,128)(2,1)S(1)}, u32[]{:S(2)}, u32[]{:S(2)}) collective-permute-start(bf16[768,256]{0,1:T(8,128)(2,1)S(1)} %maximum_select_fusion.2), channel_id=1, source_target_pairs={{0,4},{1,5},{2,6},{3,7},{4,0},{5,1},{6,2},{7,3},{8,12},{9,13},{10,... | collective-permute-start | bytes 1179656 | tf_op jit(solution)/shard_map/ppermute | solution.py:18
  627.7 6.4 copy-start.19
  627.7 6.4 copy-start.20
  650.5 2.2 copy-start.11
  652.9 2.2 copy-start.12
  652.9 2.2 copy-start.13
  652.9 2.2 copy-start.14
  652.9 2.2 copy-start.15
  652.9 2.2 copy-start.16
  652.9 2.2 copy-start.17
  (5 other events, 8.7 us)
Sparse Core Ops, SparseCore 0:
  73.2 203.4 all-gather.1
where the time goes:
time: 758 us; the launch traced here: 756 us
  blocking collectives  495 us (65%)
  local copies, waits for them, and re-layouts  78.2 us (10%)
  waiting for transfers between devices  59.5 us (8%)
  starting transfers between devices  40.4 us (5%)
  matrix products  37.6 us (5%)
  other arithmetic  30.6 us (4%)
  between operations  14 us (2%)
    all_gather x1, blocking collectives, local(): lax.all_gather(key_three, 'seg', axis=0, tiled=True)  212 us
    all_gather x1, blocking collectives, local(): lax.all_gather(value_three, 'seg', axis=0, tiled=True)  200 us
    all_to_all x1, blocking collectives, local(): lax.all_to_all(attention_heads, 'grp', split_axis=0, concat_axis=1, tiled...  83.2 us
    ppermute x6, starting transfers between devices, partner(): return lax.ppermute(value, axis, pairs)  21.5 us
    all_to_all x1, waiting for transfers between devices, local(): lax.all_to_all(values, 'grp', split_axis=1, concat_axis=0, tiled=True)  19.2 us
    all_to_all x1, waiting for transfers between devices, local(): lax.all_to_all(keys, 'grp', split_axis=1, concat_axis=0, tiled=True)  19.2 us
    dynamic_slice x60, local copies, waits for them, and re-layouts, attend(): lax.map(one_head, (jnp.moveaxis(query_heads, 1, 0), jnp.moveaxis(key_head...  18 us
    dot_general x36, matrix products, one_block(): jnp.dot(block_q, head_k.T, preferred_element_type=jnp.float32) * scale  16.1 us
  transfers between devices with their start and end apart: 10, of which 5 were waited for; matrix products, arithmetic and copies ran while one was open for 18% of the time, Pallas kernels for 0%

commit v1 on v0

v1 whole, which is shorter than its diff:
```python
import functools
import math

import jax
import jax.numpy as jnp
from jax import lax
from jax.experimental import pallas as pl
from jax.experimental.pallas import tpu as pltpu
from jax.sharding import Mesh
from jax.sharding import PartitionSpec as P

H = 32
HD = 64
R2 = 8
R3 = 64
D = H * HD
GRP = 8
ROWS = 192
SEG1 = ROWS * GRP
OWN = H // GRP
WIDTH = OWN * HD
N2 = SEG1 // R2
N3 = SEG1 // R3
PAD3 = 32
PICK = N2 + PAD3
BLOCK = 512
SCALE2 = HD**-0.5 * math.log2(math.e)
VMEM_LIMIT = 40 * 2**20
GROUP = ("zl", "core")
NT = (((1,), (1,)), ((), ()))


def fine_mesh(mesh):
    return Mesh(mesh.devices.reshape(4, 2, 8, 2, 4), ("zl", "core", "y", "zh", "x"))


def pack_kernel(k_ref, v_ref, out_ref):
    out_ref[0, :, :WIDTH] = k_ref[...]
    out_ref[0, :, WIDTH:] = v_ref[...]


def pack(keys, values):
    block = pl.BlockSpec((ROWS, WIDTH), lambda j: (0, j))
    return pl.pallas_call(
        pack_kernel,
        grid=(GRP,),
        in_specs=[block, block],
        out_specs=pl.BlockSpec((1, ROWS, 2 * WIDTH), lambda j: (j, 0, 0)),
        out_shape=jax.ShapeDtypeStruct((GRP, ROWS, 2 * WIDTH), jnp.bfloat16),
        name="pack_kv",
    )(keys, values)


def pick_kernel(off_ref, kv_ref, out_ref):
    row = lax.broadcasted_iota(jnp.int32, (PICK, SEG1), 0)
    col = lax.broadcasted_iota(jnp.int32, (PICK, SEG1), 1)
    lane = lax.broadcasted_iota(jnp.int32, (PICK, 2 * HD), 1)
    for pair in range(OWN // 2):
        parts = []
        for parity in range(2):
            head = 2 * pair + parity
            two = row * R2 + off_ref[head]
            three = (row - N2) * R3 + off_ref[OWN + head]
            target = jnp.where(row < N2, two, jnp.where(row < N2 + N3, three, -1))
            onehot = jnp.where(col == target, 1.0, 0.0).astype(jnp.bfloat16)
            parts.append(
                [
                    jnp.dot(
                        onehot,
                        kv_ref[:, base + pair * 2 * HD : base + (pair + 1) * 2 * HD],
                        preferred_element_type=jnp.float32,
                    )
                    for base in (0, WIDTH)
                ]
            )
        for which, base in enumerate((0, WIDTH)):
            chosen = jnp.where(lane < HD, parts[0][which], parts[1][which])
            out_ref[:, base + pair * 2 * HD : base + (pair + 1) * 2 * HD] = chosen.astype(jnp.bfloat16)


def pick(offsets, kv):
    return pl.pallas_call(
        pick_kernel,
        grid_spec=pltpu.PrefetchScalarGridSpec(
            num_scalar_prefetch=1,
            grid=(1,),
            in_specs=[pl.BlockSpec((SEG1, 2 * WIDTH), lambda i, off: (0, 0))],
            out_specs=pl.BlockSpec((PICK, 2 * WIDTH), lambda i, off: (0, 0)),
        ),
        out_shape=jax.ShapeDtypeStruct((PICK, 2 * WIDTH), jnp.bfloat16),
        compiler_params=pltpu.CompilerParams(vmem_limit_bytes=VMEM_LIMIT),
        cost_estimate=pl.CostEstimate(flops=4 * 10**9, bytes_accessed=2 * 10**6, transcendentals=0),
        name="pick_rows",
    )(offsets, kv)


def soft(scores):
    largest = jnp.max(scores, axis=-1, keepdims=True)
    return largest, jnp.exp2((scores - largest) * SCALE2).astype(jnp.bfloat16)


def attention_kernel(off_ref, q_ref, k_ref, v_ref, k2_ref, v2_ref, k3_ref, v3_ref, out_ref, acc, top, aug, aug2, aug3):
    pair = pl.program_id(0)
    for parity in range(2):
        head = 2 * pair + parity

        def mine(rows):
            lane = lax.broadcasted_iota(jnp.int32, (rows, 2 * HD), 1)
            return (lane >= HD) if parity else (lane < HD)

        one = jnp.ones((), jnp.bfloat16)
        aug[...] = jnp.where(mine(SEG1), v_ref[...], one)
        aug2[...] = jnp.where(mine(aug2.shape[0]), v2_ref[...], one)
        aug3[...] = jnp.where(mine(aug3.shape[0]), v3_ref[...], one)

        def level_one(block, carry):
            rows = pl.ds(pl.multiple_of(block * BLOCK, BLOCK), BLOCK)
            own_q = jnp.where(mine(BLOCK), q_ref[rows, :], jnp.zeros((), jnp.bfloat16))
            scores = lax.dot_general(own_q, k_ref[...], NT, preferred_element_type=jnp.float32)
            largest, expo = soft(scores)
            acc[rows, :] = jnp.dot(expo, aug[...], preferred_element_type=jnp.float32)
            top[rows, :] = jnp.broadcast_to(largest, (BLOCK, 2 * HD))
            return carry

        lax.fori_loop(0, SEG1 // BLOCK, level_one, 0)

        def sparse_level(count, used, rate, offset, far_k, far_v, period, valid):
            row = lax.broadcasted_iota(jnp.int32, (count, SEG1), 0)
            col = lax.broadcasted_iota(jnp.int32, (count, SEG1), 1)
            onehot = jnp.where(col == row * rate + offset, 1.0, 0.0).astype(jnp.bfloat16)
            own_q = jnp.dot(onehot, q_ref[...], preferred_element_type=jnp.float32)
            own_q = jnp.where(mine(count), own_q, 0.0).astype(jnp.bfloat16)
            scores = lax.dot_general(own_q, far_k[...], NT, preferred_element_type=jnp.float32)
            place = lax.broadcasted_iota(jnp.int32, (1, scores.shape[1]), 1)
            scores = jnp.where(lax.rem(place, period) < valid, scores, -1e30)
            largest, expo = soft(scores)
            part = jnp.dot(expo, far_v[...], preferred_element_type=jnp.float32)[:used]
            largest = jnp.broadcast_to(largest[:used], (used, 2 * HD))
            rows = pl.ds(offset, used, stride=rate)
            old_top = top[rows, :]
            peak = jnp.maximum(old_top, largest)
            top[rows, :] = peak
            acc[rows, :] = acc[rows, :] * jnp.exp2((old_top - peak) * SCALE2) + part * jnp.exp2((largest - peak) * SCALE2)

        sparse_level(N2, N2, R2, off_ref[head], k2_ref, aug2, PICK, N2)
        sparse_level(PAD3, N3, R3, off_ref[OWN + head], k3_ref, aug3, PAD3, N3)
        full = acc[...]
        result = (full / pltpu.roll(full, HD, 1)).astype(jnp.bfloat16)
        if parity == 0:
            out_ref[...] = result
        else:
            out_ref[...] = jnp.where(mine(SEG1), result, out_ref[...])


def attend(offsets, q, kv, far_two, far_three):
    pairs = OWN // 2

    def spec(rows, shift):
        return pl.BlockSpec((rows, 2 * HD), lambda i, off: (0, i + shift))

    rows2, rows3 = far_two.shape[0], far_three.shape[0]
    return pl.pallas_call(
        attention_kernel,
        grid_spec=pltpu.PrefetchScalarGridSpec(
            num_scalar_prefetch=1,
            grid=(pairs,),
            in_specs=[
                spec(SEG1, 0),
                spec(SEG1, 0),
                spec(SEG1, pairs),
                spec(rows2, 0),
                spec(rows2, pairs),
                spec(rows3, 0),
                spec(rows3, pairs),
            ],
            out_specs=spec(SEG1, 0),
            scratch_shapes=[
                pltpu.VMEM((SEG1, 2 * HD), jnp.float32),
                pltpu.VMEM((SEG1, 2 * HD), jnp.float32),
                pltpu.VMEM((SEG1, 2 * HD), jnp.bfloat16),
                pltpu.VMEM((rows2, 2 * HD), jnp.bfloat16),
                pltpu.VMEM((rows3, 2 * HD), jnp.bfloat16),
            ],
        ),
        out_shape=jax.ShapeDtypeStruct((SEG1, WIDTH), jnp.bfloat16),
        compiler_params=pltpu.CompilerParams(vmem_limit_bytes=VMEM_LIMIT),
        cost_estimate=pl.CostEstimate(flops=20 * 10**9, bytes_accessed=8 * 10**6, transcendentals=10**7),
        name="attend_levels",
    )(offsets, q, kv, kv, far_two, far_two, far_three, far_three)


def project_kernel(att_ref, w_ref, out_ref):
    total = jnp.dot(att_ref[0], w_ref[0, :WIDTH], preferred_element_type=jnp.float32)
    for g in range(1, GRP):
        total += jnp.dot(att_ref[g], w_ref[0, g * WIDTH : (g + 1) * WIDTH], preferred_element_type=jnp.float32)
    out_ref[...] = total.astype(jnp.bfloat16)


def project(att, w_halves):
    columns = 512
    per_half = w_halves.shape[2] // columns
    return pl.pallas_call(
        project_kernel,
        grid=(D // columns,),
        in_specs=[
            pl.BlockSpec((GRP, ROWS, WIDTH), lambda j: (0, 0, 0)),
            pl.BlockSpec((1, D, columns), lambda j: (j // per_half, 0, j % per_half)),
        ],
        out_specs=pl.BlockSpec((ROWS, columns), lambda j: (0, j)),
        out_shape=jax.ShapeDtypeStruct((ROWS, D), jnp.bfloat16),
        compiler_params=pltpu.CompilerParams(vmem_limit_bytes=VMEM_LIMIT),
        cost_estimate=pl.CostEstimate(flops=2 * ROWS * D * D, bytes_accessed=10 * 10**6, transcendentals=0),
        name="project",
    )(att, w_halves)


def gather_weights(w_rows):
    half = D // 2
    core = lax.axis_index("core")
    mine = lax.dynamic_slice_in_dim(w_rows, core * half, half, axis=1)
    both = lax.all_gather(mine, "zh", axis=0, tiled=False)
    line = lax.all_gather(both, "x", axis=1, tiled=False)
    line = line.reshape(WIDTH, half)
    columns = lax.all_gather(line, "y", axis=0, tiled=True)
    return lax.all_gather(columns, "core", axis=0, tiled=False)


def local(queries, keys, values, offsets_two, offsets_three, w_out):
    first_head = lax.axis_index(GROUP) * OWN
    offsets = jnp.concatenate(
        [
            lax.dynamic_slice_in_dim(offsets_two, first_head, OWN),
            lax.dynamic_slice_in_dim(offsets_three, first_head, OWN),
        ]
    )
    exchange = functools.partial(lax.all_to_all, axis_name=GROUP, split_axis=0, concat_axis=0, tiled=True)
    kv = exchange(pack(keys, values)).reshape(SEG1, 2 * WIDTH)
    q = exchange(jnp.swapaxes(queries.reshape(ROWS, GRP, WIDTH), 0, 1)).reshape(SEG1, WIDTH)
    picked = pick(offsets, kv)
    other = lax.ppermute(picked, "zh", [(0, 1), (1, 0)])
    far_two = lax.all_gather(jnp.concatenate([picked, other], 0), "x", axis=0, tiled=True)
    near_three = far_two.reshape(8, PICK, 2 * WIDTH)[:, N2:].reshape(8 * PAD3, 2 * WIDTH)
    far_three = lax.all_gather(near_three, "y", axis=0, tiled=True)
    att = attend(offsets, q, kv, far_two, far_three)
    att = exchange(att.reshape(GRP, ROWS, WIDTH))
    return project(att, gather_weights(w_out))


def solution(mesh):
    rows = P(("y", "zh", "x", "zl", "core"), None)
    return jax.shard_map(
        local,
        mesh=fine_mesh(mesh),
        in_specs=(rows, rows, rows, P(), P(), P(("y", "zh", "x"), None)),
        out_specs=rows,
        check_vma=False,
    )
```

time: 758 us -> 293 us (0.39)
  blocking collectives: 495 us -> 75.7 us
  waiting for transfers between devices: 59.5 us -> 132 us
  local copies, waits for them, and re-layouts: 78.2 us -> 9.47 us
  Pallas kernels: 0 us -> 44.6 us
  matrix products: 37.6 us -> 0 us
  other arithmetic: 30.6 us -> 0.88 us
  starting transfers between devices: 40.4 us -> 16.9 us
    all_gather x2, blocking collectives: 411 us -> 20.5 us  [the longest x1 12.1 us: gather_weights(): line = lax.all_gather(both, 'x', axis=1, tiled=False)]
    all_gather x1 -> x4, waiting for transfers between devices: 0.02 us -> 84.5 us  [the longest x1 56.1 us: gather_weights(): columns = lax.all_gather(line, 'y', axis=0, tiled=True)]
    pallas_call x0 -> x4, Pallas kernels: none -> 44.6 us  [the longest x1 33.2 us: attend(): pl.pallas_call(attention_kernel, grid_spec=pltpu.PrefetchScalarGridSpec(n...]
    dot_general x76 -> x0, matrix products: 37.6 us -> none  [the longest x36 16.1 us: one_block(): jnp.dot(block_q, head_k.T, preferred_element_type=jnp.float32) * scale]
    all_to_all x1 -> x2, blocking collectives: 83.2 us -> 55.3 us  [the longest x1 29.4 us: local(): att = exchange(att.reshape(GRP, ROWS, WIDTH))]
    reshape x27 -> x1, local copies, waits for them, and re-layouts: 25.1 us -> 0.05 us  [local(): queries.reshape(ROWS, GRP, WIDTH)]
    dynamic_slice x62 -> x3, local copies, waits for them, and re-layouts: 18.2 us -> 0.16 us  [the longest x1 0.08 us: local(): lax.dynamic_slice_in_dim(offsets_three, first_head, OWN)]
    ppermute x6 -> x1, starting transfers between devices: 21.5 us -> 6.32 us  [local(): other = lax.ppermute(picked, 'zh', [(0, 1), (1, 0)])]
  transfers between devices with their start and end apart: 10 -> 6, of which waited for: 5 -> 5; matrix products, arithmetic and copies ran while one was open for 18% -> 1% of each run, Pallas kernels for 0% -> 11%
where the time goes in v1:
time: 293 us
  waiting for transfers between devices  132 us (45%)
  blocking collectives  75.7 us (26%)
  Pallas kernels  44.6 us (15%)
  starting transfers between devices  16.9 us (6%)
  between operations  13.2 us (5%)
  local copies, waits for them, and re-layouts  9.47 us (3%)
    all_gather x1, waiting for transfers between devices, gather_weights(): columns = lax.all_gather(line, 'y', axis=0, tiled=True)  56.1 us
    all_to_all x1, waiting for transfers between devices, local(): kv = exchange(pack(keys, values)).reshape(SEG1, 2 * WIDTH)  36.7 us
    pallas_call x1, Pallas kernels, attend(): pl.pallas_call(attention_kernel, grid_spec=pltpu.PrefetchScalarGridSpec(n...  33.2 us
    all_to_all x1, blocking collectives, local(): att = exchange(att.reshape(GRP, ROWS, WIDTH))  29.4 us
    all_to_all x1, blocking collectives, local(): exchange(jnp.swapaxes(queries.reshape(ROWS, GRP, WIDTH), 0, 1))  25.9 us
    all_gather x1, waiting for transfers between devices, local(): lax.all_gather(jnp.concatenate([picked, other], 0), 'x', axis=0, tiled=True)  14.4 us
    all_gather x1, waiting for transfers between devices, local(): far_three = lax.all_gather(near_three, 'y', axis=0, tiled=True)  14 us
    all_gather x1, blocking collectives, gather_weights(): line = lax.all_gather(both, 'x', axis=1, tiled=False)  12.1 us
  transfers between devices with their start and end apart: 6, of which 5 were waited for; matrix products, arithmetic and copies ran while one was open for 1% of the time, Pallas kernels for 11%

profile of v1, /device:TPU:1, one launch (start us, length us, event | category | flops | bytes accessed | tf_op | source)
XLA Modules:
  0.0 292.7 jit_solution(4365702013525004868)
XLA Ops:
  6.5 5.5 %pack_kv.1 = bf16[8,192,512]{2,1,0:T(8,128)(2,1)} custom-call(bf16[192,2048]{1,0:T(8,128)(2,1)} %k_ref.1, bf16[192,2048]{1,0:T(8,128)(2,1)} %v_ref.1), custom_call_target="tpu_custom_call" | custom-call | tf_op jit(solution)/shard_map/pack_kv/pallas_call | solution.py:44
  12.0 10.5 %all-to-all-start.1 = ((bf16[8,192,512]{2,1,0:T(8,128)(2,1)}), bf16[8,192,512]{2,1,0:T(8,128)(2,1)S(1)}, u32[]{:S(2)}, u32[]{:S(2)}) async-start(bf16[8,192,512]{2,1,0:T(8,128)(2,1)} %pack_kv.1), calls=%async_computation.1 | async-start | bytes 3145728 | tf_op jit(solution)/shard_map/all_to_all | solution.py:237
  22.5 0.1 dynamic_slice.10
  22.6 0.1 dynamic_slice.9
  22.7 0.1 pad_add_fusion.off_ref
  22.8 36.7 %all-to-all-done.1 = bf16[8,192,512]{2,1,0:T(8,128)(2,1)S(1)} async-done(((bf16[8,192,512]{2,1,0:T(8,128)(2,1)}), bf16[8,192,512]{2,1,0:T(8,128)(2,1)S(1)}, u32[]{:S(2)}, u32[]{:S(2)}) %all-to-all-start.1) | async-done | bytes 1572896 | tf_op jit(solution)/shard_map/all_to_all | solution.py:237
  59.5 2.3 pick_rows.1
  61.8 6.3 %collective-permute-start = (bf16[224,512]{1,0:T(8,128)(2,1)S(1)}, bf16[224,512]{1,0:T(8,128)(2,1)S(1)}, u32[]{:S(2)}, u32[]{:S(2)}) collective-permute-start(bf16[224,512]{1,0:T(8,128)(2,1)S(1)} %pick_rows.1), channel_id=1, source_target_pairs={{0,4},{4,0},{1,5},{5,1},{2,6},{6,2},{3,7},{7,3},{8,12},{12,8},{9,1... | collective-permute-start | bytes 688136 | tf_op jit(solution)/shard_map/ppermute | solution.py:240
  68.1 10.6 %collective-permute-done = bf16[224,512]{1,0:T(8,128)(2,1)S(1)} collective-permute-done((bf16[224,512]{1,0:T(8,128)(2,1)S(1)}, bf16[224,512]{1,0:T(8,128)(2,1)S(1)}, u32[]{:S(2)}, u32[]{:S(2)}) %collective-permute-start) | collective-permute-done | bytes 229408 | tf_op jit(solution)/shard_map/ppermute | solution.py:240
  78.8 0.8 pad_maximum_fusion
  79.6 0.0 all-gather.8.cloned.1.call-update
  79.6 0.0 all-gather.12.cloned.1.call-start
  79.7 8.4 %all-gather = bf16[64,1024]{1,0:T(8,128)(2,1)S(1)} all-gather(bf16[32,1024]{1,0:T(8,128)(2,1)S(1)} %constant_dynamic-slice_fusion), channel_id=2, replica_groups=mesh['zl'=4,'core'=2,'y'=8,'zh'=2,'x'=4] {'zh'}, dimensions={0}, use_global_device_ids=true | all-gather | bytes 196608 | tf_op jit(solution)/shard_map/all_gather | solution.py:221
  88.1 12.1 %all-gather.1 = bf16[2,128,1024]{2,1,0:T(8,128)(2,1)} all-gather(bf16[2,32,1024]{2,1,0:T(8,128)(2,1)S(1)} %bitcast.26), channel_id=3, replica_groups=mesh['zl'=4,'core'=2,'y'=8,'zh'=2,'x'=4] {'x'}, dimensions={1}, use_global_device_ids=true | all-gather | bytes 655360 | tf_op jit(solution)/shard_map/all_gather | solution.py:222
  100.1 0.0 all-gather.12.cloned.1.call-update
  100.2 0.0 all-gather.10.cloned.1.call-start
  100.2 14.4 %all-gather.8.cloned.1.call-done.k2_ref.v2_ref = bf16[1792,512]{1,0:T(8,128)(2,1)} async-done(((bf16[448,512]{1,0:T(8,128)(2,1)}), bf16[1792,512]{1,0:T(8,128)(2,1)}) %all-gather.8.cloned.1.call-update) | async-done | bytes 1835024 | tf_op jit(solution)/shard_map/all_gather | solution.py:241
  114.6 1.7 slice.4
  116.3 0.0 all-gather.10.cloned.1.call-update
  116.3 0.0 all-gather.14.cloned.1.call-start
  116.3 56.1 %all-gather.12.cloned.1.call-done = bf16[2048,1024]{1,0:T(8,128)(2,1)} async-done(((bf16[256,1024]{1,0:T(8,128)(2,1)}), bf16[2048,1024]{1,0:T(8,128)(2,1)}) %all-gather.12.cloned.1.call-update) | async-done | bytes 4194320 | tf_op jit(solution)/shard_map/all_gather | solution.py:224
  172.5 0.0 all-gather.14.cloned.1.call-update
  172.5 1.1 copy-done.4
  173.6 0.1 copy.10
  173.6 25.9 %all_to_all.15 = bf16[8,192,256]{2,1,0:T(8,128)(2,1)S(1)} all-to-all(bf16[8,192,256]{2,1,0:T(8,128)(2,1)S(1)} %bitcast.22), channel_id=1, replica_groups=mesh['zl'=4,'core'=2,'y'=8,'zh'=2,'x'=4] {'zl','core'}, dimensions={0} | all-to-all | bytes 1572864 | tf_op jit(solution)/shard_map/all_to_all | solution.py:238
  199.5 14.0 %all-gather.10.cloned.1.call-done.k3_ref.v3_ref = bf16[2048,512]{1,0:T(8,128)(2,1)} async-done(((bf16[256,512]{1,0:T(8,128)(2,1)}), bf16[2048,512]{1,0:T(8,128)(2,1)}) %all-gather.10.cloned.1.call-update) | async-done | bytes 2097168 | tf_op jit(solution)/shard_map/all_gather | solution.py:243
  213.5 1.5 copy-done.2
  215.0 1.6 copy-done.3
  216.6 33.2 %attend_levels.1 = bf16[1536,256]{1,0:T(8,128)(2,1)S(1)} custom-call(s32[8]{0:T(128)S(1)} %pad_add_fusion.off_ref, bf16[1536,256]{1,0:T(8,128)(2,1)S(1)} %bitcast.19, bf16[1536,512]{1,0:T(8,128)(2,1)S(1)} %bitcast.17, bf16[1536,512]{1,0:T(8,128)(2,1)S(1)} %bitcast.18, bf16[1792,512]{1,0:T(8,128)(2,1)S(1)} %copy-done.2, bf16[1792,512]{1,0:T(8,128)(2,1)S(1)} %copy-done.2, ...), custom_call_target="tpu_custom_call" | custom-call | flops 20000000000 | bytes 8000000 | tf_op jit(solution)/shard_map/attend_levels/pallas_call | solution.py:162
  249.8 29.4 %all_to_all.16.att_ref = bf16[8,192,256]{2,1,0:T(8,128)(2,1)S(1)} all-to-all(bf16[8,192,256]{2,1,0:T(8,128)(2,1)S(1)} %bitcast.20), channel_id=1, replica_groups=mesh['zl'=4,'core'=2,'y'=8,'zh'=2,'x'=4] {'zl','core'}, dimensions={0} | all-to-all | bytes 1572864 | tf_op jit(solution)/shard_map/all_to_all | solution.py:245
  279.2 3.4 %copy-done.1 = bf16[4096,1024]{1,0:T(8,128)(2,1)S(1)} copy-done((bf16[4096,1024]{1,0:T(8,128)(2,1)S(1)}, bf16[4096,1024]{1,0:T(8,128)(2,1)}, u32[]{:S(2)}) %copy-start.1) | copy-done | bytes 8388632
  282.6 3.6 %project.1 = bf16[192,2048]{1,0:T(8,128)(2,1)} custom-call(bf16[8,192,256]{2,1,0:T(8,128)(2,1)S(1)} %all_to_all.16.att_ref, bf16[2,2048,1024]{2,1,0:T(8,128)(2,1)S(1)} %bitcast.15), custom_call_target="tpu_custom_call" | custom-call | flops 1610612736 | bytes 10000000 | tf_op jit(solution)/shard_map/project/pallas_call | solution.py:202
  (13 shorter events, 0.0 us)
Async XLA Ops:
  6.5 73.1 %copy-start = (bf16[32,2048]{1,0:T(8,128)(2,1)S(1)}, bf16[32,2048]{1,0:T(8,128)(2,1)}, u32[]{:S(2)}) copy-start(bf16[32,2048]{1,0:T(8,128)(2,1)} %param.11) | copy-start | bytes 393220
  12.0 10.5 %copy-start.5 = (s32[32]{0:T(128)S(1)}, s32[32]{0:T(128)}, u32[]{:S(2)}) copy-start(s32[32]{0:T(128)} %param.10) | copy-start | bytes 388
  12.0 10.6 %copy-start.6 = (s32[32]{0:T(128)S(1)}, s32[32]{0:T(128)}, u32[]{:S(2)}) copy-start(s32[32]{0:T(128)} %param.9) | copy-start | bytes 388
  12.0 47.5 %all-to-all-start.1 = ((bf16[8,192,512]{2,1,0:T(8,128)(2,1)}), bf16[8,192,512]{2,1,0:T(8,128)(2,1)S(1)}, u32[]{:S(2)}, u32[]{:S(2)}) async-start(bf16[8,192,512]{2,1,0:T(8,128)(2,1)} %pack_kv.1), calls=%async_computation.1 | async-start | bytes 3145728 | tf_op jit(solution)/shard_map/all_to_all | solution.py:237
  22.5 92.0 %all-gather.8.cloned.1.call-start = ((), (), s32[]{:S(2)}) async-start(), calls=%async_computation.3 | async-start | bytes 2293760 | tf_op jit(solution)/shard_map/all_gather | solution.py:241
  61.8 17.0 %collective-permute-start = (bf16[224,512]{1,0:T(8,128)(2,1)S(1)}, bf16[224,512]{1,0:T(8,128)(2,1)S(1)}, u32[]{:S(2)}, u32[]{:S(2)}) collective-permute-start(bf16[224,512]{1,0:T(8,128)(2,1)S(1)} %pick_rows.1), channel_id=1, source_target_pairs={{0,4},{4,0},{1,5},{5,1},{2,6},{6,2},{3,7},{7,3},{8,12},{12,8},{9,1... | collective-permute-start | bytes 688136 | tf_op jit(solution)/shard_map/ppermute | solution.py:240
  79.6 92.9 %all-gather.12.cloned.1.call-start = ((), (), s32[]{:S(2)}) async-start(), calls=%async_computation.5 | async-start | bytes 4718592 | tf_op jit(solution)/shard_map/all_gather | solution.py:224
  100.2 113.4 %all-gather.10.cloned.1.call-start = ((), (), s32[]{:S(2)}) async-start(), calls=%async_computation.4 | async-start | bytes 2359296 | tf_op jit(solution)/shard_map/all_gather | solution.py:243
  116.3 162.9 %all-gather.14.cloned.1.call-start = ((), (), s32[]{:S(2)}) async-start(), calls=%async_computation.6 | async-start | bytes 12582912 | tf_op jit(solution)/shard_map/all_gather | solution.py:225
  172.4 1.1 copy-start.4
  213.5 1.5 copy-start.2
  215.0 1.6 copy-start.3
  279.2 3.4 %copy-start.1 = (bf16[4096,1024]{1,0:T(8,128)(2,1)S(1)}, bf16[4096,1024]{1,0:T(8,128)(2,1)}, u32[]{:S(2)}) copy-start(bf16[4096,1024]{1,0:T(8,128)(2,1)} %all-gather.14.cloned.1.call-done) | copy-start | bytes 25165828
Sparse Core Ops, SparseCore 0:
  79.7 34.8 all-gather.7
  116.7 55.7 all-gather.11
  174.5 38.9 all-gather.9
  215.5 32.2 all-gather.13

commit v2 on v0

v2 whole, which is shorter than its diff:
```python
import functools
import math

import jax
import jax.numpy as jnp
from jax import lax
from jax.experimental import pallas as pl
from jax.experimental.pallas import tpu as pltpu
from jax.sharding import Mesh
from jax.sharding import PartitionSpec as P

H = 32
HD = 64
PAIR = 2 * HD
R2 = 8
R3 = 64
D = H * HD
GRP = 8
XS = 4
ROWS = 192
SEG1 = ROWS * GRP
OWN = H // GRP
WIDTH = OWN * HD
LOCAL2 = ROWS // R2
LOCAL3 = ROWS // R3
PICK = 32
SENT = PICK + PICK // 2
BLOCK = 256
SCALE2 = HD**-0.5 * math.log2(math.e)
VMEM_LIMIT = 40 * 2**20
GROUP = ("zl", "core")
NT = (((1,), (1,)), ((), ()))
BF16 = jnp.bfloat16
F32 = jnp.float32


def fine_mesh(mesh):
    return Mesh(mesh.devices.reshape(4, 2, 8, 2, XS), ("zl", "core", "y", "zh", "x"))


def params():
    return pltpu.CompilerParams(vmem_limit_bytes=VMEM_LIMIT)


def cost(flops, traffic, transcendentals=0):
    return pl.CostEstimate(flops=flops, bytes_accessed=traffic, transcendentals=transcendentals)


def iota(shape, dim):
    return lax.broadcasted_iota(jnp.int32, shape, dim)


def pack_kernel(two_ref, three_ref, q_ref, k_ref, v_ref, first_ref, second_ref, small_ref):
    step = pl.program_id(0)
    columns = pl.ds(pl.multiple_of(step * WIDTH, WIDTH), WIDTH)
    for pair, out_ref in enumerate((first_ref, second_ref)):
        narrow = pl.ds(pl.multiple_of(step * WIDTH + pair * PAIR, PAIR), PAIR)
        for which, ref in enumerate((q_ref, k_ref, v_ref)):
            out_ref[0, :, which * PAIR : (which + 1) * PAIR] = ref[:, narrow]
    row = iota((OWN * PICK, ROWS), 0)
    place = row % PICK
    target = jnp.full((OWN * PICK, ROWS), -1, jnp.int32)
    for i in range(OWN):
        two = place * R2 + two_ref[step * OWN + i]
        three = (place - LOCAL2) * R3 + three_ref[step * OWN + i]
        own = jnp.where(place < LOCAL2, two, jnp.where(place < LOCAL2 + LOCAL3, three, -1))
        target = jnp.where(row // PICK == i, own, target)
    onehot = jnp.where(iota((OWN * PICK, ROWS), 1) == target, 1.0, 0.0).astype(BF16)
    picked = [jnp.dot(onehot, ref[:, columns], preferred_element_type=F32) for ref in (q_ref, k_ref, v_ref)]
    low = iota((PICK, PAIR), 1) < HD
    for i in range(OWN):
        rows, lanes = slice(i * PICK, (i + 1) * PICK), slice(i // 2 * PAIR, (i // 2 + 1) * PAIR)
        q, k, v = (part[rows, lanes] for part in picked)
        if i % 2:
            k = pltpu.roll(k, HD, 1)
            head, tail = pltpu.roll(q[: PICK // 2], HD, 1), q[PICK // 2 :]
        else:
            v = pltpu.roll(v, HD, 1)
            head, tail = q[: PICK // 2], pltpu.roll(q[PICK // 2 :], HD, 1)
        small_ref[i, :PICK, :] = jnp.where(low, k, v).astype(BF16)
        small_ref[i, PICK:, :] = jnp.where(low[: PICK // 2], head, tail).astype(BF16)


def pack(offsets_two, offsets_three, queries, keys, values):
    whole = pl.BlockSpec((ROWS, D), lambda j, *_: (0, 0))
    chunk = pl.BlockSpec((1, ROWS, 3 * PAIR), lambda j, *_: (j, 0, 0))
    chunk_shape = jax.ShapeDtypeStruct((GRP, ROWS, 3 * PAIR), BF16)
    return pl.pallas_call(
        pack_kernel,
        grid_spec=pltpu.PrefetchScalarGridSpec(
            num_scalar_prefetch=2,
            grid=(GRP,),
            in_specs=[whole] * 3,
            out_specs=[chunk, chunk, pl.BlockSpec((OWN, SENT, PAIR), lambda j, *_: (j, 0, 0))],
        ),
        out_shape=[chunk_shape, chunk_shape, jax.ShapeDtypeStruct((H, SENT, PAIR), BF16)],
        compiler_params=params(),
        cost_estimate=cost(10**9, 5 * 10**6),
        name="pack",
    )(offsets_two, offsets_three, queries, keys, values)


def compact_kernel(own_ref, other_ref, out_ref):
    count = H * LOCAL3
    row = iota((count, H * PICK), 0)
    target = row // LOCAL3 * PICK + LOCAL2 + row % LOCAL3
    onehot = jnp.where(iota((count, H * PICK), 1) == target, 1.0, 0.0).astype(BF16)
    for which, ref in enumerate((own_ref, other_ref)):
        chosen = jnp.dot(onehot, ref[...], preferred_element_type=F32)
        out_ref[which * count : (which + 1) * count, :] = chosen.astype(BF16)


def compact(own, other):
    return pl.pallas_call(
        compact_kernel,
        out_shape=jax.ShapeDtypeStruct((2 * H * LOCAL3, PAIR), BF16),
        compiler_params=params(),
        cost_estimate=cost(10**8, 10**6),
        name="compact_three",
    )(own, other)


def sparse_kernel(place_ref, got_ref, other_ref, far_ref, out_ref):
    low = iota((1, PAIR), 1) < HD
    zero, one = jnp.zeros((), BF16), jnp.ones((), BF16)
    own = got_ref[:, :PICK, :].reshape(H * PICK, PAIR)
    other = other_ref[...].reshape(H * PICK, PAIR)
    far = far_ref[...]
    half = PICK // 2
    raw = got_ref[:, PICK:, :].reshape(H * half, PAIR).astype(F32)
    head = jnp.where(low, raw, 0.0)
    tail = jnp.where(low, pltpu.roll(raw, HD, 1), 0.0).reshape(H, half, PAIR)
    tail_two = tail[:, : LOCAL2 - half].reshape(-1, PAIR)
    tail_three = tail[:, LOCAL2 - half :].reshape(-1, PAIR)

    def attend(q, sets):
        q = q.astype(BF16)
        scores = []
        for kv, masked in sets:
            part = lax.dot_general(q, kv, NT, preferred_element_type=F32)
            if masked:
                part = jnp.where(iota((1, kv.shape[0]), 1) % PICK < LOCAL2, part, -1e30)
            scores.append(part)
        largest = functools.reduce(jnp.maximum, [jnp.max(part, axis=-1, keepdims=True) for part in scores])
        total = None
        for (kv, _), part in zip(sets, scores):
            expo = jnp.exp2((part - largest) * SCALE2).astype(BF16)
            part = jnp.dot(expo, jnp.where(low, one, kv), preferred_element_type=F32)
            total = part if total is None else total + part
        weight = total[:, :1]
        log_sum = largest * SCALE2 + jnp.log2(weight)
        top = log_sum.astype(BF16).astype(F32)
        middle = (log_sum - top).astype(BF16).astype(F32)
        rest = log_sum - top - middle
        lane = iota((1, PAIR), 1)
        stats = jnp.where(lane < 16, top, jnp.where(lane < 32, middle, rest))
        return jnp.where(low, stats, total / weight)

    two = ((own, True), (other, True))
    rows = H * half // 2
    first = jnp.concatenate([attend(head[:rows], two), attend(head[rows:], two)], 0)
    first = first.reshape(GRP, XS, half, PAIR)
    second = attend(tail_two, two).reshape(GRP, XS, LOCAL2 - half, PAIR)
    third = attend(tail_three, ((far, False),)).reshape(GRP, XS, PICK - LOCAL2, PAIR)
    second = jnp.concatenate([second, third], axis=2)
    for x in range(XS):
        where = (x - place_ref[0] + XS) % XS
        out_ref[where, :, :half, :] = first[:, x].astype(BF16)
        out_ref[where, :, half:, :] = second[:, x].astype(BF16)


def sparse_levels(place, got, other, far):
    shape = (XS, GRP, PICK, PAIR)
    return pl.pallas_call(
        sparse_kernel,
        in_specs=[pl.BlockSpec(memory_space=pltpu.SMEM)] + [pl.BlockSpec(memory_space=pltpu.VMEM)] * 3,
        out_shape=jax.ShapeDtypeStruct(shape, BF16),
        compiler_params=params(),
        cost_estimate=cost(4 * 10**9, 2 * 10**6, 2 * 10**6),
        name="sparse_levels",
    )(place, got, other, far)


def dense_kernel(head, scalar_ref, qkv_ref, back_ref, out_ref, acc, top, aug, few):
    zero, one = jnp.zeros((), BF16), jnp.ones((), BF16)

    def mine(parity, rows):
        lane = iota((rows, PAIR), 1)
        return (lane >= HD) if parity else (lane < HD)

    for parity in range(2):
        aug[parity] = jnp.where(mine(parity, SEG1), qkv_ref[:, 2 * PAIR :], one)

    def level_one(block, carry):
        rows = pl.ds(pl.multiple_of(block * BLOCK, BLOCK), BLOCK)
        q = qkv_ref[rows, :PAIR]
        scores = [
            lax.dot_general(
                jnp.where(mine(parity, BLOCK), q, zero), qkv_ref[:, PAIR : 2 * PAIR], NT, preferred_element_type=F32
            )
            for parity in range(2)
        ]
        for parity in range(2):
            largest = jnp.max(scores[parity], axis=-1, keepdims=True)
            expo = jnp.exp2((scores[parity] - largest) * SCALE2).astype(BF16)
            acc[parity, rows, :] = jnp.dot(expo, aug[parity], preferred_element_type=F32)
            top[parity, rows, :] = jnp.broadcast_to(largest * SCALE2, (BLOCK, PAIR))
        return carry

    lax.fori_loop(0, SEG1 // BLOCK, level_one, 0)

    for parity in range(2):
        back = back_ref[(scalar_ref[0] - head - parity + XS) % XS].astype(F32)

        def merge(rows, part, parity=parity):
            log_sum = part[:, 0:1] + part[:, 16:17] + part[:, 32:33]
            shaped = part if parity else pltpu.roll(part, HD, 1)
            shaped = jnp.where(mine(parity, part.shape[0]), shaped, 1.0)
            old = top[parity, rows, :]
            peak = jnp.maximum(old, log_sum)
            top[parity, rows, :] = peak
            acc[parity, rows, :] = acc[parity, rows, :] * jnp.exp2(old - peak) + shaped * jnp.exp2(log_sum - peak)

        two = scalar_ref[1 + parity]
        merge(pl.ds(two, SEG1 // R2, stride=R2), back[:, :LOCAL2].reshape(SEG1 // R2, PAIR))
        for g in range(GRP):
            few[g * LOCAL3 : (g + 1) * LOCAL3, :] = back[g, LOCAL2 : LOCAL2 + LOCAL3]
        three = scalar_ref[3 + parity]
        merge(pl.ds(three, SEG1 // R3, stride=R3), few[...])
    result = [acc[parity] / pltpu.roll(acc[parity], HD, 1) for parity in range(2)]
    out_ref[...] = jnp.where(mine(0, SEG1), result[0], result[1]).astype(BF16)


def dense_level(head, scalars, qkv, back):
    return pl.pallas_call(
        functools.partial(dense_kernel, head),
        in_specs=[pl.BlockSpec(memory_space=pltpu.SMEM)] + [pl.BlockSpec(memory_space=pltpu.VMEM)] * 2,
        out_shape=jax.ShapeDtypeStruct((SEG1, PAIR), BF16),
        scratch_shapes=[
            pltpu.VMEM((2, SEG1, PAIR), F32),
            pltpu.VMEM((2, SEG1, PAIR), F32),
            pltpu.VMEM((2, SEG1, PAIR), BF16),
            pltpu.VMEM((SEG1 // R3, PAIR), F32),
        ],
        compiler_params=params(),
        cost_estimate=cost(10 * 10**9, 4 * 10**6, 5 * 10**6),
        name="dense_level",
    )(scalars, qkv, back)


def project_kernel(first_ref, second_ref, w_ref, out_ref):
    part = D // H // 2
    total = None
    for g in range(GRP):
        weights = [w_ref[0, g * WIDTH + (x * 2 + zh) * part : g * WIDTH + (x * 2 + zh + 1) * part] for zh in range(2) for x in range(XS)]
        att = jnp.concatenate([first_ref[g], second_ref[g]], axis=1)
        term = jnp.dot(att, jnp.concatenate(weights, 0), preferred_element_type=F32)
        total = term if total is None else total + term
    out_ref[...] = total.astype(BF16)


def project(first, second, w_halves):
    columns = 512
    per_half = D // 2 // columns
    att = pl.BlockSpec((GRP, ROWS, PAIR), lambda j: (0, 0, 0))
    return pl.pallas_call(
        project_kernel,
        grid=(D // columns,),
        in_specs=[att, att, pl.BlockSpec((1, D, columns), lambda j: (j // per_half, 0, j % per_half))],
        out_specs=pl.BlockSpec((ROWS, columns), lambda j: (0, j)),
        out_shape=jax.ShapeDtypeStruct((ROWS, D), BF16),
        compiler_params=pltpu.CompilerParams(vmem_limit_bytes=56 * 2**20),
        cost_estimate=cost(2 * ROWS * D * D, 10 * 10**6),
        name="project",
    )(first, second, w_halves)


def swap(value):
    return lax.ppermute(value, "zh", [(0, 1), (1, 0)])


def after(value, *events):
    return lax.optimization_barrier((value, *events))[0]


def local(queries, keys, values, offsets_two, offsets_three, w_out):
    half = D // 2
    exchange = functools.partial(lax.all_to_all, axis_name=GROUP, split_axis=0, concat_axis=0, tiled=True)
    x = lax.axis_index("x")
    first_head = lax.axis_index(GROUP) * OWN
    own_two = lax.dynamic_slice_in_dim(offsets_two, first_head, OWN)
    own_three = lax.dynamic_slice_in_dim(offsets_three, first_head, OWN)

    chunk_a, chunk_b, small = pack(offsets_two, offsets_three, queries, keys, values)
    got = lax.all_to_all(small, ("zl", "core", "x"), split_axis=0, concat_axis=0, tiled=True)
    w_own = lax.dynamic_slice_in_dim(w_out, lax.axis_index("core") * half, half, axis=1)
    w_other = swap(w_own)
    upper = lax.axis_index("zh") == 1
    w_both = jnp.concatenate([jnp.where(upper, w_other, w_own), jnp.where(upper, w_own, w_other)], 0)
    w_columns = lax.all_gather(w_both, ("y", "x"), axis=0, tiled=True)

    own = got[:, :PICK]
    other = swap(own)
    qkv_a = exchange(after(chunk_a, got)).reshape(SEG1, 3 * PAIR)
    far = lax.all_gather(compact(own.reshape(H * PICK, PAIR), other.reshape(H * PICK, PAIR)), "y", axis=0, tiled=True)
    parts = sparse_levels(x.reshape(1), got, other, far)
    back = [parts[0]]
    for step in range(1, XS):
        back.append(lax.ppermute(parts[step], "x", [(i, (i + step) % XS) for i in range(XS)]))
    back = jnp.stack(back)
    qkv_b = exchange(after(chunk_b, qkv_a)).reshape(SEG1, 3 * PAIR)

    def scalars(head):
        return jnp.concatenate([x.reshape(1), own_two[head : head + 2], own_three[head : head + 2]])

    att_a = dense_level(0, scalars(0), qkv_a, back)
    w_halves = lax.all_gather(after(w_columns, qkv_b), "core", axis=0, tiled=False)
    att_b = dense_level(2, scalars(2), qkv_b, back)
    out_a = exchange(after(att_a, qkv_b).reshape(GRP, ROWS, PAIR))
    out_b = exchange(att_b.reshape(GRP, ROWS, PAIR))
    return project(out_a, out_b, w_halves)


def solution(mesh):
    rows = P(("y", "zh", "x", "zl", "core"), None)
    return jax.shard_map(
        local,
        mesh=fine_mesh(mesh),
        in_specs=(rows, rows, rows, P(), P(), P(("y", "zh", "x"), None)),
        out_specs=rows,
        check_vma=False,
    )
```

time: 758 us -> 233 us (0.31)
  blocking collectives: 495 us -> 123 us
  local copies, waits for them, and re-layouts: 78.2 us -> 6.43 us
  waiting for transfers between devices: 59.5 us -> 15.4 us
  matrix products: 37.6 us -> 0 us
  Pallas kernels: 0 us -> 30.1 us
  other arithmetic: 30.6 us -> 1.72 us
    all_gather x2 -> x1, blocking collectives: 411 us -> 21 us  [local(): lax.all_gather(compact(own.reshape(H * PICK, PAIR), other.reshape(H * PIC...]
    all_to_all x3 -> x1, waiting for transfers between devices: 51 us -> 3.63 us  [local(): out_b = exchange(att_b.reshape(GRP, ROWS, PAIR))]
    dot_general x76 -> x0, matrix products: 37.6 us -> none  [the longest x36 16.1 us: one_block(): jnp.dot(block_q, head_k.T, preferred_element_type=jnp.float32) * scale]
    pallas_call x0 -> x6, Pallas kernels: none -> 30.1 us  [the longest x2 16.9 us: dense_level(): pl.pallas_call(functools.partial(dense_kernel, head), in_specs=[pl.BlockS...]
    reshape x27 -> x0, local copies, waits for them, and re-layouts: 25.1 us -> none  [the longest x6 9.35 us: choose_rows(): shaped = matrix.reshape(count, rate, heads, HD)]
    all_to_all x1 -> x4, blocking collectives: 83.2 us -> 102 us  [the longest x1 31.8 us: local(): qkv_b = exchange(after(chunk_b, qkv_a)).reshape(SEG1, 3 * PAIR)]
    dynamic_slice x62 -> x3, local copies, waits for them, and re-layouts: 18.2 us -> 0.99 us  [the longest x1 0.84 us: local(): lax.dynamic_slice_in_dim(w_out, lax.axis_index('core') * half, half, axis=1)]
    dynamic_update_slice x96 -> x0, local copies, waits for them, and re-layouts: 13.6 us -> none  [the longest x24 10.7 us: attend(): lax.map(one_head, (jnp.moveaxis(query_heads, 1, 0), jnp.moveaxis(key_head...]
  transfers between devices with their start and end apart: 10 -> 8, of which waited for: 5 -> 4; matrix products, arithmetic and copies ran while one was open for 18% -> 0% of each run, Pallas kernels for 0% -> 10%
where the time goes in v2:
time: 233 us; the launch traced here: 232 us
  blocking collectives  123 us (53%)
  starting transfers between devices  42.7 us (18%)
  Pallas kernels  30.1 us (13%)
  waiting for transfers between devices  15.4 us (7%)
  between operations  13.5 us (6%)
  local copies, waits for them, and re-layouts  6.43 us (3%)
    all_to_all x1, blocking collectives, local(): qkv_b = exchange(after(chunk_b, qkv_a)).reshape(SEG1, 3 * PAIR)  31.8 us
    all_to_all x1, blocking collectives, local(): qkv_a = exchange(after(chunk_a, got)).reshape(SEG1, 3 * PAIR)  31.5 us
    all_to_all x1, blocking collectives, local(): lax.all_to_all(small, ('zl', 'core', 'x'), split_axis=0, concat_axis=0, t...  22.7 us
    all_gather x1, blocking collectives, local(): lax.all_gather(compact(own.reshape(H * PICK, PAIR), other.reshape(H * PIC...  21 us
    ppermute x2, starting transfers between devices, swap(): return lax.ppermute(value, 'zh', [(0, 1), (1, 0)])  18.6 us
    pallas_call x2, Pallas kernels, dense_level(): pl.pallas_call(functools.partial(dense_kernel, head), in_specs=[pl.BlockS...  16.9 us
    all_to_all x1, blocking collectives, local(): out_a = exchange(after(att_a, qkv_b).reshape(GRP, ROWS, PAIR))  15.6 us
    all_to_all x1, starting transfers between devices, local(): out_b = exchange(att_b.reshape(GRP, ROWS, PAIR))  15.3 us
  transfers between devices with their start and end apart: 8, of which 4 were waited for; matrix products, arithmetic and copies ran while one was open for 0% of the time, Pallas kernels for 10%

profile of v2, /device:TPU:1, one launch (start us, length us, event | category | flops | bytes accessed | tf_op | source)
XLA Modules:
  0.0 232.5 jit_solution(13654393854321118087)
XLA Ops:
  6.5 0.8 constant_dynamic-slice_fusion
  7.4 11.5 %collective-permute-start.4 = (bf16[32,1024]{1,0:T(8,128)(2,1)S(1)}, bf16[32,1024]{1,0:T(8,128)(2,1)S(1)}, u32[]{:S(2)}, u32[]{:S(2)}) collective-permute-start(bf16[32,1024]{1,0:T(8,128)(2,1)S(1)} %constant_dynamic-slice_fusion), channel_id=1, source_target_pairs={{0,4},{4,0},{1,5},{5,1},{2,6},{6,2},{3,7},{7,3},{8,12},{12,8},{9,1... | collective-permute-start | bytes 196616 | tf_op jit(solution)/shard_map/ppermute | solution.py:279
  18.8 1.7 collective-permute-done.4
  20.6 0.9 broadcast_select_fusion.1
  21.4 0.7 pad_maximum_fusion.1
  22.2 1.1 copy-done
  23.3 1.1 copy-done.1
  24.4 1.1 copy-done.2
  25.6 0.7 copy-done.3
  26.2 0.7 copy-done.5
  26.9 3.4 %pack.1 = (bf16[8,192,384]{2,1,0:T(8,128)(2,1)S(1)}, bf16[8,192,384]{2,1,0:T(8,128)(2,1)S(1)}, bf16[32,48,128]{2,1,0:T(8,128)(2,1)S(1)}) custom-call(s32[32]{0:T(128)S(1)} %copy-done.5, s32[32]{0:T(128)S(1)} %copy-done.3, bf16[192,2048]{1,0:T(8,128)(2,1)S(1)} %copy-done, bf16[192,2048]{1,0:T(8,128)(2,1)S(1)} %copy-done.1, bf16[192,2048]{1,0:T(8,128)(2,1)S(1)} %copy-done.2), custom_call_target="tpu_custom_call" | custom-call | flops 1000000000 | bytes 5000000 | tf_op jit(solution)/shard_map/pack/pallas_call | solution.py:88
  30.3 22.7 %all_to_all.25.got_ref = bf16[32,48,128]{2,1,0:T(8,128)(2,1)S(1)} all-to-all(bf16[32,48,128]{2,1,0:T(8,128)(2,1)S(1)} %get-tuple-element.13), channel_id=1, replica_groups=mesh['zl'=4,'core'=2,'y'=8,'zh'=2,'x'=4] {'zl','core','x'}, dimensions={0} | all-to-all | bytes 786432 | tf_op jit(solution)/shard_map/all_to_all | solution.py:295
  52.9 31.5 %all_to_all.26 = bf16[8,192,384]{2,1,0:T(8,128)(2,1)S(1)} all-to-all(bf16[8,192,384]{2,1,0:T(8,128)(2,1)S(1)} %get-tuple-element.14), channel_id=1, replica_groups=mesh['zl'=4,'core'=2,'y'=8,'zh'=2,'x'=4] {'zl','core'}, dimensions={0} | all-to-all | bytes 2359296 | tf_op jit(solution)/shard_map/all_to_all | solution.py:304
  84.4 31.8 %all_to_all.27 = bf16[8,192,384]{2,1,0:T(8,128)(2,1)S(1)} all-to-all(bf16[8,192,384]{2,1,0:T(8,128)(2,1)S(1)} %get-tuple-element.16), channel_id=1, replica_groups=mesh['zl'=4,'core'=2,'y'=8,'zh'=2,'x'=4] {'zl','core'}, dimensions={0} | all-to-all | bytes 2359296 | tf_op jit(solution)/shard_map/all_to_all | solution.py:311
  116.2 0.6 copy-done.4
  117.0 7.1 %collective-permute-start = (bf16[32,32,128]{2,1,0:T(8,128)(2,1)S(1)}, bf16[32,32,128]{2,1,0:T(8,128)(2,1)S(1)}, u32[]{:S(2)}, u32[]{:S(2)}) collective-permute-start(bf16[32,32,128]{2,1,0:T(8,128)(2,1)S(1)} %slice.36), channel_id=1, source_target_pairs={{0,4},{4,0},{1,5},{5,1},{2,6},{6,2},{3,7},{7,3},{8,12},{12,8},{9,1... | collective-permute-start | bytes 786440 | tf_op jit(solution)/shard_map/ppermute | solution.py:279
  124.2 0.1 pad_add_fusion.1.scalar_ref
  124.3 7.9 %collective-permute-done.other_ref = bf16[32,32,128]{2,1,0:T(8,128)(2,1)S(1)} collective-permute-done((bf16[32,32,128]{2,1,0:T(8,128)(2,1)S(1)}, bf16[32,32,128]{2,1,0:T(8,128)(2,1)S(1)}, u32[]{:S(2)}, u32[]{:S(2)}) %collective-permute-start) | collective-permute-done | bytes 262176 | tf_op jit(solution)/shard_map/ppermute | solution.py:279
  132.2 0.3 compact_three.1
  132.4 21.0 %all_gather.12.far_ref = bf16[1536,128]{1,0:T(8,128)(2,1)S(1)} all-gather(bf16[192,128]{1,0:T(8,128)(2,1)S(1)} %compact_three.1), channel_id=1, replica_groups=mesh['zl'=4,'core'=2,'y'=8,'zh'=2,'x'=4] {'y'}, dimensions={0}, use_global_device_ids=true | all-gather | bytes 442368 | tf_op jit(solution)/shard_map/all_gather | solution.py:305
  153.5 3.4 %sparse_levels.1 = bf16[4,8,32,128]{3,2,1,0:T(8,128)(2,1)S(1)} custom-call(s32[1]{0:T(128)} %bitcast.place_ref, bf16[32,48,128]{2,1,0:T(8,128)(2,1)S(1)} %all_to_all.25.got_ref, bf16[32,32,128]{2,1,0:T(8,128)(2,1)S(1)} %collective-permute-done.other_ref, bf16[1536,128]{1,0:T(8,128)(2,1)S(1)} %all_gather.12.far_ref), custom_call_target="tpu_custom_call" | custom-call | flops 4000000000 | bytes 2000000 | tf_op jit(solution)/shard_map/sparse_levels/pallas_call | solution.py:174
  156.9 1.9 collective-permute-start.1
  158.9 4.1 %collective-permute-start.2 = (bf16[8,32,128]{2,1,0:T(8,128)(2,1)S(1)}, bf16[8,32,128]{2,1,0:T(8,128)(2,1)S(1)}, u32[]{:S(2)}, u32[]{:S(2)}) collective-permute-start(bf16[8,32,128]{2,1,0:T(8,128)(2,1)S(1)} %get-tuple-element.21), channel_id=1, source_target_pairs={{0,2},{1,3},{2,0},{3,1},{4,6},{5,7},{6,4},{7,5},{8,10},{9,11},{10,... | collective-permute-start | bytes 196616 | tf_op jit(solution)/shard_map/ppermute | solution.py:309
  163.0 2.7 %collective-permute-start.3 = (bf16[8,32,128]{2,1,0:T(8,128)(2,1)S(1)}, bf16[8,32,128]{2,1,0:T(8,128)(2,1)S(1)}, u32[]{:S(2)}, u32[]{:S(2)}) collective-permute-start(bf16[8,32,128]{2,1,0:T(8,128)(2,1)S(1)} %get-tuple-element.20), channel_id=1, source_target_pairs={{0,3},{1,0},{2,1},{3,2},{4,7},{5,4},{6,5},{7,6},{8,11},{9,8},{10,9... | collective-permute-start | bytes 196616 | tf_op jit(solution)/shard_map/ppermute | solution.py:309
  165.7 0.1 pad_add_fusion.scalar_ref
  165.8 2.2 collective-permute-done.3
  168.0 8.8 %dense_level.3 = bf16[1536,128]{1,0:T(8,128)(2,1)} custom-call(s32[5]{0:T(128)S(1)} %pad_add_fusion.1.scalar_ref, bf16[1536,384]{1,0:T(8,128)(2,1)S(1)} %bitcast.18, bf16[4,8,32,128]{3,2,1,0:T(8,128)(2,1)S(1)} %pad_maximum_fusion.back_ref), custom_call_target="tpu_custom_call" | custom-call | flops 10000000000 | bytes 4000000 | tf_op jit(solution)/shard_map/dense_level/pallas_call | solution.py:235
  176.9 15.3 %all-to-all-start.4 = ((bf16[8,192,128]{2,1,0:T(8,128)(2,1)}), bf16[8,192,128]{2,1,0:T(8,128)(2,1)S(1)}, u32[]{:S(2)}, u32[]{:S(2)}) async-start(bf16[8,192,128]{2,1,0:T(8,128)(2,1)} %bitcast.12), calls=%async_computation.4 | async-start | bytes 786432 | tf_op jit(solution)/shard_map/all_to_all | solution.py:320
  192.1 8.1 %dense_level.2 = bf16[1536,128]{1,0:T(8,128)(2,1)S(1)} custom-call(s32[5]{0:T(128)S(1)} %pad_add_fusion.scalar_ref, bf16[1536,384]{1,0:T(8,128)(2,1)S(1)} %bitcast.17, bf16[4,8,32,128]{3,2,1,0:T(8,128)(2,1)S(1)} %pad_maximum_fusion.back_ref), custom_call_target="tpu_custom_call" | custom-call | flops 10000000000 | bytes 4000000 | tf_op jit(solution)/shard_map/dense_level/pallas_call | solution.py:235
  200.2 3.6 %all-to-all-done.4.second_ref = bf16[8,192,128]{2,1,0:T(8,128)(2,1)S(1)} async-done(((bf16[8,192,128]{2,1,0:T(8,128)(2,1)}), bf16[8,192,128]{2,1,0:T(8,128)(2,1)S(1)}, u32[]{:S(2)}, u32[]{:S(2)}) %all-to-all-start.4) | async-done | bytes 393248 | tf_op jit(solution)/shard_map/all_to_all | solution.py:320
  203.8 15.6 %all_to_all.28.first_ref = bf16[8,192,128]{2,1,0:T(8,128)(2,1)} all-to-all(bf16[8,192,128]{2,1,0:T(8,128)(2,1)S(1)} %bitcast.20), channel_id=1, replica_groups=mesh['zl'=4,'core'=2,'y'=8,'zh'=2,'x'=4] {'zl','core'}, dimensions={0} | all-to-all | bytes 786432 | tf_op jit(solution)/shard_map/all_to_all | solution.py:319
  219.5 6.2 %project.1 = bf16[192,2048]{1,0:T(8,128)(2,1)} custom-call(bf16[8,192,128]{2,1,0:T(8,128)(2,1)} %all_to_all.28.first_ref, bf16[8,192,128]{2,1,0:T(8,128)(2,1)} %copy-done.7, bf16[2,2048,1024]{2,1,0:T(8,128)(2,1)} %bitcast.22), custom_call_target="tpu_custom_call" | custom-call | flops 1610612736 | bytes 10000000 | tf_op jit(solution)/shard_map/project/pallas_call | solution.py:266
  (24 shorter events, 0.4 us)
Async XLA Ops:
  6.5 109.7 %all-gather.4.cloned.1.call-start = ((), (), s32[]{:S(2)}) async-start(), calls=%async_computation.5 | async-start | bytes 4325376 | tf_op jit(solution)/shard_map/all_gather | solution.py:300
  7.4 13.2 %collective-permute-start.4 = (bf16[32,1024]{1,0:T(8,128)(2,1)S(1)}, bf16[32,1024]{1,0:T(8,128)(2,1)S(1)}, u32[]{:S(2)}, u32[]{:S(2)}) collective-permute-start(bf16[32,1024]{1,0:T(8,128)(2,1)S(1)} %constant_dynamic-slice_fusion), channel_id=1, source_target_pairs={{0,4},{4,0},{1,5},{5,1},{2,6},{6,2},{3,7},{7,3},{8,12},{12,8},{9,1... | collective-permute-start | bytes 196616 | tf_op jit(solution)/shard_map/ppermute | solution.py:279
  22.1 197.3 %all-gather.6.cloned.1.call-start = ((), (), s32[]{:S(2)}) async-start(), calls=%async_computation.6 | async-start | bytes 12582912 | tf_op jit(solution)/shard_map/all_gather | solution.py:317
  22.2 1.1 copy-start
  23.3 1.1 copy-start.1
  24.4 1.1 copy-start.2
  25.6 0.7 copy-start.3
  26.2 0.7 copy-start.5
  116.2 0.7 copy-start.4
  116.2 0.7 copy-start.6
  117.0 15.1 %collective-permute-start = (bf16[32,32,128]{2,1,0:T(8,128)(2,1)S(1)}, bf16[32,32,128]{2,1,0:T(8,128)(2,1)S(1)}, u32[]{:S(2)}, u32[]{:S(2)}) collective-permute-start(bf16[32,32,128]{2,1,0:T(8,128)(2,1)S(1)} %slice.36), channel_id=1, source_target_pairs={{0,4},{4,0},{1,5},{5,1},{2,6},{6,2},{3,7},{7,3},{8,12},{12,8},{9,1... | collective-permute-start | bytes 786440 | tf_op jit(solution)/shard_map/ppermute | solution.py:279
  156.9 8.9 %collective-permute-start.1 = (bf16[8,32,128]{2,1,0:T(8,128)(2,1)S(1)}, bf16[8,32,128]{2,1,0:T(8,128)(2,1)S(1)}, u32[]{:S(2)}, u32[]{:S(2)}) collective-permute-start(bf16[8,32,128]{2,1,0:T(8,128)(2,1)S(1)} %get-tuple-element.22), channel_id=1, source_target_pairs={{0,1},{1,2},{2,3},{3,0},{4,5},{5,6},{6,7},{7,4},{8,9},{9,10},{10,1... | collective-permute-start | bytes 196616 | tf_op jit(solution)/shard_map/ppermute | solution.py:309
  158.9 6.9 %collective-permute-start.2 = (bf16[8,32,128]{2,1,0:T(8,128)(2,1)S(1)}, bf16[8,32,128]{2,1,0:T(8,128)(2,1)S(1)}, u32[]{:S(2)}, u32[]{:S(2)}) collective-permute-start(bf16[8,32,128]{2,1,0:T(8,128)(2,1)S(1)} %get-tuple-element.21), channel_id=1, source_target_pairs={{0,2},{1,3},{2,0},{3,1},{4,6},{5,7},{6,4},{7,5},{8,10},{9,11},{10,... | collective-permute-start | bytes 196616 | tf_op jit(solution)/shard_map/ppermute | solution.py:309
  163.0 5.0 %collective-permute-start.3 = (bf16[8,32,128]{2,1,0:T(8,128)(2,1)S(1)}, bf16[8,32,128]{2,1,0:T(8,128)(2,1)S(1)}, u32[]{:S(2)}, u32[]{:S(2)}) collective-permute-start(bf16[8,32,128]{2,1,0:T(8,128)(2,1)S(1)} %get-tuple-element.20), channel_id=1, source_target_pairs={{0,3},{1,0},{2,1},{3,2},{4,7},{5,4},{6,5},{7,6},{8,11},{9,8},{10,9... | collective-permute-start | bytes 196616 | tf_op jit(solution)/shard_map/ppermute | solution.py:309
  176.9 27.0 %all-to-all-start.4 = ((bf16[8,192,128]{2,1,0:T(8,128)(2,1)}), bf16[8,192,128]{2,1,0:T(8,128)(2,1)S(1)}, u32[]{:S(2)}, u32[]{:S(2)}) async-start(bf16[8,192,128]{2,1,0:T(8,128)(2,1)} %bitcast.12), calls=%async_computation.4 | async-start | bytes 786432 | tf_op jit(solution)/shard_map/all_to_all | solution.py:320
  203.8 15.6 %copy-start.7 = (bf16[8,192,128]{2,1,0:T(8,128)(2,1)}, bf16[8,192,128]{2,1,0:T(8,128)(2,1)S(1)}, u32[]{:S(2)}) copy-start(bf16[8,192,128]{2,1,0:T(8,128)(2,1)S(1)} %all-to-all-done.4.second_ref) | copy-start | bytes 1179652
Sparse Core Ops, SparseCore 0:
  22.2 88.1 all-gather.3
  116.3 29.1 all-gather.5

commit v3 on v2

--- a/solution.py
+++ b/solution.py
@@ -24,6 +24,7 @@
 LOCAL2 = ROWS // R2
 LOCAL3 = ROWS // R3
 PICK = 32
+BULK = PAIR + 2 * WIDTH
 SENT = PICK + PICK // 2
 BLOCK = 256
 SCALE2 = HD**-0.5 * math.log2(math.e)
@@ -53,10 +54,10 @@
 def pack_kernel(two_ref, three_ref, q_ref, k_ref, v_ref, first_ref, second_ref, small_ref):
     step = pl.program_id(0)
     columns = pl.ds(pl.multiple_of(step * WIDTH, WIDTH), WIDTH)
-    for pair, out_ref in enumerate((first_ref, second_ref)):
-        narrow = pl.ds(pl.multiple_of(step * WIDTH + pair * PAIR, PAIR), PAIR)
-        for which, ref in enumerate((q_ref, k_ref, v_ref)):
-            out_ref[0, :, which * PAIR : (which + 1) * PAIR] = ref[:, narrow]
+    first_ref[0, :, :PAIR] = q_ref[:, pl.ds(pl.multiple_of(step * WIDTH, PAIR), PAIR)]
+    first_ref[0, :, PAIR : PAIR + WIDTH] = k_ref[:, columns]
+    first_ref[0, :, PAIR + WIDTH :] = v_ref[:, columns]
+    second_ref[0] = q_ref[:, pl.ds(pl.multiple_of(step * WIDTH + PAIR, PAIR), PAIR)]
     row = iota((OWN * PICK, ROWS), 0)
     place = row % PICK
     target = jnp.full((OWN * PICK, ROWS), -1, jnp.int32)
@@ -83,18 +84,23 @@
 
 def pack(offsets_two, offsets_three, queries, keys, values):
     whole = pl.BlockSpec((ROWS, D), lambda j, *_: (0, 0))
-    chunk = pl.BlockSpec((1, ROWS, 3 * PAIR), lambda j, *_: (j, 0, 0))
-    chunk_shape = jax.ShapeDtypeStruct((GRP, ROWS, 3 * PAIR), BF16)
+
+    def chunk(columns):
+        return pl.BlockSpec((1, ROWS, columns), lambda j, *_: (j, 0, 0))
+
+    def chunk_shape(columns):
+        return jax.ShapeDtypeStruct((GRP, ROWS, columns), BF16)
+
     return pl.pallas_call(
         pack_kernel,
         grid_spec=pltpu.PrefetchScalarGridSpec(
             num_scalar_prefetch=2,
             grid=(GRP,),
             in_specs=[whole] * 3,
-            out_specs=[chunk, chunk, pl.BlockSpec((OWN, SENT, PAIR), lambda j, *_: (j, 0, 0))],
+            out_specs=[chunk(BULK), chunk(PAIR), pl.BlockSpec((OWN, SENT, PAIR), lambda j, *_: (j, 0, 0))],
         ),
-        out_shape=[chunk_shape, chunk_shape, jax.ShapeDtypeStruct((H, SENT, PAIR), BF16)],
-        compiler_params=params(),
+        out_shape=[chunk_shape(BULK), chunk_shape(PAIR), jax.ShapeDtypeStruct((H, SENT, PAIR), BF16)],
+        compiler_params=pltpu.CompilerParams(vmem_limit_bytes=56 * 2**20),
         cost_estimate=cost(10**9, 5 * 10**6),
         name="pack",
     )(offsets_two, offsets_three, queries, keys, values)
@@ -181,23 +187,23 @@
     )(place, got, other, far)
 
 
-def dense_kernel(head, scalar_ref, qkv_ref, back_ref, out_ref, acc, top, aug, few):
+def dense_kernel(head, scalar_ref, q_ref, bulk_ref, back_ref, out_ref, acc, top, aug, few):
     zero, one = jnp.zeros((), BF16), jnp.ones((), BF16)
+    keys = slice(PAIR + head * HD, PAIR + head * HD + PAIR)
+    values = slice(keys.start + WIDTH, keys.stop + WIDTH)
 
     def mine(parity, rows):
         lane = iota((rows, PAIR), 1)
         return (lane >= HD) if parity else (lane < HD)
 
     for parity in range(2):
-        aug[parity] = jnp.where(mine(parity, SEG1), qkv_ref[:, 2 * PAIR :], one)
+        aug[parity] = jnp.where(mine(parity, SEG1), bulk_ref[:, values], one)
 
     def level_one(block, carry):
         rows = pl.ds(pl.multiple_of(block * BLOCK, BLOCK), BLOCK)
-        q = qkv_ref[rows, :PAIR]
+        q = q_ref[rows, :PAIR]
         scores = [
-            lax.dot_general(
-                jnp.where(mine(parity, BLOCK), q, zero), qkv_ref[:, PAIR : 2 * PAIR], NT, preferred_element_type=F32
-            )
+            lax.dot_general(jnp.where(mine(parity, BLOCK), q, zero), bulk_ref[:, keys], NT, preferred_element_type=F32)
             for parity in range(2)
         ]
         for parity in range(2):
@@ -231,10 +237,10 @@
     out_ref[...] = jnp.where(mine(0, SEG1), result[0], result[1]).astype(BF16)
 
 
-def dense_level(head, scalars, qkv, back):
+def dense_level(head, scalars, q, bulk, back):
     return pl.pallas_call(
         functools.partial(dense_kernel, head),
-        in_specs=[pl.BlockSpec(memory_space=pltpu.SMEM)] + [pl.BlockSpec(memory_space=pltpu.VMEM)] * 2,
+        in_specs=[pl.BlockSpec(memory_space=pltpu.SMEM)] + [pl.BlockSpec(memory_space=pltpu.VMEM)] * 3,
         out_shape=jax.ShapeDtypeStruct((SEG1, PAIR), BF16),
         scratch_shapes=[
             pltpu.VMEM((2, SEG1, PAIR), F32),
@@ -245,38 +251,62 @@
         compiler_params=params(),
         cost_estimate=cost(10 * 10**9, 4 * 10**6, 5 * 10**6),
         name="dense_level",
-    )(scalars, qkv, back)
-
-
-def project_kernel(first_ref, second_ref, w_ref, out_ref):
+    )(scalars, q, bulk, back)
+
+
+def project_kernel(place_ref, first_ref, second_ref, own_ref, other_ref, out_ref):
     part = D // H // 2
-    total = None
-    for g in range(GRP):
-        weights = [w_ref[0, g * WIDTH + (x * 2 + zh) * part : g * WIDTH + (x * 2 + zh + 1) * part] for zh in range(2) for x in range(XS)]
-        att = jnp.concatenate([first_ref[g], second_ref[g]], axis=1)
-        term = jnp.dot(att, jnp.concatenate(weights, 0), preferred_element_type=F32)
-        total = term if total is None else total + term
-    out_ref[...] = total.astype(BF16)
-
-
-def project(first, second, w_halves):
+    _, zh, x = (place_ref[i] for i in range(3))
+
+    def write(w_ref):
+        total = None
+        for g in range(GRP):
+            weights = []
+            for other_zh in range(2):
+                for other_x in range(XS):
+                    turn = (x - other_x + XS) % XS * 2 + (zh + other_zh) % 2
+                    weights.append(w_ref[pl.ds(pl.multiple_of(g * WIDTH + turn * part, part), part), :])
+            att = jnp.concatenate([first_ref[g], second_ref[g]], axis=1)
+            term = jnp.dot(att, jnp.concatenate(weights, 0), preferred_element_type=F32)
+            total = term if total is None else total + term
+        out_ref[...] = total.astype(BF16)
+
+    is_own = pl.program_id(0) < pl.num_programs(0) // 2
+    pl.when(is_own)(lambda: write(own_ref))
+    pl.when(jnp.logical_not(is_own))(lambda: write(other_ref))
+
+
+def project(place, first, second, own, other):
     columns = 512
-    per_half = D // 2 // columns
-    att = pl.BlockSpec((GRP, ROWS, PAIR), lambda j: (0, 0, 0))
+    half = D // 2 // columns
+    att = pl.BlockSpec((GRP, ROWS, PAIR), lambda j, place: (0, 0, 0))
     return pl.pallas_call(
         project_kernel,
-        grid=(D // columns,),
-        in_specs=[att, att, pl.BlockSpec((1, D, columns), lambda j: (j // per_half, 0, j % per_half))],
-        out_specs=pl.BlockSpec((ROWS, columns), lambda j: (0, j)),
+        grid_spec=pltpu.PrefetchScalarGridSpec(
+            num_scalar_prefetch=1,
+            grid=(2 * half,),
+            in_specs=[
+                att,
+                att,
+                pl.BlockSpec((D, columns), lambda j, place: (0, jnp.minimum(j, half - 1))),
+                pl.BlockSpec((D, columns), lambda j, place: (0, jnp.maximum(j - half, 0))),
+            ],
+            out_specs=pl.BlockSpec((ROWS, columns), lambda j, place: (0, (j + place[0] * half) % (2 * half))),
+        ),
         out_shape=jax.ShapeDtypeStruct((ROWS, D), BF16),
         compiler_params=pltpu.CompilerParams(vmem_limit_bytes=56 * 2**20),
         cost_estimate=cost(2 * ROWS * D * D, 10 * 10**6),
         name="project",
-    )(first, second, w_halves)
-
-
-def swap(value):
-    return lax.ppermute(value, "zh", [(0, 1), (1, 0)])
+    )(place, first, second, own, other)
+
+
+def shift(value, axis, step):
+    size = lax.axis_size(axis)
+    return lax.ppermute(value, axis, [(i, (i + step) % size) for i in range(size)])
+
+
+def turns(value, axis):
+    return [value] + [shift(value, axis, step) for step in range(1, lax.axis_size(axis))]
 
 
 def after(value, *events):
@@ -291,34 +321,31 @@
     own_two = lax.dynamic_slice_in_dim(offsets_two, first_head, OWN)
     own_three = lax.dynamic_slice_in_dim(offsets_three, first_head, OWN)
 
-    chunk_a, chunk_b, small = pack(offsets_two, offsets_three, queries, keys, values)
+    place = jnp.stack([lax.axis_index(name).astype(jnp.int32) for name in ("core", "zh", "x")])
+
+    bulk, rest, small = pack(offsets_two, offsets_three, queries, keys, values)
     got = lax.all_to_all(small, ("zl", "core", "x"), split_axis=0, concat_axis=0, tiled=True)
-    w_own = lax.dynamic_slice_in_dim(w_out, lax.axis_index("core") * half, half, axis=1)
-    w_other = swap(w_own)
-    upper = lax.axis_index("zh") == 1
-    w_both = jnp.concatenate([jnp.where(upper, w_other, w_own), jnp.where(upper, w_own, w_other)], 0)
-    w_columns = lax.all_gather(w_both, ("y", "x"), axis=0, tiled=True)
-
+    bulk = exchange(after(bulk, got)).reshape(SEG1, BULK)
     own = got[:, :PICK]
-    other = swap(own)
-    qkv_a = exchange(after(chunk_a, got)).reshape(SEG1, 3 * PAIR)
+    other = shift(own, "zh", 1)
+    w_rows = lax.dynamic_slice_in_dim(w_out, lax.axis_index("core") * half, half, axis=1)
+    w_rows = jnp.concatenate(turns(jnp.concatenate(turns(after(w_rows, got), "zh"), 0), "x"), 0)
+    w_own = lax.all_gather(w_rows, "y", axis=0, tiled=True)
     far = lax.all_gather(compact(own.reshape(H * PICK, PAIR), other.reshape(H * PICK, PAIR)), "y", axis=0, tiled=True)
     parts = sparse_levels(x.reshape(1), got, other, far)
-    back = [parts[0]]
-    for step in range(1, XS):
-        back.append(lax.ppermute(parts[step], "x", [(i, (i + step) % XS) for i in range(XS)]))
-    back = jnp.stack(back)
-    qkv_b = exchange(after(chunk_b, qkv_a)).reshape(SEG1, 3 * PAIR)
+    back = jnp.stack([parts[0]] + [shift(parts[step], "x", step) for step in range(1, XS)])
+    rest = exchange(after(rest, bulk, back)).reshape(SEG1, PAIR)
 
     def scalars(head):
         return jnp.concatenate([x.reshape(1), own_two[head : head + 2], own_three[head : head + 2]])
 
-    att_a = dense_level(0, scalars(0), qkv_a, back)
-    w_halves = lax.all_gather(after(w_columns, qkv_b), "core", axis=0, tiled=False)
-    att_b = dense_level(2, scalars(2), qkv_b, back)
-    out_a = exchange(after(att_a, qkv_b).reshape(GRP, ROWS, PAIR))
+    att_a = dense_level(0, scalars(0), bulk, bulk, back)
+    att_b = dense_level(2, scalars(2), rest, bulk, back)
+    w_own = after(w_own, att_a)
+    w_other = shift(w_own, "core", 1)
+    out_a = exchange(att_a.reshape(GRP, ROWS, PAIR))
     out_b = exchange(att_b.reshape(GRP, ROWS, PAIR))
-    return project(out_a, out_b, w_halves)
+    return project(place, out_a, out_b, w_own, w_other)
 
 
 def solution(mesh):

time: 233 us -> 237 us (1.017)
  blocking collectives: 123 us -> 20.6 us
  waiting for transfers between devices: 15.4 us -> 91.4 us
  starting transfers between devices: 42.7 us -> 73 us
  Pallas kernels: 30.1 us -> 35.2 us
  local copies, waits for them, and re-layouts: 6.43 us -> 1.9 us
    all_to_all x4 -> x0, blocking collectives: 102 us -> none  [the longest x1 31.8 us: local(): qkv_b = exchange(after(chunk_b, qkv_a)).reshape(SEG1, 3 * PAIR)]
    ppermute x5 -> x9, waiting for transfers between devices: 11.8 us -> 52.1 us  [shift(): lax.ppermute(value, axis, [(i, (i + step) % size) for i in range(size)])]
    all_to_all x0 -> x4, waiting for transfers between devices: none -> 28.2 us  [the longest x1 13.7 us: local(): lax.all_to_all(small, ('zl', 'core', 'x'), split_axis=0, concat_axis=0, t...]
    all_to_all x0 -> x4, starting transfers between devices: none -> 25.6 us  [the longest x1 11.5 us: local(): lax.all_to_all(small, ('zl', 'core', 'x'), split_axis=0, concat_axis=0, t...]
    ppermute x5 -> x9, starting transfers between devices: 27.4 us -> 43.1 us  [shift(): lax.ppermute(value, axis, [(i, (i + step) % size) for i in range(size)])]
    all_to_all x1, starting transfers between devices: 15.3 us -> 4.23 us  [local(): out_b = exchange(att_b.reshape(GRP, ROWS, PAIR))]
    all_to_all x1, waiting for transfers between devices: 3.63 us -> 11.1 us  [local(): out_b = exchange(att_b.reshape(GRP, ROWS, PAIR))]
    unnamed x16 -> x15, local copies, waits for them, and re-layouts: 5.33 us -> 1.6 us
  transfers between devices with their start and end apart: 8 -> 15, of which waited for: 4 -> 10; matrix products, arithmetic and copies ran while one was open for 0% -> 0% of each run, Pallas kernels for 10% -> 9%
where the time goes in v3:
time: 237 us
  waiting for transfers between devices  91.4 us (39%)
  starting transfers between devices  73 us (31%)
  Pallas kernels  35.2 us (15%)
  blocking collectives  20.6 us (9%)
  between operations  13.6 us (6%)
    ppermute x9, waiting for transfers between devices, shift(): lax.ppermute(value, axis, [(i, (i + step) % size) for i in range(size)])  52.1 us
    ppermute x9, starting transfers between devices, shift(): lax.ppermute(value, axis, [(i, (i + step) % size) for i in range(size)])  43.1 us
    all_gather x1, blocking collectives, local(): lax.all_gather(compact(own.reshape(H * PICK, PAIR), other.reshape(H * PIC...  20.6 us
    pallas_call x2, Pallas kernels, dense_level(): pl.pallas_call(functools.partial(dense_kernel, head), in_specs=[pl.BlockS...  17.7 us
    all_to_all x1, waiting for transfers between devices, local(): lax.all_to_all(small, ('zl', 'core', 'x'), split_axis=0, concat_axis=0, t...  13.7 us
    all_to_all x1, waiting for transfers between devices, local(): rest = exchange(after(rest, bulk, back)).reshape(SEG1, PAIR)  11.6 us
    all_to_all x1, starting transfers between devices, local(): lax.all_to_all(small, ('zl', 'core', 'x'), split_axis=0, concat_axis=0, t...  11.5 us
    all_to_all x1, waiting for transfers between devices, local(): out_b = exchange(att_b.reshape(GRP, ROWS, PAIR))  11.1 us
  transfers between devices with their start and end apart: 15, of which 10 were waited for; matrix products, arithmetic and copies ran while one was open for 0% of the time, Pallas kernels for 9%

profile of v3, /device:TPU:1, one launch (start us, length us, event | category | flops | bytes accessed | tf_op | source)
XLA Modules:
  0.0 236.5 jit_solution(5196814208910989703)
XLA Ops:
  6.5 6.4 %pack.1 = (bf16[8,192,640]{2,1,0:T(8,128)(2,1)}, bf16[8,192,128]{2,1,0:T(8,128)(2,1)}, bf16[32,48,128]{2,1,0:T(8,128)(2,1)}) custom-call(s32[32]{0:T(128)} %two_ref.1, s32[32]{0:T(128)} %three_ref.1, bf16[192,2048]{1,0:T(8,128)(2,1)} %q_ref.1, bf16[192,2048]{1,0:T(8,128)(2,1)} %k_ref.1, bf16[192,2048]{1,0:T(8,128)(2,1)} %v_ref.1), custom_call_target="tpu_custom_call" | custom-call | flops 1000000000 | bytes 5000000 | tf_op jit(solution)/shard_map/pack/pallas_call | solution.py:94
  13.0 11.5 %all-to-all-start = ((bf16[32,48,128]{2,1,0:T(8,128)(2,1)}), bf16[32,48,128]{2,1,0:T(8,128)(2,1)S(1)}, u32[]{:S(2)}, u32[]{:S(2)}) async-start(bf16[32,48,128]{2,1,0:T(8,128)(2,1)} %get-tuple-element.13), calls=%async_computation | async-start | bytes 786432 | tf_op jit(solution)/shard_map/all_to_all | solution.py:327
  24.6 13.7 %all-to-all-done.got_ref = bf16[32,48,128]{2,1,0:T(8,128)(2,1)S(1)} async-done(((bf16[32,48,128]{2,1,0:T(8,128)(2,1)}), bf16[32,48,128]{2,1,0:T(8,128)(2,1)S(1)}, u32[]{:S(2)}, u32[]{:S(2)}) %all-to-all-start) | async-done | bytes 393248 | tf_op jit(solution)/shard_map/all_to_all | solution.py:327
  38.3 7.9 %collective-permute-start.4 = (bf16[32,1024]{1,0:T(8,128)(2,1)S(1)}, bf16[32,1024]{1,0:T(8,128)(2,1)S(1)}, u32[]{:S(2)}, u32[]{:S(2)}) collective-permute-start(bf16[32,1024]{1,0:T(8,128)(2,1)S(1)} %constant_dynamic-slice_fusion), channel_id=1, source_target_pairs={{0,4},{4,0},{1,5},{5,1},{2,6},{6,2},{3,7},{7,3},{8,12},{12,8},{9,1... | collective-permute-start | bytes 196616 | tf_op jit(solution)/shard_map/ppermute | solution.py:305
  46.2 2.1 collective-permute-done.4
  48.4 2.4 %collective-permute-start.5 = (bf16[64,1024]{1,0:T(8,128)(2,1)S(1)}, bf16[64,1024]{1,0:T(8,128)(2,1)S(1)}, u32[]{:S(2)}, u32[]{:S(2)}) collective-permute-start(bf16[64,1024]{1,0:T(8,128)(2,1)S(1)} %get-tuple-element.23), channel_id=1, source_target_pairs={{0,1},{1,2},{2,3},{3,0},{4,5},{5,6},{6,7},{7,4},{8,9},{9,10},{10,1... | collective-permute-start | bytes 393224 | tf_op jit(solution)/shard_map/ppermute | solution.py:305
  50.8 3.0 %collective-permute-start.6 = (bf16[64,1024]{1,0:T(8,128)(2,1)S(1)}, bf16[64,1024]{1,0:T(8,128)(2,1)S(1)}, u32[]{:S(2)}, u32[]{:S(2)}) collective-permute-start(bf16[64,1024]{1,0:T(8,128)(2,1)S(1)} %get-tuple-element.23), channel_id=1, source_target_pairs={{0,2},{1,3},{2,0},{3,1},{4,6},{5,7},{6,4},{7,5},{8,10},{9,11},{10,... | collective-permute-start | bytes 393224 | tf_op jit(solution)/shard_map/ppermute | solution.py:305
  53.7 3.3 %collective-permute-start.7 = (bf16[64,1024]{1,0:T(8,128)(2,1)S(1)}, bf16[64,1024]{1,0:T(8,128)(2,1)S(1)}, u32[]{:S(2)}, u32[]{:S(2)}) collective-permute-start(bf16[64,1024]{1,0:T(8,128)(2,1)S(1)} %get-tuple-element.23), channel_id=1, source_target_pairs={{0,3},{1,0},{2,1},{3,2},{4,7},{5,4},{6,5},{7,6},{8,11},{9,8},{10,9... | collective-permute-start | bytes 393224 | tf_op jit(solution)/shard_map/ppermute | solution.py:305
  57.0 1.6 collective-permute-done.6
  58.6 2.6 %collective-permute-done.7 = bf16[64,1024]{1,0:T(8,128)(2,1)S(1)} collective-permute-done((bf16[64,1024]{1,0:T(8,128)(2,1)S(1)}, bf16[64,1024]{1,0:T(8,128)(2,1)S(1)}, u32[]{:S(2)}, u32[]{:S(2)}) %collective-permute-start.7) | collective-permute-done | bytes 131104 | tf_op jit(solution)/shard_map/ppermute | solution.py:305
  61.3 0.8 copy-done.3
  62.1 5.2 %all-to-all-start.1 = ((bf16[8,192,640]{2,1,0:T(8,128)(2,1)}), bf16[8,192,640]{2,1,0:T(8,128)(2,1)S(1)}, u32[]{:S(2)}, u32[]{:S(2)}) async-start(bf16[8,192,640]{2,1,0:T(8,128)(2,1)} %get-tuple-element.14), calls=%async_computation.1 | async-start | bytes 3932160 | tf_op jit(solution)/shard_map/all_to_all | solution.py:328
  67.3 7.4 %collective-permute-start = (bf16[32,32,128]{2,1,0:T(8,128)(2,1)S(1)}, bf16[32,32,128]{2,1,0:T(8,128)(2,1)S(1)}, u32[]{:S(2)}, u32[]{:S(2)}) collective-permute-start(bf16[32,32,128]{2,1,0:T(8,128)(2,1)S(1)} %slice.36), channel_id=1, source_target_pairs={{0,4},{4,0},{1,5},{5,1},{2,6},{6,2},{3,7},{7,3},{8,12},{12,8},{9,1... | collective-permute-start | bytes 786440 | tf_op jit(solution)/shard_map/ppermute | solution.py:305
  75.0 41.9 %collective-permute-done.other_ref = bf16[32,32,128]{2,1,0:T(8,128)(2,1)S(1)} collective-permute-done((bf16[32,32,128]{2,1,0:T(8,128)(2,1)S(1)}, bf16[32,32,128]{2,1,0:T(8,128)(2,1)S(1)}, u32[]{:S(2)}, u32[]{:S(2)}) %collective-permute-start) | collective-permute-done | bytes 262176 | tf_op jit(solution)/shard_map/ppermute | solution.py:305
  117.1 20.6 %all_gather.6.far_ref = bf16[1536,128]{1,0:T(8,128)(2,1)S(1)} all-gather(bf16[192,128]{1,0:T(8,128)(2,1)S(1)} %compact_three.1), channel_id=1, replica_groups=mesh['zl'=4,'core'=2,'y'=8,'zh'=2,'x'=4] {'y'}, dimensions={0}, use_global_device_ids=true | all-gather | bytes 442368 | tf_op jit(solution)/shard_map/all_gather | solution.py:334
  137.7 3.4 %sparse_levels.1 = bf16[4,8,32,128]{3,2,1,0:T(8,128)(2,1)S(1)} custom-call(s32[1]{0:T(128)} %bitcast.2.place_ref, bf16[32,48,128]{2,1,0:T(8,128)(2,1)S(1)} %all-to-all-done.got_ref, bf16[32,32,128]{2,1,0:T(8,128)(2,1)S(1)} %collective-permute-done.other_ref, bf16[1536,128]{1,0:T(8,128)(2,1)S(1)} %all_gather.6.far_ref), custom_call_target="tpu_custom_call" | custom-call | flops 4000000000 | bytes 2000000 | tf_op jit(solution)/shard_map/sparse_levels/pallas_call | solution.py:180
  141.2 4.3 %collective-permute-start.3 = (bf16[8,32,128]{2,1,0:T(8,128)(2,1)S(1)}, bf16[8,32,128]{2,1,0:T(8,128)(2,1)S(1)}, u32[]{:S(2)}, u32[]{:S(2)}) collective-permute-start(bf16[8,32,128]{2,1,0:T(8,128)(2,1)S(1)} %get-tuple-element.20), channel_id=1, source_target_pairs={{0,3},{1,0},{2,1},{3,2},{4,7},{5,4},{6,5},{7,6},{8,11},{9,8},{10,9... | collective-permute-start | bytes 196616 | tf_op jit(solution)/shard_map/ppermute | solution.py:305
  145.5 2.2 collective-permute-start.2
  147.7 2.2 collective-permute-start.1
  150.0 2.0 collective-permute-done.2
  152.0 1.9 collective-permute-done.1
  154.0 8.9 %dense_level.2 = bf16[1536,128]{1,0:T(8,128)(2,1)} custom-call(s32[5]{0:T(128)S(1)} %pad_add_fusion.1.scalar_ref, bf16[1536,640]{1,0:T(8,128)(2,1)S(1)} %bitcast.18, bf16[1536,640]{1,0:T(8,128)(2,1)S(1)} %bitcast.19, bf16[4,8,32,128]{3,2,1,0:T(8,128)(2,1)S(1)} %pad_maximum_fusion.back_ref), custom_call_target="tpu_custom_call" | custom-call | flops 10000000000 | bytes 4000000 | tf_op jit(solution)/shard_map/dense_level/pallas_call | solution.py:241
  162.8 10.4 %collective-permute-start.8 = (bf16[2048,1024]{1,0:T(8,128)(2,1)}, bf16[2048,1024]{1,0:T(8,128)(2,1)}, u32[]{:S(2)}, u32[]{:S(2)}) collective-permute-start(bf16[2048,1024]{1,0:T(8,128)(2,1)} %all-gather.2.cloned.1.call-done.own_ref), channel_id=1, source_target_pairs={{0,64},{64,0},{1,65},{65,1},{2,66},{66,2},{3,67},{67,3},{4,68},{68... | collective-permute-start | bytes 12582920 | tf_op jit(solution)/shard_map/ppermute | solution.py:305
  173.3 4.7 %all-to-all-start.3 = ((bf16[8,192,128]{2,1,0:T(8,128)(2,1)}), bf16[8,192,128]{2,1,0:T(8,128)(2,1)S(1)}, u32[]{:S(2)}, u32[]{:S(2)}) async-start(bf16[8,192,128]{2,1,0:T(8,128)(2,1)} %get-tuple-element.16), calls=%async_computation.3 | async-start | bytes 786432 | tf_op jit(solution)/shard_map/all_to_all | solution.py:337
  178.0 11.6 %all-to-all-done.3 = bf16[8,192,128]{2,1,0:T(8,128)(2,1)S(1)} async-done(((bf16[8,192,128]{2,1,0:T(8,128)(2,1)}), bf16[8,192,128]{2,1,0:T(8,128)(2,1)S(1)}, u32[]{:S(2)}, u32[]{:S(2)}) %all-to-all-start.3) | async-done | bytes 393248 | tf_op jit(solution)/shard_map/all_to_all | solution.py:337
  189.6 4.2 %all-to-all-start.2 = ((bf16[8,192,128]{2,1,0:T(8,128)(2,1)}), bf16[8,192,128]{2,1,0:T(8,128)(2,1)S(1)}, u32[]{:S(2)}, u32[]{:S(2)}) async-start(bf16[8,192,128]{2,1,0:T(8,128)(2,1)} %bitcast.12), calls=%async_computation.2 | async-start | bytes 786432 | tf_op jit(solution)/shard_map/all_to_all | solution.py:346
  193.8 8.8 %dense_level.3 = bf16[1536,128]{1,0:T(8,128)(2,1)} custom-call(s32[5]{0:T(128)S(1)} %pad_add_fusion.2.scalar_ref, bf16[1536,128]{1,0:T(8,128)(2,1)S(1)} %bitcast.22, bf16[1536,640]{1,0:T(8,128)(2,1)S(1)} %bitcast.20, bf16[4,8,32,128]{3,2,1,0:T(8,128)(2,1)S(1)} %pad_maximum_fusion.back_ref), custom_call_target="tpu_custom_call" | custom-call | flops 10000000000 | bytes 4000000 | tf_op jit(solution)/shard_map/dense_level/pallas_call | solution.py:241
  202.7 2.9 %all-to-all-done.2.first_ref = bf16[8,192,128]{2,1,0:T(8,128)(2,1)S(1)} async-done(((bf16[8,192,128]{2,1,0:T(8,128)(2,1)}), bf16[8,192,128]{2,1,0:T(8,128)(2,1)S(1)}, u32[]{:S(2)}, u32[]{:S(2)}) %all-to-all-start.2) | async-done | bytes 393248 | tf_op jit(solution)/shard_map/all_to_all | solution.py:346
  205.6 4.2 %all-to-all-start.4 = ((bf16[8,192,128]{2,1,0:T(8,128)(2,1)}), bf16[8,192,128]{2,1,0:T(8,128)(2,1)S(1)}, u32[]{:S(2)}, u32[]{:S(2)}) async-start(bf16[8,192,128]{2,1,0:T(8,128)(2,1)} %bitcast.14), calls=%async_computation.4 | async-start | bytes 786432 | tf_op jit(solution)/shard_map/all_to_all | solution.py:347
  210.4 11.1 %all-to-all-done.4.second_ref = bf16[8,192,128]{2,1,0:T(8,128)(2,1)S(1)} async-done(((bf16[8,192,128]{2,1,0:T(8,128)(2,1)}), bf16[8,192,128]{2,1,0:T(8,128)(2,1)S(1)}, u32[]{:S(2)}, u32[]{:S(2)}) %all-to-all-start.4) | async-done | bytes 393248 | tf_op jit(solution)/shard_map/all_to_all | solution.py:347
  221.5 0.8 copy-done.2
  222.3 7.4 %project.1 = bf16[192,2048]{1,0:T(8,128)(2,1)} custom-call(s32[3]{0:T(128)} %pad_add_fusion.place_ref, bf16[8,192,128]{2,1,0:T(8,128)(2,1)} %copy-done.1, bf16[8,192,128]{2,1,0:T(8,128)(2,1)} %copy-done.2, bf16[2048,1024]{1,0:T(8,128)(2,1)} %all-gather.2.cloned.1.call-done.own_ref, bf16[2048,1024]{1,0:T(8,128)(2,1)} %collective-permute-done.8.other_ref), custom_call_target="tpu_custom_call" | custom-call | flops 1610612736 | bytes 10000000 | tf_op jit(solution)/shard_map/project/pallas_call | solution.py:283
  (33 shorter events, 1.5 us)
Async XLA Ops:
  6.5 18.0 %copy-start = (bf16[32,2048]{1,0:T(8,128)(2,1)S(1)}, bf16[32,2048]{1,0:T(8,128)(2,1)}, u32[]{:S(2)}) copy-start(bf16[32,2048]{1,0:T(8,128)(2,1)} %param.11) | copy-start | bytes 393220
  13.0 61.7 %copy-start.4 = (s32[32]{0:T(128)S(1)}, s32[32]{0:T(128)}, u32[]{:S(2)}) copy-start(s32[32]{0:T(128)} %two_ref.1) | copy-start | bytes 388
  13.0 61.8 %copy-start.5 = (s32[32]{0:T(128)S(1)}, s32[32]{0:T(128)}, u32[]{:S(2)}) copy-start(s32[32]{0:T(128)} %three_ref.1) | copy-start | bytes 388
  13.0 25.3 %all-to-all-start = ((bf16[32,48,128]{2,1,0:T(8,128)(2,1)}), bf16[32,48,128]{2,1,0:T(8,128)(2,1)S(1)}, u32[]{:S(2)}, u32[]{:S(2)}) async-start(bf16[32,48,128]{2,1,0:T(8,128)(2,1)} %get-tuple-element.13), calls=%async_computation | async-start | bytes 786432 | tf_op jit(solution)/shard_map/all_to_all | solution.py:327
  24.5 138.3 %all-gather.2.cloned.1.call-start = ((), (), s32[]{:S(2)}) async-start(), calls=%async_computation.5 | async-start | bytes 4718592 | tf_op jit(solution)/shard_map/all_gather | solution.py:333
  38.3 10.0 %collective-permute-start.4 = (bf16[32,1024]{1,0:T(8,128)(2,1)S(1)}, bf16[32,1024]{1,0:T(8,128)(2,1)S(1)}, u32[]{:S(2)}, u32[]{:S(2)}) collective-permute-start(bf16[32,1024]{1,0:T(8,128)(2,1)S(1)} %constant_dynamic-slice_fusion), channel_id=1, source_target_pairs={{0,4},{4,0},{1,5},{5,1},{2,6},{6,2},{3,7},{7,3},{8,12},{12,8},{9,1... | collective-permute-start | bytes 196616 | tf_op jit(solution)/shard_map/ppermute | solution.py:305
  48.4 8.7 %collective-permute-start.5 = (bf16[64,1024]{1,0:T(8,128)(2,1)S(1)}, bf16[64,1024]{1,0:T(8,128)(2,1)S(1)}, u32[]{:S(2)}, u32[]{:S(2)}) collective-permute-start(bf16[64,1024]{1,0:T(8,128)(2,1)S(1)} %get-tuple-element.23), channel_id=1, source_target_pairs={{0,1},{1,2},{2,3},{3,0},{4,5},{5,6},{6,7},{7,4},{8,9},{9,10},{10,1... | collective-permute-start | bytes 393224 | tf_op jit(solution)/shard_map/ppermute | solution.py:305
  50.8 7.8 %collective-permute-start.6 = (bf16[64,1024]{1,0:T(8,128)(2,1)S(1)}, bf16[64,1024]{1,0:T(8,128)(2,1)S(1)}, u32[]{:S(2)}, u32[]{:S(2)}) collective-permute-start(bf16[64,1024]{1,0:T(8,128)(2,1)S(1)} %get-tuple-element.23), channel_id=1, source_target_pairs={{0,2},{1,3},{2,0},{3,1},{4,6},{5,7},{6,4},{7,5},{8,10},{9,11},{10,... | collective-permute-start | bytes 393224 | tf_op jit(solution)/shard_map/ppermute | solution.py:305
  53.7 7.5 %collective-permute-start.7 = (bf16[64,1024]{1,0:T(8,128)(2,1)S(1)}, bf16[64,1024]{1,0:T(8,128)(2,1)S(1)}, u32[]{:S(2)}, u32[]{:S(2)}) collective-permute-start(bf16[64,1024]{1,0:T(8,128)(2,1)S(1)} %get-tuple-element.23), channel_id=1, source_target_pairs={{0,3},{1,0},{2,1},{3,2},{4,7},{5,4},{6,5},{7,6},{8,11},{9,8},{10,9... | collective-permute-start | bytes 393224 | tf_op jit(solution)/shard_map/ppermute | solution.py:305
  61.2 0.8 copy-start.3
  62.1 91.9 %all-to-all-start.1 = ((bf16[8,192,640]{2,1,0:T(8,128)(2,1)}), bf16[8,192,640]{2,1,0:T(8,128)(2,1)S(1)}, u32[]{:S(2)}, u32[]{:S(2)}) async-start(bf16[8,192,640]{2,1,0:T(8,128)(2,1)} %get-tuple-element.14), calls=%async_computation.1 | async-start | bytes 3932160 | tf_op jit(solution)/shard_map/all_to_all | solution.py:328
  67.3 49.5 %collective-permute-start = (bf16[32,32,128]{2,1,0:T(8,128)(2,1)S(1)}, bf16[32,32,128]{2,1,0:T(8,128)(2,1)S(1)}, u32[]{:S(2)}, u32[]{:S(2)}) collective-permute-start(bf16[32,32,128]{2,1,0:T(8,128)(2,1)S(1)} %slice.36), channel_id=1, source_target_pairs={{0,4},{4,0},{1,5},{5,1},{2,6},{6,2},{3,7},{7,3},{8,12},{12,8},{9,1... | collective-permute-start | bytes 786440 | tf_op jit(solution)/shard_map/ppermute | solution.py:305
  141.2 8.8 %collective-permute-start.3 = (bf16[8,32,128]{2,1,0:T(8,128)(2,1)S(1)}, bf16[8,32,128]{2,1,0:T(8,128)(2,1)S(1)}, u32[]{:S(2)}, u32[]{:S(2)}) collective-permute-start(bf16[8,32,128]{2,1,0:T(8,128)(2,1)S(1)} %get-tuple-element.20), channel_id=1, source_target_pairs={{0,3},{1,0},{2,1},{3,2},{4,7},{5,4},{6,5},{7,6},{8,11},{9,8},{10,9... | collective-permute-start | bytes 196616 | tf_op jit(solution)/shard_map/ppermute | solution.py:305
  145.5 6.5 %collective-permute-start.2 = (bf16[8,32,128]{2,1,0:T(8,128)(2,1)S(1)}, bf16[8,32,128]{2,1,0:T(8,128)(2,1)S(1)}, u32[]{:S(2)}, u32[]{:S(2)}) collective-permute-start(bf16[8,32,128]{2,1,0:T(8,128)(2,1)S(1)} %get-tuple-element.21), channel_id=1, source_target_pairs={{0,2},{1,3},{2,0},{3,1},{4,6},{5,7},{6,4},{7,5},{8,10},{9,11},{10,... | collective-permute-start | bytes 196616 | tf_op jit(solution)/shard_map/ppermute | solution.py:305
  147.7 6.2 %collective-permute-start.1 = (bf16[8,32,128]{2,1,0:T(8,128)(2,1)S(1)}, bf16[8,32,128]{2,1,0:T(8,128)(2,1)S(1)}, u32[]{:S(2)}, u32[]{:S(2)}) collective-permute-start(bf16[8,32,128]{2,1,0:T(8,128)(2,1)S(1)} %get-tuple-element.22), channel_id=1, source_target_pairs={{0,1},{1,2},{2,3},{3,0},{4,5},{5,6},{6,7},{7,4},{8,9},{9,10},{10,1... | collective-permute-start | bytes 196616 | tf_op jit(solution)/shard_map/ppermute | solution.py:305
  162.8 58.7 %collective-permute-start.8 = (bf16[2048,1024]{1,0:T(8,128)(2,1)}, bf16[2048,1024]{1,0:T(8,128)(2,1)}, u32[]{:S(2)}, u32[]{:S(2)}) collective-permute-start(bf16[2048,1024]{1,0:T(8,128)(2,1)} %all-gather.2.cloned.1.call-done.own_ref), channel_id=1, source_target_pairs={{0,64},{64,0},{1,65},{65,1},{2,66},{66,2},{3,67},{67,3},{4,68},{68... | collective-permute-start | bytes 12582920 | tf_op jit(solution)/shard_map/ppermute | solution.py:305
  173.3 16.4 %all-to-all-start.3 = ((bf16[8,192,128]{2,1,0:T(8,128)(2,1)}), bf16[8,192,128]{2,1,0:T(8,128)(2,1)S(1)}, u32[]{:S(2)}, u32[]{:S(2)}) async-start(bf16[8,192,128]{2,1,0:T(8,128)(2,1)} %get-tuple-element.16), calls=%async_computation.3 | async-start | bytes 786432 | tf_op jit(solution)/shard_map/all_to_all | solution.py:337
  189.6 15.9 %all-to-all-start.2 = ((bf16[8,192,128]{2,1,0:T(8,128)(2,1)}), bf16[8,192,128]{2,1,0:T(8,128)(2,1)S(1)}, u32[]{:S(2)}, u32[]{:S(2)}) async-start(bf16[8,192,128]{2,1,0:T(8,128)(2,1)} %bitcast.12), calls=%async_computation.2 | async-start | bytes 786432 | tf_op jit(solution)/shard_map/all_to_all | solution.py:346
  205.6 15.9 %copy-start.1 = (bf16[8,192,128]{2,1,0:T(8,128)(2,1)}, bf16[8,192,128]{2,1,0:T(8,128)(2,1)S(1)}, u32[]{:S(2)}) copy-start(bf16[8,192,128]{2,1,0:T(8,128)(2,1)S(1)} %all-to-all-done.2.first_ref) | copy-start | bytes 1179652
  205.6 15.9 %all-to-all-start.4 = ((bf16[8,192,128]{2,1,0:T(8,128)(2,1)}), bf16[8,192,128]{2,1,0:T(8,128)(2,1)S(1)}, u32[]{:S(2)}, u32[]{:S(2)}) async-start(bf16[8,192,128]{2,1,0:T(8,128)(2,1)} %bitcast.14), calls=%async_computation.4 | async-start | bytes 786432 | tf_op jit(solution)/shard_map/all_to_all | solution.py:347
  221.5 0.8 copy-start.2
Sparse Core Ops, SparseCore 0:
  62.2 59.4 all-gather.1

commit v4 on v3

v4 whole, which is shorter than its diff:
```python
import functools
import math

import jax
import jax.numpy as jnp
from jax import lax
from jax.experimental import pallas as pl
from jax.experimental.pallas import tpu as pltpu
from jax.sharding import Mesh
from jax.sharding import PartitionSpec as P

H = 32
HD = 64
PAIR = 2 * HD
R2 = 8
R3 = 64
D = H * HD
GRP = 8
XS = 4
ZH = 2
ROWS = 192
SEG1 = ROWS * GRP
OWN = H // GRP
WIDTH = OWN * HD
LOCAL2 = ROWS // R2
LOCAL3 = ROWS // R3
PICK = 32
SENT = PICK + PICK // 2
BLOCK = 256
PART = 256
PER_STEP = 2
SCALE2 = HD**-0.5 * math.log2(math.e)
VMEM_LIMIT = 40 * 2**20
GROUP = ("zl", "core")
NT = (((1,), (1,)), ((), ()))
BF16 = jnp.bfloat16
F32 = jnp.float32


def fine_mesh(mesh):
    return Mesh(mesh.devices.reshape(4, 2, 8, 2, XS), ("zl", "core", "y", "zh", "x"))


def params():
    return pltpu.CompilerParams(vmem_limit_bytes=VMEM_LIMIT)


def cost(flops, traffic, transcendentals=0):
    return pl.CostEstimate(flops=flops, bytes_accessed=traffic, transcendentals=transcendentals)


def iota(shape, dim):
    return lax.broadcasted_iota(jnp.int32, shape, dim)


def pick_kernel(two_ref, three_ref, q_ref, k_ref, v_ref, small_ref):
    for group in range(PER_STEP):
        pick_group(group, two_ref, three_ref, q_ref, k_ref, v_ref, small_ref)


def pick_group(group, two_ref, three_ref, q_ref, k_ref, v_ref, small_ref):
    step = pl.program_id(0) * PER_STEP + group
    columns = slice(group * WIDTH, (group + 1) * WIDTH)
    row = iota((OWN * PICK, ROWS), 0)
    place = row % PICK
    target = jnp.full((OWN * PICK, ROWS), -1, jnp.int32)
    for i in range(OWN):
        two = place * R2 + two_ref[step * OWN + i]
        three = (place - LOCAL2) * R3 + three_ref[step * OWN + i]
        own = jnp.where(place < LOCAL2, two, jnp.where(place < LOCAL2 + LOCAL3, three, -1))
        target = jnp.where(row // PICK == i, own, target)
    onehot = jnp.where(iota((OWN * PICK, ROWS), 1) == target, 1.0, 0.0).astype(BF16)
    picked = [jnp.dot(onehot, ref[:, columns], preferred_element_type=F32) for ref in (q_ref, k_ref, v_ref)]
    low = iota((PICK, PAIR), 1) < HD
    for i in range(OWN):
        rows, lanes = slice(i * PICK, (i + 1) * PICK), slice(i // 2 * PAIR, (i // 2 + 1) * PAIR)
        q, k, v = (part[rows, lanes] for part in picked)
        if i % 2:
            k = pltpu.roll(k, HD, 1)
            head, tail = pltpu.roll(q[: PICK // 2], HD, 1), q[PICK // 2 :]
        else:
            v = pltpu.roll(v, HD, 1)
            head, tail = q[: PICK // 2], pltpu.roll(q[PICK // 2 :], HD, 1)
        kv = jnp.where(low, k, v).astype(BF16)
        lines = jnp.where(low[: PICK // 2], head, tail).astype(BF16)
        for zh in range(ZH):
            small_ref[group * OWN + i, zh, :PICK, :] = kv
            small_ref[group * OWN + i, zh, PICK:, :] = lines


def pick(offsets_two, offsets_three, queries, keys, values):
    block = pl.BlockSpec((ROWS, PER_STEP * WIDTH), lambda j, *_: (0, j))
    return pl.pallas_call(
        pick_kernel,
        grid_spec=pltpu.PrefetchScalarGridSpec(
            num_scalar_prefetch=2,
            grid=(GRP // PER_STEP,),
            in_specs=[block] * 3,
            out_specs=pl.BlockSpec((PER_STEP * OWN, ZH, SENT, PAIR), lambda j, *_: (j, 0, 0, 0)),
        ),
        out_shape=jax.ShapeDtypeStruct((H, ZH, SENT, PAIR), BF16),
        compiler_params=pltpu.CompilerParams(vmem_limit_bytes=56 * 2**20),
        cost_estimate=cost(10**9, 4 * 10**6),
        name="pick",
    )(offsets_two, offsets_three, queries, keys, values)


def pack_kernel(q_ref, k_ref, v_ref, first_ref, second_ref):
    for pair, out_ref in enumerate((first_ref, second_ref)):
        for which, ref in enumerate((q_ref, k_ref, v_ref)):
            out_ref[0, :, which * PAIR : (which + 1) * PAIR] = ref[:, pair * PAIR : (pair + 1) * PAIR]


def pack(queries, keys, values):
    block = pl.BlockSpec((ROWS, WIDTH), lambda j: (0, j))
    chunk = pl.BlockSpec((1, ROWS, 3 * PAIR), lambda j: (j, 0, 0))
    shape = jax.ShapeDtypeStruct((GRP, ROWS, 3 * PAIR), BF16)
    return pl.pallas_call(
        pack_kernel,
        grid=(GRP,),
        in_specs=[block] * 3,
        out_specs=[chunk] * 2,
        out_shape=[shape] * 2,
        compiler_params=pltpu.CompilerParams(vmem_limit_bytes=56 * 2**20),
        cost_estimate=cost(0, 5 * 10**6),
        name="pack",
    )(queries, keys, values)


def compact_kernel(got_ref, out_ref):
    count, keys = ZH * H * LOCAL3, ZH * H * PICK
    row = iota((count, keys), 0)
    target = row // LOCAL3 * PICK + LOCAL2 + row % LOCAL3
    onehot = jnp.where(iota((count, keys), 1) == target, 1.0, 0.0).astype(BF16)
    chosen = jnp.dot(onehot, got_ref[:, :, :PICK, :].reshape(keys, PAIR), preferred_element_type=F32)
    out_ref[...] = chosen.astype(BF16)


def compact(got):
    return pl.pallas_call(
        compact_kernel,
        out_shape=jax.ShapeDtypeStruct((ZH * H * LOCAL3, PAIR), BF16),
        compiler_params=params(),
        cost_estimate=cost(10**8, 10**6),
        name="compact_three",
    )(got)


def sparse_kernel(place_ref, got_ref, far_ref, out_ref):
    low = iota((1, PAIR), 1) < HD
    one = jnp.ones((), BF16)
    near = got_ref[:, :, :PICK, :].reshape(ZH * H * PICK, PAIR)
    far = far_ref[...]
    half = PICK // 2
    raw = got_ref[:, pl.ds(place_ref[1], 1), PICK:, :].reshape(H * half, PAIR).astype(F32)
    head = jnp.where(low, raw, 0.0)
    tail = jnp.where(low, pltpu.roll(raw, HD, 1), 0.0).reshape(H, half, PAIR)
    tail_two = tail[:, : LOCAL2 - half].reshape(-1, PAIR)
    tail_three = tail[:, LOCAL2 - half :].reshape(-1, PAIR)

    def attend(q, kv, masked):
        scores = lax.dot_general(q.astype(BF16), kv, NT, preferred_element_type=F32)
        if masked:
            scores = jnp.where(iota((1, kv.shape[0]), 1) % PICK < LOCAL2, scores, -1e30)
        largest = jnp.max(scores, axis=-1, keepdims=True)
        expo = jnp.exp2((scores - largest) * SCALE2).astype(BF16)
        total = jnp.dot(expo, jnp.where(low, one, kv), preferred_element_type=F32)
        weight = total[:, :1]
        log_sum = largest * SCALE2 + jnp.log2(weight)
        top = log_sum.astype(BF16).astype(F32)
        middle = (log_sum - top).astype(BF16).astype(F32)
        rest = log_sum - top - middle
        lane = iota((1, PAIR), 1)
        stats = jnp.where(lane < 16, top, jnp.where(lane < 32, middle, rest))
        return jnp.where(low, stats, total / weight)

    rows = H * half // 2
    first = jnp.concatenate([attend(head[:rows], near, True), attend(head[rows:], near, True)], 0)
    first = first.reshape(GRP, XS, half, PAIR)
    second = attend(tail_two, near, True).reshape(GRP, XS, LOCAL2 - half, PAIR)
    third = attend(tail_three, far, False).reshape(GRP, XS, PICK - LOCAL2, PAIR)
    second = jnp.concatenate([second, third], axis=2)
    for x in range(XS):
        where = (x - place_ref[0] + XS) % XS
        out_ref[where, :, :half, :] = first[:, x].astype(BF16)
        out_ref[where, :, half:, :] = second[:, x].astype(BF16)


def sparse_levels(place, got, far):
    shape = (XS, GRP, PICK, PAIR)
    return pl.pallas_call(
        sparse_kernel,
        in_specs=[pl.BlockSpec(memory_space=pltpu.SMEM)] + [pl.BlockSpec(memory_space=pltpu.VMEM)] * 2,
        out_shape=jax.ShapeDtypeStruct(shape, BF16),
        compiler_params=params(),
        cost_estimate=cost(4 * 10**9, 2 * 10**6, 2 * 10**6),
        name="sparse_levels",
    )(place, got, far)


def dense_kernel(pair, scalar_ref, qkv_ref, back_ref, out_ref, acc, top, aug, scores, few):
    zero, one = jnp.zeros((), BF16), jnp.ones((), BF16)
    blocks, parts = SEG1 // BLOCK, SEG1 // PART

    def mine(parity, rows):
        lane = iota((rows, PAIR), 1)
        return (lane >= HD) if parity else (lane < HD)

    def rows_of(block):
        return pl.ds(pl.multiple_of(block * BLOCK, BLOCK), BLOCK)

    columns, keys, values = (slice(i * PAIR, (i + 1) * PAIR) for i in range(3))
    for parity in range(2):
        aug[parity] = jnp.where(mine(parity, SEG1), qkv_ref[:, values], one)

    def step(ahead, parity, largest, block):
        q, expected, total = None, None, None
        if ahead is not None:
            q = jnp.where(mine(ahead[0], BLOCK), qkv_ref[rows_of(ahead[1]), columns], zero)
        for part in range(parts):
            lanes = slice(part * PART, (part + 1) * PART)
            if ahead is not None:
                fresh = lax.dot_general(q, qkv_ref[lanes, keys], NT, preferred_element_type=F32)
                scores[ahead[0], :, lanes] = fresh
                for i in range(0, PART, PAIR):
                    piece = fresh[:, i : i + PAIR]
                    expected = piece if expected is None else jnp.maximum(expected, piece)
            if parity is not None:
                expo = jnp.exp2((scores[parity, :, lanes] - largest) * SCALE2).astype(BF16)
                term = jnp.dot(expo, aug[parity, lanes, :], preferred_element_type=F32)
                total = term if total is None else total + term
        if parity is not None:
            acc[parity, rows_of(block), :] = total
            top[parity, rows_of(block), :] = jnp.broadcast_to(largest * SCALE2, (BLOCK, PAIR))
        if ahead is not None:
            return jnp.max(expected, axis=-1, keepdims=True)

    def level_one(block, largest):
        other = step((1, block), 0, largest, block)
        return step((0, jnp.minimum(block + 1, blocks - 1)), 1, other, block)

    lax.fori_loop(0, blocks, level_one, step((0, 0), None, None, None))

    for parity in range(2):
        head = pair * 2 + parity
        back = back_ref[(scalar_ref[0] - head + XS) % XS].astype(F32)

        def merge(rows, part, parity=parity):
            log_sum = part[:, 0:1] + part[:, 16:17] + part[:, 32:33]
            shaped = part if parity else pltpu.roll(part, HD, 1)
            shaped = jnp.where(mine(parity, part.shape[0]), shaped, 1.0)
            old = top[parity, rows, :]
            peak = jnp.maximum(old, log_sum)
            top[parity, rows, :] = peak
            acc[parity, rows, :] = acc[parity, rows, :] * jnp.exp2(old - peak) + shaped * jnp.exp2(log_sum - peak)

        merge(pl.ds(scalar_ref[1 + head], SEG1 // R2, stride=R2), back[:, :LOCAL2].reshape(SEG1 // R2, PAIR))
        for g in range(GRP):
            few[g * LOCAL3 : (g + 1) * LOCAL3, :] = back[g, LOCAL2 : LOCAL2 + LOCAL3]
        merge(pl.ds(scalar_ref[1 + OWN + head], SEG1 // R3, stride=R3), few[...])
    result = [acc[parity] / pltpu.roll(acc[parity], HD, 1) for parity in range(2)]
    out_ref[...] = jnp.where(mine(0, SEG1), result[0], result[1]).astype(BF16)


def dense_level(pair, scalars, qkv, back):
    return pl.pallas_call(
        functools.partial(dense_kernel, pair),
        in_specs=[pl.BlockSpec(memory_space=pltpu.SMEM)] + [pl.BlockSpec(memory_space=pltpu.VMEM)] * 2,
        out_shape=jax.ShapeDtypeStruct((SEG1, PAIR), BF16),
        scratch_shapes=[
            pltpu.VMEM((2, SEG1, PAIR), F32),
            pltpu.VMEM((2, SEG1, PAIR), F32),
            pltpu.VMEM((2, SEG1, PAIR), BF16),
            pltpu.VMEM((2, BLOCK, SEG1), F32),
            pltpu.VMEM((SEG1 // R3, PAIR), F32),
        ],
        compiler_params=params(),
        cost_estimate=cost(10 * 10**9, 2 * 10**6, 5 * 10**6),
        name="dense_level",
    )(scalars, qkv, back)


def project_kernel(place_ref, first_ref, second_ref, own_ref, own_far_ref, other_ref, other_far_ref, out_ref):
    upper = place_ref[1] == 1
    part = WIDTH // ZH

    def write(near_ref, far_ref):
        total = None
        for g in range(GRP):
            rows = slice(g * part, (g + 1) * part)
            near = jnp.where(upper, second_ref[g], first_ref[g])
            far = jnp.where(upper, first_ref[g], second_ref[g])
            term = jnp.dot(
                jnp.concatenate([near, far], 1),
                jnp.concatenate([near_ref[rows, :], far_ref[rows, :]], 0),
                preferred_element_type=F32,
            )
            total = term if total is None else total + term
        out_ref[...] = total.astype(BF16)

    is_own = pl.program_id(0) < pl.num_programs(0) // 2
    pl.when(is_own)(lambda: write(own_ref, own_far_ref))
    pl.when(jnp.logical_not(is_own))(lambda: write(other_ref, other_far_ref))


def project(place, first, second, own, own_far, other, other_far):
    columns = 512
    half = D // 2 // columns
    att = pl.BlockSpec((GRP, ROWS, PAIR), lambda j, place: (0, 0, 0))
    early = pl.BlockSpec((D // ZH, columns), lambda j, place: (0, jnp.minimum(j, half - 1)))
    late = pl.BlockSpec((D // ZH, columns), lambda j, place: (0, jnp.maximum(j - half, 0)))
    return pl.pallas_call(
        project_kernel,
        grid_spec=pltpu.PrefetchScalarGridSpec(
            num_scalar_prefetch=1,
            grid=(2 * half,),
            in_specs=[att, att, early, early, late, late],
            out_specs=pl.BlockSpec((ROWS, columns), lambda j, place: (0, (j + place[0] * half) % (2 * half))),
        ),
        out_shape=jax.ShapeDtypeStruct((ROWS, D), BF16),
        compiler_params=pltpu.CompilerParams(vmem_limit_bytes=24 * 2**20),
        cost_estimate=cost(2 * ROWS * D * D, 10 * 10**6),
        name="project",
    )(place, first, second, own, own_far, other, other_far)


def shift(value, axis, step):
    size = lax.axis_size(axis)
    return lax.ppermute(value, axis, [(i, (i + step) % size) for i in range(size)])


def after(value, *events):
    return lax.optimization_barrier((value, *events))[0]


def local(queries, keys, values, offsets_two, offsets_three, w_out):
    half = D // 2
    exchange = functools.partial(lax.all_to_all, axis_name=GROUP, split_axis=0, concat_axis=0, tiled=True)
    x = lax.axis_index("x")
    first_head = lax.axis_index(GROUP) * OWN
    own_two = lax.dynamic_slice_in_dim(offsets_two, first_head, OWN)
    own_three = lax.dynamic_slice_in_dim(offsets_three, first_head, OWN)

    core, zh = lax.axis_index("core"), lax.axis_index("zh")

    w_rows = lax.dynamic_slice_in_dim(w_out, core * half, half, axis=1)
    w_own = lax.all_gather(w_rows, ("y", "x"), axis=0, tiled=True)
    small = pick(offsets_two, offsets_three, queries, keys, values)
    chunk_a, chunk_b = pack(after(queries, small), keys, values)
    got = lax.all_to_all(
        small.reshape(H * ZH, SENT, PAIR), ("zl", "core", "x", "zh"), split_axis=0, concat_axis=0, tiled=True
    ).reshape(H, ZH, SENT, PAIR)
    far_rows = shift(after(w_rows, chunk_a), "zh", 1)
    w_own_far = lax.all_gather(far_rows, ("y", "x"), axis=0, tiled=True)

    qkv_a = exchange(after(chunk_a, got, far_rows)).reshape(SEG1, 3 * PAIR)
    far = lax.all_gather(compact(got), "y", axis=0, tiled=True)
    qkv_b = exchange(after(chunk_b, qkv_a, far)).reshape(SEG1, 3 * PAIR)
    parts = sparse_levels(jnp.stack([x, zh]), got, far)
    back = jnp.stack([parts[0]] + [shift(parts[step], "x", step) for step in range(1, XS)])
    scalars = jnp.concatenate([x.reshape(1), own_two, own_three])
    att_a = dense_level(0, scalars, qkv_a, back)
    out_a = exchange(after(att_a, qkv_b).reshape(GRP, ROWS, PAIR))
    att_b = dense_level(1, scalars, after(qkv_b, att_a), back)
    out_b = exchange(att_b.reshape(GRP, ROWS, PAIR))
    w_other = shift(after(w_own, att_a), "core", 1)
    w_other_far = shift(after(w_own_far, att_b), "core", 1)
    return project(jnp.stack([core, zh]), out_a, out_b, w_own, w_own_far, w_other, w_other_far)


def solution(mesh):
    rows = P(("y", "zh", "x", "zl", "core"), None)
    return jax.shard_map(
        local,
        mesh=fine_mesh(mesh),
        in_specs=(rows, rows, rows, P(), P(), P(("y", "zh", "x"), None)),
        out_specs=rows,
        check_vma=False,
    )
```

time: 237 us -> 235 us (level)
  blocking collectives: 20.6 us -> 40.3 us
  starting transfers between devices: 73 us -> 56.6 us
  waiting for transfers between devices: 91.4 us -> 75.7 us
  local copies, waits for them, and re-layouts: 1.9 us -> 7.45 us
  Pallas kernels: 35.2 us -> 39.8 us
    all_gather x1 -> x2, waiting for transfers between devices: 0.01 us -> 44.7 us  [the longest x1 44.7 us: local(): w_own_far = lax.all_gather(far_rows, ('y', 'x'), axis=0, tiled=True)]
    ppermute x9 -> x6, waiting for transfers between devices: 52.1 us -> 14.6 us  [shift(): lax.ppermute(value, axis, [(i, (i + step) % size) for i in range(size)])]
    all_to_all x4 -> x3, waiting for transfers between devices: 28.2 us -> 4.05 us  [the longest x1 4.05 us: local(): qkv_a = exchange(after(chunk_a, got, far_rows)).reshape(SEG1, 3 * PAIR)]
    ppermute x9 -> x6, starting transfers between devices: 43.1 us -> 24.7 us  [shift(): lax.ppermute(value, axis, [(i, (i + step) % size) for i in range(size)])]
    all_to_all x0 -> x1, blocking collectives: none -> 16.9 us  [local(): out_a = exchange(after(att_a, qkv_b).reshape(GRP, ROWS, PAIR))]
    unnamed x15 -> x24, local copies, waits for them, and re-layouts: 1.6 us -> 6.67 us
    pallas_call x4 -> x5, Pallas kernels: 24.4 us -> 29.4 us  [the longest x2 18 us: dense_level(): pl.pallas_call(functools.partial(dense_kernel, pair), in_specs=[pl.BlockS...]
    all_gather x1, blocking collectives: 20.6 us -> 23.4 us  [local(): far = lax.all_gather(compact(got), 'y', axis=0, tiled=True)]
  transfers between devices with their start and end apart: 15 -> 12, of which waited for: 10 -> 6; matrix products, arithmetic and copies ran while one was open for 0% -> 0% of each run, Pallas kernels for 9% -> 14%
where the time goes in v4:
time: 235 us; the launch traced here: 234 us
  waiting for transfers between devices  75.7 us (32%)
  starting transfers between devices  56.6 us (24%)
  blocking collectives  40.3 us (17%)
  Pallas kernels  39.8 us (17%)
  between operations  13.6 us (6%)
  local copies, waits for them, and re-layouts  7.45 us (3%)
    all_gather x1, waiting for transfers between devices, local(): w_own_far = lax.all_gather(far_rows, ('y', 'x'), axis=0, tiled=True)  44.7 us
    ppermute x6, starting transfers between devices, shift(): lax.ppermute(value, axis, [(i, (i + step) % size) for i in range(size)])  24.7 us
    all_gather x1, blocking collectives, local(): far = lax.all_gather(compact(got), 'y', axis=0, tiled=True)  23.4 us
    pallas_call x2, Pallas kernels, dense_level(): pl.pallas_call(functools.partial(dense_kernel, pair), in_specs=[pl.BlockS...  18 us
    all_to_all x1, blocking collectives, local(): out_a = exchange(after(att_a, qkv_b).reshape(GRP, ROWS, PAIR))  16.9 us
    all_to_all x1, starting transfers between devices, local(): lax.all_to_all(small.reshape(H * ZH, SENT, PAIR), ('zl', 'core', 'x', 'zh...  15 us
    ppermute x6, waiting for transfers between devices, shift(): lax.ppermute(value, axis, [(i, (i + step) % size) for i in range(size)])  14.6 us
    all_to_all x1, waiting for transfers between devices, local(): out_b = exchange(att_b.reshape(GRP, ROWS, PAIR))  11.6 us
  transfers between devices with their start and end apart: 12, of which 6 were waited for; matrix products, arithmetic and copies ran while one was open for 0% of the time, Pallas kernels for 14%

profile of v4, /device:TPU:1, one launch (start us, length us, event | category | flops | bytes accessed | tf_op | source)
XLA Modules:
  0.0 233.6 jit_solution(17206296442291382401)
XLA Ops:
  6.5 0.9 copy-done
  8.1 4.9 %pick.1 = bf16[32,2,48,128]{3,2,1,0:T(8,128)(2,1)} custom-call(s32[32]{0:T(128)} %two_ref.1, s32[32]{0:T(128)} %three_ref.1, bf16[192,2048]{1,0:T(8,128)(2,1)} %q_ref.2, bf16[192,2048]{1,0:T(8,128)(2,1)} %k_ref.3, bf16[192,2048]{1,0:T(8,128)(2,1)} %v_ref.3), custom_call_target="tpu_custom_call" | custom-call | flops 1000000000 | bytes 4000000 | tf_op jit(solution)/shard_map/pick/pallas_call | solution.py:93
  13.0 15.0 %all-to-all-start = ((bf16[64,48,128]{2,1,0:T(8,128)(2,1)}), bf16[64,48,128]{2,1,0:T(8,128)(2,1)S(1)}, u32[]{:S(2)}, u32[]{:S(2)}) async-start(bf16[64,48,128]{2,1,0:T(8,128)(2,1)} %bitcast.24), calls=%async_computation | async-start | bytes 1572864 | tf_op jit(solution)/shard_map/all_to_all | solution.py:350
  28.0 6.1 %pack.1 = (bf16[8,192,384]{2,1,0:T(8,128)(2,1)}, bf16[8,192,384]{2,1,0:T(8,128)(2,1)}) custom-call(bf16[192,2048]{1,0:T(8,128)(2,1)} %q_ref.2, bf16[192,2048]{1,0:T(8,128)(2,1)} %k_ref.3, bf16[192,2048]{1,0:T(8,128)(2,1)} %v_ref.3), custom_call_target="tpu_custom_call" | custom-call | bytes 5000000 | tf_op jit(solution)/shard_map/pack/pallas_call | solution.py:118
  34.1 7.2 %collective-permute-start = (bf16[32,1024]{1,0:T(8,128)(2,1)S(1)}, bf16[32,1024]{1,0:T(8,128)(2,1)S(1)}, u32[]{:S(2)}, u32[]{:S(2)}) collective-permute-start(bf16[32,1024]{1,0:T(8,128)(2,1)S(1)} %copy-done.8), channel_id=1, source_target_pairs={{0,4},{4,0},{1,5},{5,1},{2,6},{6,2},{3,7},{7,3},{8,12},{12,8},{9,1... | collective-permute-start | bytes 196616 | tf_op jit(solution)/shard_map/ppermute | solution.py:329
  41.3 10.7 %collective-permute-done = bf16[32,1024]{1,0:T(8,128)(2,1)S(1)} collective-permute-done((bf16[32,1024]{1,0:T(8,128)(2,1)S(1)}, bf16[32,1024]{1,0:T(8,128)(2,1)S(1)}, u32[]{:S(2)}, u32[]{:S(2)}) %collective-permute-start) | collective-permute-done | bytes 65568 | tf_op jit(solution)/shard_map/ppermute | solution.py:329
  52.0 5.9 %all-to-all-start.1 = ((bf16[8,192,384]{2,1,0:T(8,128)(2,1)}), bf16[8,192,384]{2,1,0:T(8,128)(2,1)S(1)}, u32[]{:S(2)}, u32[]{:S(2)}) async-start(bf16[8,192,384]{2,1,0:T(8,128)(2,1)} %get-tuple-element.18), calls=%async_computation.1 | async-start | bytes 2359296 | tf_op jit(solution)/shard_map/all_to_all | solution.py:356
  58.0 0.7 all-gather.5.cloned.1.call-update
  59.0 23.4 %all_gather.9.far_ref = bf16[1536,128]{1,0:T(8,128)(2,1)} all-gather(bf16[192,128]{1,0:T(8,128)(2,1)S(1)} %compact_three.1), channel_id=1, replica_groups=mesh['zl'=4,'core'=2,'y'=8,'zh'=2,'x'=4] {'y'}, dimensions={0}, use_global_device_ids=true | all-gather | bytes 442368 | tf_op jit(solution)/shard_map/all_gather | solution.py:357
  82.4 4.0 %all-to-all-done.1 = bf16[8,192,384]{2,1,0:T(8,128)(2,1)S(1)} async-done(((bf16[8,192,384]{2,1,0:T(8,128)(2,1)}), bf16[8,192,384]{2,1,0:T(8,128)(2,1)S(1)}, u32[]{:S(2)}, u32[]{:S(2)}) %all-to-all-start.1) | async-done | bytes 1179680 | tf_op jit(solution)/shard_map/all_to_all | solution.py:356
  86.5 6.8 %all-to-all-start.2 = ((bf16[8,192,384]{2,1,0:T(8,128)(2,1)}), bf16[8,192,384]{2,1,0:T(8,128)(2,1)S(1)}, u32[]{:S(2)}, u32[]{:S(2)}) async-start(bf16[8,192,384]{2,1,0:T(8,128)(2,1)} %get-tuple-element.20), calls=%async_computation.2 | async-start | bytes 2359296 | tf_op jit(solution)/shard_map/all_to_all | solution.py:358
  93.4 1.0 copy-done.3
  94.4 3.9 %sparse_levels.1 = bf16[4,8,32,128]{3,2,1,0:T(8,128)(2,1)S(1)} custom-call(s32[2]{0:T(128)S(1)} %pad_add_fusion.2.place_ref, bf16[32,2,48,128]{3,2,1,0:T(8,128)(2,1)S(1)} %bitcast.19, bf16[1536,128]{1,0:T(8,128)(2,1)S(1)} %copy-done.3), custom_call_target="tpu_custom_call" | custom-call | flops 4000000000 | bytes 2000000 | tf_op jit(solution)/shard_map/sparse_levels/pallas_call | solution.py:191
  98.4 3.0 %collective-permute-start.3 = (bf16[8,32,128]{2,1,0:T(8,128)(2,1)S(1)}, bf16[8,32,128]{2,1,0:T(8,128)(2,1)S(1)}, u32[]{:S(2)}, u32[]{:S(2)}) collective-permute-start(bf16[8,32,128]{2,1,0:T(8,128)(2,1)S(1)} %get-tuple-element.26), channel_id=1, source_target_pairs={{0,3},{1,0},{2,1},{3,2},{4,7},{5,4},{6,5},{7,6},{8,11},{9,8},{10,9... | collective-permute-start | bytes 196616 | tf_op jit(solution)/shard_map/ppermute | solution.py:329
  101.5 2.2 collective-permute-start.2
  103.7 2.6 %collective-permute-start.1 = (bf16[8,32,128]{2,1,0:T(8,128)(2,1)S(1)}, bf16[8,32,128]{2,1,0:T(8,128)(2,1)S(1)}, u32[]{:S(2)}, u32[]{:S(2)}) collective-permute-start(bf16[8,32,128]{2,1,0:T(8,128)(2,1)S(1)} %get-tuple-element.28), channel_id=1, source_target_pairs={{0,1},{1,2},{2,3},{3,0},{4,5},{5,6},{6,7},{7,4},{8,9},{9,10},{10,1... | collective-permute-start | bytes 196616 | tf_op jit(solution)/shard_map/ppermute | solution.py:329
  106.3 1.8 collective-permute-done.2
  108.1 2.1 collective-permute-done.1
  110.3 9.0 %dense_level.2 = bf16[1536,128]{1,0:T(8,128)(2,1)S(1)} custom-call(s32[9]{0:T(128)S(1)} %pad_add_fusion.1.scalar_ref, bf16[1536,384]{1,0:T(8,128)(2,1)S(1)} %bitcast.20, bf16[4,8,32,128]{3,2,1,0:T(8,128)(2,1)S(1)} %pad_maximum_fusion.back_ref), custom_call_target="tpu_custom_call" | custom-call | flops 10000000000 | bytes 2000000 | tf_op jit(solution)/shard_map/dense_level/pallas_call | solution.py:266
  119.3 0.7 copy-done.4
  120.0 0.7 copy-done.6
  120.7 3.3 %collective-permute-start.4 = (bf16[1024,1024]{1,0:T(8,128)(2,1)}, bf16[1024,1024]{1,0:T(8,128)(2,1)}, u32[]{:S(2)}, u32[]{:S(2)}) collective-permute-start(bf16[1024,1024]{1,0:T(8,128)(2,1)} %all-gather.3.cloned.1.call-done.own_ref), channel_id=1, source_target_pairs={{0,64},{64,0},{1,65},{65,1},{2,66},{66,2},{3,67},{67,3},{4,68},{68... | collective-permute-start | bytes 6291464 | tf_op jit(solution)/shard_map/ppermute | solution.py:329
  124.1 0.9 copy-done.7
  125.0 9.0 %dense_level.3 = bf16[1536,128]{1,0:T(8,128)(2,1)S(1)} custom-call(s32[9]{0:T(128)S(1)} %pad_add_fusion.1.scalar_ref, bf16[1536,384]{1,0:T(8,128)(2,1)S(1)} %bitcast.21, bf16[4,8,32,128]{3,2,1,0:T(8,128)(2,1)S(1)} %copy-done.7), custom_call_target="tpu_custom_call" | custom-call | flops 10000000000 | bytes 2000000 | tf_op jit(solution)/shard_map/dense_level/pallas_call | solution.py:266
  134.0 0.8 copy-done.5
  134.8 44.7 %all-gather.5.cloned.1.call-done.own_far_ref = bf16[1024,1024]{1,0:T(8,128)(2,1)} async-done(((bf16[32,1024]{1,0:T(8,128)(2,1)}), bf16[1024,1024]{1,0:T(8,128)(2,1)}) %all-gather.5.cloned.1.call-update) | async-done | bytes 2097168 | tf_op jit(solution)/shard_map/all_gather | solution.py:354
  179.6 6.3 %collective-permute-start.5 = (bf16[1024,1024]{1,0:T(8,128)(2,1)}, bf16[1024,1024]{1,0:T(8,128)(2,1)}, u32[]{:S(2)}, u32[]{:S(2)}) collective-permute-start(bf16[1024,1024]{1,0:T(8,128)(2,1)} %all-gather.5.cloned.1.call-done.own_far_ref), channel_id=1, source_target_pairs={{0,64},{64,0},{1,65},{65,1},{2,66},{66,2},{3,67},{67,3},{4,68},{68... | collective-permute-start | bytes 6291464 | tf_op jit(solution)/shard_map/ppermute | solution.py:329
  185.9 16.9 %all_to_all.25.first_ref = bf16[8,192,128]{2,1,0:T(8,128)(2,1)S(1)} all-to-all(bf16[8,192,128]{2,1,0:T(8,128)(2,1)} %bitcast.22), channel_id=1, replica_groups=mesh['zl'=4,'core'=2,'y'=8,'zh'=2,'x'=4] {'zl','core'}, dimensions={0} | all-to-all | bytes 786432 | tf_op jit(solution)/shard_map/all_to_all | solution.py:363
  202.8 4.2 %all-to-all-start.4 = ((bf16[8,192,128]{2,1,0:T(8,128)(2,1)}), bf16[8,192,128]{2,1,0:T(8,128)(2,1)S(1)}, u32[]{:S(2)}, u32[]{:S(2)}) async-start(bf16[8,192,128]{2,1,0:T(8,128)(2,1)} %bitcast.23), calls=%async_computation.4 | async-start | bytes 786432 | tf_op jit(solution)/shard_map/all_to_all | solution.py:365
  207.1 11.6 %all-to-all-done.4.second_ref = bf16[8,192,128]{2,1,0:T(8,128)(2,1)S(1)} async-done(((bf16[8,192,128]{2,1,0:T(8,128)(2,1)}), bf16[8,192,128]{2,1,0:T(8,128)(2,1)S(1)}, u32[]{:S(2)}, u32[]{:S(2)}) %all-to-all-start.4) | async-done | bytes 393248 | tf_op jit(solution)/shard_map/all_to_all | solution.py:365
  218.8 1.6 copy-done.2
  220.3 6.4 %project.1 = bf16[192,2048]{1,0:T(8,128)(2,1)} custom-call(s32[2]{0:T(128)S(1)} %pad_add_fusion.place_ref, bf16[8,192,128]{2,1,0:T(8,128)(2,1)S(1)} %all_to_all.25.first_ref, bf16[8,192,128]{2,1,0:T(8,128)(2,1)S(1)} %all-to-all-done.4.second_ref, bf16[1024,1024]{1,0:T(8,128)(2,1)S(1)} %copy-done.1, bf16[1024,1024]{1,0:T(8,128)(2,1)S(1)} %copy-done.2, ...), custom_call_target="tpu_custom_call" | custom-call | flops 1610612736 | bytes 10000000 | tf_op jit(solution)/shard_map/project/pallas_call | solution.py:312
  (35 shorter events, 1.5 us)
Async XLA Ops:
  6.5 0.9 copy-start
  6.5 114.2 %all-gather.3.cloned.1.call-start = ((), (), s32[]{:S(2)}) async-start(), calls=%async_computation.5 | async-start | bytes 2162688 | tf_op jit(solution)/shard_map/all_gather | solution.py:347
  13.0 21.1 %copy-start.8 = (bf16[32,1024]{1,0:T(8,128)(2,1)S(1)}, bf16[32,1024]{1,0:T(8,128)(2,1)}, u32[]{:S(2)}) copy-start(bf16[32,1024]{1,0:T(8,128)(2,1)} %constant_dynamic-slice_fusion) | copy-start | bytes 196612
  13.0 38.9 %all-to-all-start = ((bf16[64,48,128]{2,1,0:T(8,128)(2,1)}), bf16[64,48,128]{2,1,0:T(8,128)(2,1)S(1)}, u32[]{:S(2)}, u32[]{:S(2)}) async-start(bf16[64,48,128]{2,1,0:T(8,128)(2,1)} %bitcast.24), calls=%async_computation | async-start | bytes 1572864 | tf_op jit(solution)/shard_map/all_to_all | solution.py:350
  34.1 17.9 %collective-permute-start = (bf16[32,1024]{1,0:T(8,128)(2,1)S(1)}, bf16[32,1024]{1,0:T(8,128)(2,1)S(1)}, u32[]{:S(2)}, u32[]{:S(2)}) collective-permute-start(bf16[32,1024]{1,0:T(8,128)(2,1)S(1)} %copy-done.8), channel_id=1, source_target_pairs={{0,4},{4,0},{1,5},{5,1},{2,6},{6,2},{3,7},{7,3},{8,12},{12,8},{9,1... | collective-permute-start | bytes 196616 | tf_op jit(solution)/shard_map/ppermute | solution.py:329
  52.0 6.0 %copy-start.9 = (bf16[32,1024]{1,0:T(8,128)(2,1)}, bf16[32,1024]{1,0:T(8,128)(2,1)S(1)}, u32[]{:S(2)}) copy-start(bf16[32,1024]{1,0:T(8,128)(2,1)S(1)} %collective-permute-done) | copy-start | bytes 196612
  52.0 34.5 %all-to-all-start.1 = ((bf16[8,192,384]{2,1,0:T(8,128)(2,1)}), bf16[8,192,384]{2,1,0:T(8,128)(2,1)S(1)}, u32[]{:S(2)}, u32[]{:S(2)}) async-start(bf16[8,192,384]{2,1,0:T(8,128)(2,1)} %get-tuple-element.18), calls=%async_computation.1 | async-start | bytes 2359296 | tf_op jit(solution)/shard_map/all_to_all | solution.py:356
  57.9 35.3 %copy-start.10 = (s32[32]{0:T(128)S(1)}, s32[32]{0:T(128)}, u32[]{:S(2)}) copy-start(s32[32]{0:T(128)} %two_ref.1) | copy-start | bytes 388
  57.9 35.4 %copy-start.11 = (s32[32]{0:T(128)S(1)}, s32[32]{0:T(128)}, u32[]{:S(2)}) copy-start(s32[32]{0:T(128)} %three_ref.1) | copy-start | bytes 388
  57.9 121.7 %all-gather.5.cloned.1.call-start = ((), (), s32[]{:S(2)}) async-start(), calls=%async_computation.6 | async-start | bytes 2162688 | tf_op jit(solution)/shard_map/all_gather | solution.py:354
  86.5 37.6 %all-to-all-start.2 = ((bf16[8,192,384]{2,1,0:T(8,128)(2,1)}), bf16[8,192,384]{2,1,0:T(8,128)(2,1)S(1)}, u32[]{:S(2)}, u32[]{:S(2)}) async-start(bf16[8,192,384]{2,1,0:T(8,128)(2,1)} %get-tuple-element.20), calls=%async_computation.2 | async-start | bytes 2359296 | tf_op jit(solution)/shard_map/all_to_all | solution.py:358
  93.4 1.0 copy-start.3
  98.4 7.9 %collective-permute-start.3 = (bf16[8,32,128]{2,1,0:T(8,128)(2,1)S(1)}, bf16[8,32,128]{2,1,0:T(8,128)(2,1)S(1)}, u32[]{:S(2)}, u32[]{:S(2)}) collective-permute-start(bf16[8,32,128]{2,1,0:T(8,128)(2,1)S(1)} %get-tuple-element.26), channel_id=1, source_target_pairs={{0,3},{1,0},{2,1},{3,2},{4,7},{5,4},{6,5},{7,6},{8,11},{9,8},{10,9... | collective-permute-start | bytes 196616 | tf_op jit(solution)/shard_map/ppermute | solution.py:329
  101.5 6.7 %collective-permute-start.2 = (bf16[8,32,128]{2,1,0:T(8,128)(2,1)S(1)}, bf16[8,32,128]{2,1,0:T(8,128)(2,1)S(1)}, u32[]{:S(2)}, u32[]{:S(2)}) collective-permute-start(bf16[8,32,128]{2,1,0:T(8,128)(2,1)S(1)} %get-tuple-element.27), channel_id=1, source_target_pairs={{0,2},{1,3},{2,0},{3,1},{4,6},{5,7},{6,4},{7,5},{8,10},{9,11},{10,... | collective-permute-start | bytes 196616 | tf_op jit(solution)/shard_map/ppermute | solution.py:329
  103.7 6.5 %collective-permute-start.1 = (bf16[8,32,128]{2,1,0:T(8,128)(2,1)S(1)}, bf16[8,32,128]{2,1,0:T(8,128)(2,1)S(1)}, u32[]{:S(2)}, u32[]{:S(2)}) collective-permute-start(bf16[8,32,128]{2,1,0:T(8,128)(2,1)S(1)} %get-tuple-element.28), channel_id=1, source_target_pairs={{0,1},{1,2},{2,3},{3,0},{4,5},{5,6},{6,7},{7,4},{8,9},{9,10},{10,1... | collective-permute-start | bytes 196616 | tf_op jit(solution)/shard_map/ppermute | solution.py:329
  119.3 0.7 copy-start.4
  120.0 0.7 copy-start.6
  120.7 86.4 %collective-permute-start.4 = (bf16[1024,1024]{1,0:T(8,128)(2,1)}, bf16[1024,1024]{1,0:T(8,128)(2,1)}, u32[]{:S(2)}, u32[]{:S(2)}) collective-permute-start(bf16[1024,1024]{1,0:T(8,128)(2,1)} %all-gather.3.cloned.1.call-done.own_ref), channel_id=1, source_target_pairs={{0,64},{64,0},{1,65},{65,1},{2,66},{66,2},{3,67},{67,3},{4,68},{68... | collective-permute-start | bytes 6291464 | tf_op jit(solution)/shard_map/ppermute | solution.py:329
  124.1 1.0 copy-start.7
  125.0 93.7 %copy-start.1 = (bf16[1024,1024]{1,0:T(8,128)(2,1)S(1)}, bf16[1024,1024]{1,0:T(8,128)(2,1)}, u32[]{:S(2)}) copy-start(bf16[1024,1024]{1,0:T(8,128)(2,1)} %all-gather.3.cloned.1.call-done.own_ref) | copy-start | bytes 6291460
  134.0 0.8 copy-start.5
  179.6 39.2 %collective-permute-start.5 = (bf16[1024,1024]{1,0:T(8,128)(2,1)}, bf16[1024,1024]{1,0:T(8,128)(2,1)}, u32[]{:S(2)}, u32[]{:S(2)}) collective-permute-start(bf16[1024,1024]{1,0:T(8,128)(2,1)} %all-gather.5.cloned.1.call-done.own_far_ref), channel_id=1, source_target_pairs={{0,64},{64,0},{1,65},{65,1},{2,66},{66,2},{3,67},{67,3},{4,68},{68... | collective-permute-start | bytes 6291464 | tf_op jit(solution)/shard_map/ppermute | solution.py:329
  202.8 15.9 %all-to-all-start.4 = ((bf16[8,192,128]{2,1,0:T(8,128)(2,1)}), bf16[8,192,128]{2,1,0:T(8,128)(2,1)S(1)}, u32[]{:S(2)}, u32[]{:S(2)}) async-start(bf16[8,192,128]{2,1,0:T(8,128)(2,1)} %bitcast.23), calls=%async_computation.4 | async-start | bytes 786432 | tf_op jit(solution)/shard_map/all_to_all | solution.py:365
  218.7 1.6 copy-start.2
Sparse Core Ops, SparseCore 0:
  10.5 85.3 all-gather.2
  99.1 80.4 all-gather.4

commit v5 on v4

--- a/solution.py
+++ b/solution.py
@@ -26,11 +26,12 @@
 LOCAL3 = ROWS // R3
 PICK = 32
 SENT = PICK + PICK // 2
-BLOCK = 256
+BLOCK = 512
 PART = 256
+BULK = PAIR + 2 * WIDTH
 PER_STEP = 2
 SCALE2 = HD**-0.5 * math.log2(math.e)
-VMEM_LIMIT = 40 * 2**20
+VMEM_LIMIT = 28 * 2**20
 GROUP = ("zl", "core")
 NT = (((1,), (1,)), ((), ()))
 BF16 = jnp.bfloat16
@@ -105,22 +106,21 @@
     )(offsets_two, offsets_three, queries, keys, values)
 
 
-def pack_kernel(q_ref, k_ref, v_ref, first_ref, second_ref):
-    for pair, out_ref in enumerate((first_ref, second_ref)):
-        for which, ref in enumerate((q_ref, k_ref, v_ref)):
-            out_ref[0, :, which * PAIR : (which + 1) * PAIR] = ref[:, pair * PAIR : (pair + 1) * PAIR]
+def pack_kernel(q_ref, k_ref, v_ref, bulk_ref, rest_ref):
+    bulk_ref[0, :, :PAIR] = q_ref[:, :PAIR]
+    bulk_ref[0, :, PAIR : PAIR + WIDTH] = k_ref[...]
+    bulk_ref[0, :, PAIR + WIDTH :] = v_ref[...]
+    rest_ref[0] = q_ref[:, PAIR:]
 
 
 def pack(queries, keys, values):
     block = pl.BlockSpec((ROWS, WIDTH), lambda j: (0, j))
-    chunk = pl.BlockSpec((1, ROWS, 3 * PAIR), lambda j: (j, 0, 0))
-    shape = jax.ShapeDtypeStruct((GRP, ROWS, 3 * PAIR), BF16)
     return pl.pallas_call(
         pack_kernel,
         grid=(GRP,),
         in_specs=[block] * 3,
-        out_specs=[chunk] * 2,
-        out_shape=[shape] * 2,
+        out_specs=[pl.BlockSpec((1, ROWS, columns), lambda j: (j, 0, 0)) for columns in (BULK, PAIR)],
+        out_shape=[jax.ShapeDtypeStruct((GRP, ROWS, columns), BF16) for columns in (BULK, PAIR)],
         compiler_params=pltpu.CompilerParams(vmem_limit_bytes=56 * 2**20),
         cost_estimate=cost(0, 5 * 10**6),
         name="pack",
@@ -198,7 +198,7 @@
     )(place, got, far)
 
 
-def dense_kernel(pair, scalar_ref, qkv_ref, back_ref, out_ref, acc, top, aug, scores, few):
+def dense_kernel(pair, scalar_ref, q_ref, bulk_ref, back_ref, done_ref, out_ref, acc, top, aug, scores, few):
     zero, one = jnp.zeros((), BF16), jnp.ones((), BF16)
     blocks, parts = SEG1 // BLOCK, SEG1 // PART
 
@@ -209,18 +209,19 @@
     def rows_of(block):
         return pl.ds(pl.multiple_of(block * BLOCK, BLOCK), BLOCK)
 
-    columns, keys, values = (slice(i * PAIR, (i + 1) * PAIR) for i in range(3))
+    keys = slice(PAIR + pair * PAIR, PAIR + (pair + 1) * PAIR)
+    values = slice(keys.start + WIDTH, keys.stop + WIDTH)
     for parity in range(2):
-        aug[parity] = jnp.where(mine(parity, SEG1), qkv_ref[:, values], one)
+        aug[parity] = jnp.where(mine(parity, SEG1), bulk_ref[:, values], one)
 
     def step(ahead, parity, largest, block):
         q, expected, total = None, None, None
         if ahead is not None:
-            q = jnp.where(mine(ahead[0], BLOCK), qkv_ref[rows_of(ahead[1]), columns], zero)
+            q = jnp.where(mine(ahead[0], BLOCK), q_ref[rows_of(ahead[1]), :PAIR], zero)
         for part in range(parts):
             lanes = slice(part * PART, (part + 1) * PART)
             if ahead is not None:
-                fresh = lax.dot_general(q, qkv_ref[lanes, keys], NT, preferred_element_type=F32)
+                fresh = lax.dot_general(q, bulk_ref[lanes, keys], NT, preferred_element_type=F32)
                 scores[ahead[0], :, lanes] = fresh
                 for i in range(0, PART, PAIR):
                     piece = fresh[:, i : i + PAIR]
@@ -259,14 +260,19 @@
             few[g * LOCAL3 : (g + 1) * LOCAL3, :] = back[g, LOCAL2 : LOCAL2 + LOCAL3]
         merge(pl.ds(scalar_ref[1 + OWN + head], SEG1 // R3, stride=R3), few[...])
     result = [acc[parity] / pltpu.roll(acc[parity], HD, 1) for parity in range(2)]
-    out_ref[...] = jnp.where(mine(0, SEG1), result[0], result[1]).astype(BF16)
-
-
-def dense_level(pair, scalars, qkv, back):
+    result = jnp.where(mine(0, SEG1), result[0], result[1]).astype(BF16)
+    if pair:
+        out_ref[:, :PAIR] = done_ref[...]
+        out_ref[:, PAIR:] = result
+    else:
+        out_ref[...] = result
+
+
+def dense_level(pair, scalars, q, bulk, back, done):
     return pl.pallas_call(
         functools.partial(dense_kernel, pair),
-        in_specs=[pl.BlockSpec(memory_space=pltpu.SMEM)] + [pl.BlockSpec(memory_space=pltpu.VMEM)] * 2,
-        out_shape=jax.ShapeDtypeStruct((SEG1, PAIR), BF16),
+        in_specs=[pl.BlockSpec(memory_space=pltpu.SMEM)] + [pl.BlockSpec(memory_space=pltpu.VMEM)] * 4,
+        out_shape=jax.ShapeDtypeStruct((SEG1, PAIR * (pair + 1)), BF16),
         scratch_shapes=[
             pltpu.VMEM((2, SEG1, PAIR), F32),
             pltpu.VMEM((2, SEG1, PAIR), F32),
@@ -277,51 +283,49 @@
         compiler_params=params(),
         cost_estimate=cost(10 * 10**9, 2 * 10**6, 5 * 10**6),
         name="dense_level",
-    )(scalars, qkv, back)
-
-
-def project_kernel(place_ref, first_ref, second_ref, own_ref, own_far_ref, other_ref, other_far_ref, out_ref):
+    )(scalars, q, bulk, back, done)
+
+
+def project_kernel(place_ref, att_ref, own_ref, other_ref, out_ref):
     upper = place_ref[1] == 1
-    part = WIDTH // ZH
-
-    def write(near_ref, far_ref):
+    part = WIDTH // (XS * ZH)
+
+    def write(w_ref):
         total = None
         for g in range(GRP):
-            rows = slice(g * part, (g + 1) * part)
-            near = jnp.where(upper, second_ref[g], first_ref[g])
-            far = jnp.where(upper, first_ref[g], second_ref[g])
-            term = jnp.dot(
-                jnp.concatenate([near, far], 1),
-                jnp.concatenate([near_ref[rows, :], far_ref[rows, :]], 0),
-                preferred_element_type=F32,
-            )
+            starts = [g * WIDTH + (x * ZH + far) * part for far in range(ZH) for x in range(XS)]
+            weights = jnp.concatenate([w_ref[start : start + part, :] for start in starts], 0)
+            low, high = att_ref[g, :, :PAIR], att_ref[g, :, PAIR:]
+            att = jnp.concatenate([jnp.where(upper, high, low), jnp.where(upper, low, high)], 1)
+            term = jnp.dot(att, weights, preferred_element_type=F32)
             total = term if total is None else total + term
         out_ref[...] = total.astype(BF16)
 
     is_own = pl.program_id(0) < pl.num_programs(0) // 2
-    pl.when(is_own)(lambda: write(own_ref, own_far_ref))
-    pl.when(jnp.logical_not(is_own))(lambda: write(other_ref, other_far_ref))
-
-
-def project(place, first, second, own, own_far, other, other_far):
-    columns = 512
+    pl.when(is_own)(lambda: write(own_ref))
+    pl.when(jnp.logical_not(is_own))(lambda: write(other_ref))
+
+
+def project(place, att, own, other):
+    columns = 256
     half = D // 2 // columns
-    att = pl.BlockSpec((GRP, ROWS, PAIR), lambda j, place: (0, 0, 0))
-    early = pl.BlockSpec((D // ZH, columns), lambda j, place: (0, jnp.minimum(j, half - 1)))
-    late = pl.BlockSpec((D // ZH, columns), lambda j, place: (0, jnp.maximum(j - half, 0)))
     return pl.pallas_call(
         project_kernel,
         grid_spec=pltpu.PrefetchScalarGridSpec(
             num_scalar_prefetch=1,
             grid=(2 * half,),
-            in_specs=[att, att, early, early, late, late],
+            in_specs=[
+                pl.BlockSpec((GRP, ROWS, WIDTH), lambda j, place: (0, 0, 0)),
+                pl.BlockSpec((D, columns), lambda j, place: (0, jnp.minimum(j, half - 1))),
+                pl.BlockSpec((D, columns), lambda j, place: (0, jnp.maximum(j - half, 0))),
+            ],
             out_specs=pl.BlockSpec((ROWS, columns), lambda j, place: (0, (j + place[0] * half) % (2 * half))),
         ),
         out_shape=jax.ShapeDtypeStruct((ROWS, D), BF16),
         compiler_params=pltpu.CompilerParams(vmem_limit_bytes=24 * 2**20),
         cost_estimate=cost(2 * ROWS * D * D, 10 * 10**6),
         name="project",
-    )(place, first, second, own, own_far, other, other_far)
+    )(place, att, own, other)
 
 
 def shift(value, axis, step):
@@ -344,28 +348,26 @@
     core, zh = lax.axis_index("core"), lax.axis_index("zh")
 
     w_rows = lax.dynamic_slice_in_dim(w_out, core * half, half, axis=1)
+    far_rows = shift(w_rows, "zh", 1)
+    small = pick(offsets_two, offsets_three, queries, keys, values)
+    bulk, rest = pack(after(queries, small), keys, values)
+    w_rows = jnp.concatenate([after(w_rows, small), far_rows], 0)
     w_own = lax.all_gather(w_rows, ("y", "x"), axis=0, tiled=True)
-    small = pick(offsets_two, offsets_three, queries, keys, values)
-    chunk_a, chunk_b = pack(after(queries, small), keys, values)
     got = lax.all_to_all(
-        small.reshape(H * ZH, SENT, PAIR), ("zl", "core", "x", "zh"), split_axis=0, concat_axis=0, tiled=True
+        after(small, far_rows).reshape(H * ZH, SENT, PAIR), ("zl", "core", "x", "zh"), split_axis=0, concat_axis=0, tiled=True
     ).reshape(H, ZH, SENT, PAIR)
-    far_rows = shift(after(w_rows, chunk_a), "zh", 1)
-    w_own_far = lax.all_gather(far_rows, ("y", "x"), axis=0, tiled=True)
-
-    qkv_a = exchange(after(chunk_a, got, far_rows)).reshape(SEG1, 3 * PAIR)
+
+    bulk = exchange(after(bulk, got)).reshape(SEG1, BULK)
     far = lax.all_gather(compact(got), "y", axis=0, tiled=True)
-    qkv_b = exchange(after(chunk_b, qkv_a, far)).reshape(SEG1, 3 * PAIR)
     parts = sparse_levels(jnp.stack([x, zh]), got, far)
     back = jnp.stack([parts[0]] + [shift(parts[step], "x", step) for step in range(1, XS)])
+    rest = exchange(after(rest, bulk, back)).reshape(SEG1, PAIR)
     scalars = jnp.concatenate([x.reshape(1), own_two, own_three])
-    att_a = dense_level(0, scalars, qkv_a, back)
-    out_a = exchange(after(att_a, qkv_b).reshape(GRP, ROWS, PAIR))
-    att_b = dense_level(1, scalars, after(qkv_b, att_a), back)
-    out_b = exchange(att_b.reshape(GRP, ROWS, PAIR))
-    w_other = shift(after(w_own, att_a), "core", 1)
-    w_other_far = shift(after(w_own_far, att_b), "core", 1)
-    return project(jnp.stack([core, zh]), out_a, out_b, w_own, w_own_far, w_other, w_other_far)
+    att = dense_level(0, scalars, bulk, bulk, back, back)
+    att = dense_level(1, scalars, rest, bulk, back, att)
+    w_other = shift(after(w_own, att), "core", 1)
+    att = exchange(att.reshape(GRP, ROWS, WIDTH))
+    return project(jnp.stack([core, zh]), att, w_own, w_other)
 
 
 def solution(mesh):

time: 235 us -> 178 us (0.76)
  waiting for transfers between devices: 75.7 us -> 52.6 us
  blocking collectives: 40.3 us -> 21.6 us
  starting transfers between devices: 56.6 us -> 44.6 us
  local copies, waits for them, and re-layouts: 7.45 us -> 3.27 us
    all_gather x1 -> x0, waiting for transfers between devices: 44.7 us -> none  [local(): w_own_far = lax.all_gather(far_rows, ('y', 'x'), axis=0, tiled=True)]
    all_to_all x4, waiting for transfers between devices: 15.7 us -> 47.3 us  [the longest x1 20 us: local(): att = exchange(att.reshape(GRP, ROWS, WIDTH))]
    all_to_all x1 -> x0, blocking collectives: 16.9 us -> none  [local(): out_a = exchange(after(att_a, qkv_b).reshape(GRP, ROWS, PAIR))]
    ppermute x6 -> x5, waiting for transfers between devices: 14.6 us -> 5.37 us  [shift(): lax.ppermute(value, axis, [(i, (i + step) % size) for i in range(size)])]
    all_to_all x4, starting transfers between devices: 31.9 us -> 23.2 us  [the longest x1 9.72 us: local(): lax.all_to_all(after(small, far_rows).reshape(H * ZH, SENT, PAIR), ('zl',...]
    unnamed x24 -> x8, local copies, waits for them, and re-layouts: 6.67 us -> 3.1 us
    ppermute x6 -> x5, starting transfers between devices: 24.7 us -> 21.4 us  [shift(): lax.ppermute(value, axis, [(i, (i + step) % size) for i in range(size)])]
  transfers between devices with their start and end apart: 12 -> 10, of which waited for: 6 -> 6; matrix products, arithmetic and copies ran while one was open for 0% -> 0% of each run, Pallas kernels for 14% -> 18%
where the time goes in v5:
time: 178 us; the launch traced here: 177 us
  waiting for transfers between devices  52.6 us (30%)
  starting transfers between devices  44.6 us (25%)
  Pallas kernels  40.2 us (23%)
  blocking collectives  21.6 us (12%)
  between operations  13.5 us (8%)
  local copies, waits for them, and re-layouts  3.27 us (2%)
    all_gather x1, blocking collectives, local(): far = lax.all_gather(compact(got), 'y', axis=0, tiled=True)  21.6 us
    ppermute x5, starting transfers between devices, shift(): lax.ppermute(value, axis, [(i, (i + step) % size) for i in range(size)])  21.4 us
    all_to_all x1, waiting for transfers between devices, local(): att = exchange(att.reshape(GRP, ROWS, WIDTH))  20 us
    all_to_all x1, waiting for transfers between devices, local(): lax.all_to_all(after(small, far_rows).reshape(H * ZH, SENT, PAIR), ('zl',...  16.9 us
    pallas_call x2, Pallas kernels, dense_level(): pl.pallas_call(functools.partial(dense_kernel, pair), in_specs=[pl.BlockS...  16.9 us
    all_to_all x1, starting transfers between devices, local(): lax.all_to_all(after(small, far_rows).reshape(H * ZH, SENT, PAIR), ('zl',...  9.72 us
    pallas_call x1, Pallas kernels, project(): pl.pallas_call(project_kernel, grid_spec=pltpu.PrefetchScalarGridSpec(num...  8.05 us
    all_to_all x1, waiting for transfers between devices, local(): bulk = exchange(after(bulk, got)).reshape(SEG1, BULK)  6.61 us
  transfers between devices with their start and end apart: 10, of which 6 were waited for; matrix products, arithmetic and copies ran while one was open for 0% of the time, Pallas kernels for 18%

profile of v5, /device:TPU:1, one launch (start us, length us, event | category | flops | bytes accessed | tf_op | source)
XLA Modules:
  0.0 176.7 jit_solution(6014803144548091854)
XLA Ops:
  6.5 0.9 copy-done
  7.4 11.5 %collective-permute-start = (bf16[32,1024]{1,0:T(8,128)(2,1)S(1)}, bf16[32,1024]{1,0:T(8,128)(2,1)S(1)}, u32[]{:S(2)}, u32[]{:S(2)}) collective-permute-start(bf16[32,1024]{1,0:T(8,128)(2,1)S(1)} %constant_dynamic-slice_fusion), channel_id=1, source_target_pairs={{0,4},{4,0},{1,5},{5,1},{2,6},{6,2},{3,7},{7,3},{8,12},{12,8},{9,1... | collective-permute-start | bytes 196616 | tf_op jit(solution)/shard_map/ppermute | solution.py:333
  18.9 4.9 %pick.1 = bf16[32,2,48,128]{3,2,1,0:T(8,128)(2,1)} custom-call(s32[32]{0:T(128)} %two_ref.1, s32[32]{0:T(128)} %three_ref.1, bf16[192,2048]{1,0:T(8,128)(2,1)} %q_ref.2, bf16[192,2048]{1,0:T(8,128)(2,1)} %k_ref.3, bf16[192,2048]{1,0:T(8,128)(2,1)} %v_ref.3), custom_call_target="tpu_custom_call" | custom-call | flops 1000000000 | bytes 4000000 | tf_op jit(solution)/shard_map/pick/pallas_call | solution.py:94
  23.9 0.7 pad_maximum_fusion.1
  24.5 0.0 all-gather.2.cloned.1.call-update
  24.6 9.7 %all-to-all-start = ((bf16[64,48,128]{2,1,0:T(8,128)(2,1)}), bf16[64,48,128]{2,1,0:T(8,128)(2,1)S(1)}, u32[]{:S(2)}, u32[]{:S(2)}) async-start(bf16[64,48,128]{2,1,0:T(8,128)(2,1)} %bitcast.23), calls=%async_computation | async-start | bytes 1572864 | tf_op jit(solution)/shard_map/all_to_all | solution.py:356
  34.3 6.0 %pack.1 = (bf16[8,192,640]{2,1,0:T(8,128)(2,1)}, bf16[8,192,128]{2,1,0:T(8,128)(2,1)}) custom-call(bf16[192,2048]{1,0:T(8,128)(2,1)} %q_ref.2, bf16[192,2048]{1,0:T(8,128)(2,1)} %k_ref.3, bf16[192,2048]{1,0:T(8,128)(2,1)} %v_ref.3), custom_call_target="tpu_custom_call" | custom-call | bytes 5000000 | tf_op jit(solution)/shard_map/pack/pallas_call | solution.py:118
  40.3 16.9 %all-to-all-done = bf16[64,48,128]{2,1,0:T(8,128)(2,1)S(1)} async-done(((bf16[64,48,128]{2,1,0:T(8,128)(2,1)}), bf16[64,48,128]{2,1,0:T(8,128)(2,1)S(1)}, u32[]{:S(2)}, u32[]{:S(2)}) %all-to-all-start) | async-done | bytes 786464 | tf_op jit(solution)/shard_map/all_to_all | solution.py:356
  57.2 5.8 %all-to-all-start.1 = ((bf16[8,192,640]{2,1,0:T(8,128)(2,1)}), bf16[8,192,640]{2,1,0:T(8,128)(2,1)S(1)}, u32[]{:S(2)}, u32[]{:S(2)}) async-start(bf16[8,192,640]{2,1,0:T(8,128)(2,1)} %get-tuple-element.17), calls=%async_computation.1 | async-start | bytes 3932160 | tf_op jit(solution)/shard_map/all_to_all | solution.py:360
  63.0 0.1 dynamic_slice.9
  63.1 0.1 dynamic_slice.10
  63.1 0.1 pad_add_fusion.2.place_ref
  63.2 0.4 compact_three.1
  63.6 21.6 %all_gather.6.far_ref = bf16[1536,128]{1,0:T(8,128)(2,1)S(1)} all-gather(bf16[192,128]{1,0:T(8,128)(2,1)S(1)} %compact_three.1), channel_id=1, replica_groups=mesh['zl'=4,'core'=2,'y'=8,'zh'=2,'x'=4] {'y'}, dimensions={0}, use_global_device_ids=true | all-gather | bytes 442368 | tf_op jit(solution)/shard_map/all_gather | solution.py:361
  85.2 4.0 %sparse_levels.1 = bf16[4,8,32,128]{3,2,1,0:T(8,128)(2,1)S(1)} custom-call(s32[2]{0:T(128)S(1)} %pad_add_fusion.2.place_ref, bf16[32,2,48,128]{3,2,1,0:T(8,128)(2,1)S(1)} %bitcast.18, bf16[1536,128]{1,0:T(8,128)(2,1)S(1)} %all_gather.6.far_ref), custom_call_target="tpu_custom_call" | custom-call | flops 4000000000 | bytes 2000000 | tf_op jit(solution)/shard_map/sparse_levels/pallas_call | solution.py:191
  89.2 1.9 %collective-permute-start.3 = (bf16[8,32,128]{2,1,0:T(8,128)(2,1)S(1)}, bf16[8,32,128]{2,1,0:T(8,128)(2,1)S(1)}, u32[]{:S(2)}, u32[]{:S(2)}) collective-permute-start(bf16[8,32,128]{2,1,0:T(8,128)(2,1)S(1)} %get-tuple-element.22), channel_id=1, source_target_pairs={{0,3},{1,0},{2,1},{3,2},{4,7},{5,4},{6,5},{7,6},{8,11},{9,8},{10,9... | collective-permute-start | bytes 196616 | tf_op jit(solution)/shard_map/ppermute | solution.py:333
  91.1 2.3 %collective-permute-start.2 = (bf16[8,32,128]{2,1,0:T(8,128)(2,1)S(1)}, bf16[8,32,128]{2,1,0:T(8,128)(2,1)S(1)}, u32[]{:S(2)}, u32[]{:S(2)}) collective-permute-start(bf16[8,32,128]{2,1,0:T(8,128)(2,1)S(1)} %get-tuple-element.23), channel_id=1, source_target_pairs={{0,2},{1,3},{2,0},{3,1},{4,6},{5,7},{6,4},{7,5},{8,10},{9,11},{10,... | collective-permute-start | bytes 196616 | tf_op jit(solution)/shard_map/ppermute | solution.py:333
  93.5 3.0 %collective-permute-start.1 = (bf16[8,32,128]{2,1,0:T(8,128)(2,1)S(1)}, bf16[8,32,128]{2,1,0:T(8,128)(2,1)S(1)}, u32[]{:S(2)}, u32[]{:S(2)}) collective-permute-start(bf16[8,32,128]{2,1,0:T(8,128)(2,1)S(1)} %get-tuple-element.24), channel_id=1, source_target_pairs={{0,1},{1,2},{2,3},{3,0},{4,5},{5,6},{6,7},{7,4},{8,9},{9,10},{10,1... | collective-permute-start | bytes 196616 | tf_op jit(solution)/shard_map/ppermute | solution.py:333
  96.4 0.1 pad_add_fusion.1.scalar_ref
  96.5 2.0 %collective-permute-done.2 = bf16[8,32,128]{2,1,0:T(8,128)(2,1)S(1)} collective-permute-done((bf16[8,32,128]{2,1,0:T(8,128)(2,1)S(1)}, bf16[8,32,128]{2,1,0:T(8,128)(2,1)S(1)}, u32[]{:S(2)}, u32[]{:S(2)}) %collective-permute-start.2) | collective-permute-done | bytes 65568 | tf_op jit(solution)/shard_map/ppermute | solution.py:333
  98.5 3.3 %collective-permute-done.1 = bf16[8,32,128]{2,1,0:T(8,128)(2,1)S(1)} collective-permute-done((bf16[8,32,128]{2,1,0:T(8,128)(2,1)S(1)}, bf16[8,32,128]{2,1,0:T(8,128)(2,1)S(1)}, u32[]{:S(2)}, u32[]{:S(2)}) %collective-permute-start.1) | collective-permute-done | bytes 65568 | tf_op jit(solution)/shard_map/ppermute | solution.py:333
  101.9 6.6 %all-to-all-done.1 = bf16[8,192,640]{2,1,0:T(8,128)(2,1)S(1)} async-done(((bf16[8,192,640]{2,1,0:T(8,128)(2,1)}), bf16[8,192,640]{2,1,0:T(8,128)(2,1)S(1)}, u32[]{:S(2)}, u32[]{:S(2)}) %all-to-all-start.1) | async-done | bytes 1966112 | tf_op jit(solution)/shard_map/all_to_all | solution.py:360
  108.5 4.1 %all-to-all-start.2 = ((bf16[8,192,128]{2,1,0:T(8,128)(2,1)}), bf16[8,192,128]{2,1,0:T(8,128)(2,1)S(1)}, u32[]{:S(2)}, u32[]{:S(2)}) async-start(bf16[8,192,128]{2,1,0:T(8,128)(2,1)} %get-tuple-element.18), calls=%async_computation.2 | async-start | bytes 786432 | tf_op jit(solution)/shard_map/all_to_all | solution.py:364
  112.6 8.0 %dense_level.2.done_ref = bf16[1536,128]{1,0:T(8,128)(2,1)S(1)} custom-call(s32[9]{0:T(128)S(1)} %pad_add_fusion.1.scalar_ref, bf16[1536,640]{1,0:T(8,128)(2,1)S(1)} %bitcast.19, bf16[1536,640]{1,0:T(8,128)(2,1)S(1)} %bitcast.20, bf16[4,8,32,128]{3,2,1,0:T(8,128)(2,1)S(1)} %pad_maximum_fusion.back_ref.done_ref, ...), custom_call_target="tpu_custom_call" | custom-call | flops 10000000000 | bytes 2000000 | tf_op jit(solution)/shard_map/dense_level/pallas_call | solution.py:272
  120.6 3.7 %all-to-all-done.2 = bf16[8,192,128]{2,1,0:T(8,128)(2,1)S(1)} async-done(((bf16[8,192,128]{2,1,0:T(8,128)(2,1)}), bf16[8,192,128]{2,1,0:T(8,128)(2,1)S(1)}, u32[]{:S(2)}, u32[]{:S(2)}) %all-to-all-start.2) | async-done | bytes 393248 | tf_op jit(solution)/shard_map/all_to_all | solution.py:364
  124.3 8.9 %dense_level.3 = bf16[1536,256]{1,0:T(8,128)(2,1)} custom-call(s32[9]{0:T(128)S(1)} %pad_add_fusion.1.scalar_ref, bf16[1536,128]{1,0:T(8,128)(2,1)S(1)} %bitcast.22, bf16[1536,640]{1,0:T(8,128)(2,1)S(1)} %bitcast.21, bf16[4,8,32,128]{3,2,1,0:T(8,128)(2,1)S(1)} %pad_maximum_fusion.back_ref.done_ref, bf16[1536,128]{1,0:T(8,128)(2,1)S(1)} %dense_level.2.done_ref), custom_call_target="tpu_custom_call" | custom-call | flops 10000000000 | bytes 2000000 | tf_op jit(solution)/shard_map/dense_level/pallas_call | solution.py:272
  133.3 2.8 %collective-permute-start.4 = (bf16[2048,1024]{1,0:T(8,128)(2,1)}, bf16[2048,1024]{1,0:T(8,128)(2,1)}, u32[]{:S(2)}, u32[]{:S(2)}) collective-permute-start(bf16[2048,1024]{1,0:T(8,128)(2,1)} %all-gather.2.cloned.1.call-done.own_ref), channel_id=1, source_target_pairs={{0,64},{64,0},{1,65},{65,1},{2,66},{66,2},{3,67},{67,3},{4,68},{68... | collective-permute-start | bytes 12582920 | tf_op jit(solution)/shard_map/ppermute | solution.py:333
  136.0 3.5 %all-to-all-start.3 = ((bf16[8,192,256]{2,1,0:T(8,128)(2,1)}), bf16[8,192,256]{2,1,0:T(8,128)(2,1)S(1)}, u32[]{:S(2)}, u32[]{:S(2)}) async-start(bf16[8,192,256]{2,1,0:T(8,128)(2,1)} %bitcast.13), calls=%async_computation.3 | async-start | bytes 1572864 | tf_op jit(solution)/shard_map/all_to_all | solution.py:369
  139.6 0.1 pad_add_fusion.place_ref
  139.6 20.0 %all-to-all-done.3.att_ref = bf16[8,192,256]{2,1,0:T(8,128)(2,1)S(1)} async-done(((bf16[8,192,256]{2,1,0:T(8,128)(2,1)}), bf16[8,192,256]{2,1,0:T(8,128)(2,1)S(1)}, u32[]{:S(2)}, u32[]{:S(2)}) %all-to-all-start.3) | async-done | bytes 786464 | tf_op jit(solution)/shard_map/all_to_all | solution.py:369
  159.6 2.2 %copy-done.1 = bf16[2048,1024]{1,0:T(8,128)(2,1)S(1)} copy-done((bf16[2048,1024]{1,0:T(8,128)(2,1)S(1)}, bf16[2048,1024]{1,0:T(8,128)(2,1)}, u32[]{:S(2)}) %copy-start.1) | copy-done | bytes 4194328
  161.8 8.1 %project.1 = bf16[192,2048]{1,0:T(8,128)(2,1)} custom-call(s32[2]{0:T(128)S(1)} %pad_add_fusion.place_ref, bf16[8,192,256]{2,1,0:T(8,128)(2,1)S(1)} %all-to-all-done.3.att_ref, bf16[2048,1024]{1,0:T(8,128)(2,1)S(1)} %copy-done.1, bf16[2048,1024]{1,0:T(8,128)(2,1)} %collective-permute-done.4.other_ref), custom_call_target="tpu_custom_call" | custom-call | flops 1610612736 | bytes 10000000 | tf_op jit(solution)/shard_map/project/pallas_call | solution.py:312
  (14 shorter events, 0.1 us)
Async XLA Ops:
  6.5 0.9 copy-start
  6.5 126.7 %all-gather.2.cloned.1.call-start = ((), (), s32[]{:S(2)}) async-start(), calls=%async_computation.4 | async-start | bytes 4325376 | tf_op jit(solution)/shard_map/all_gather | solution.py:355
  7.4 16.4 %collective-permute-start = (bf16[32,1024]{1,0:T(8,128)(2,1)S(1)}, bf16[32,1024]{1,0:T(8,128)(2,1)S(1)}, u32[]{:S(2)}, u32[]{:S(2)}) collective-permute-start(bf16[32,1024]{1,0:T(8,128)(2,1)S(1)} %constant_dynamic-slice_fusion), channel_id=1, source_target_pairs={{0,4},{4,0},{1,5},{5,1},{2,6},{6,2},{3,7},{7,3},{8,12},{12,8},{9,1... | collective-permute-start | bytes 196616 | tf_op jit(solution)/shard_map/ppermute | solution.py:333
  23.8 39.2 %copy-start.2 = (s32[32]{0:T(128)S(1)}, s32[32]{0:T(128)}, u32[]{:S(2)}) copy-start(s32[32]{0:T(128)} %two_ref.1) | copy-start | bytes 388
  23.8 39.2 %copy-start.3 = (s32[32]{0:T(128)S(1)}, s32[32]{0:T(128)}, u32[]{:S(2)}) copy-start(s32[32]{0:T(128)} %three_ref.1) | copy-start | bytes 388
  24.6 32.6 %all-to-all-start = ((bf16[64,48,128]{2,1,0:T(8,128)(2,1)}), bf16[64,48,128]{2,1,0:T(8,128)(2,1)S(1)}, u32[]{:S(2)}, u32[]{:S(2)}) async-start(bf16[64,48,128]{2,1,0:T(8,128)(2,1)} %bitcast.23), calls=%async_computation | async-start | bytes 1572864 | tf_op jit(solution)/shard_map/all_to_all | solution.py:356
  57.2 51.3 %all-to-all-start.1 = ((bf16[8,192,640]{2,1,0:T(8,128)(2,1)}), bf16[8,192,640]{2,1,0:T(8,128)(2,1)S(1)}, u32[]{:S(2)}, u32[]{:S(2)}) async-start(bf16[8,192,640]{2,1,0:T(8,128)(2,1)} %get-tuple-element.17), calls=%async_computation.1 | async-start | bytes 3932160 | tf_op jit(solution)/shard_map/all_to_all | solution.py:360
  89.2 7.3 %collective-permute-start.3 = (bf16[8,32,128]{2,1,0:T(8,128)(2,1)S(1)}, bf16[8,32,128]{2,1,0:T(8,128)(2,1)S(1)}, u32[]{:S(2)}, u32[]{:S(2)}) collective-permute-start(bf16[8,32,128]{2,1,0:T(8,128)(2,1)S(1)} %get-tuple-element.22), channel_id=1, source_target_pairs={{0,3},{1,0},{2,1},{3,2},{4,7},{5,4},{6,5},{7,6},{8,11},{9,8},{10,9... | collective-permute-start | bytes 196616 | tf_op jit(solution)/shard_map/ppermute | solution.py:333
  91.1 7.4 %collective-permute-start.2 = (bf16[8,32,128]{2,1,0:T(8,128)(2,1)S(1)}, bf16[8,32,128]{2,1,0:T(8,128)(2,1)S(1)}, u32[]{:S(2)}, u32[]{:S(2)}) collective-permute-start(bf16[8,32,128]{2,1,0:T(8,128)(2,1)S(1)} %get-tuple-element.23), channel_id=1, source_target_pairs={{0,2},{1,3},{2,0},{3,1},{4,6},{5,7},{6,4},{7,5},{8,10},{9,11},{10,... | collective-permute-start | bytes 196616 | tf_op jit(solution)/shard_map/ppermute | solution.py:333
  93.5 8.4 %collective-permute-start.1 = (bf16[8,32,128]{2,1,0:T(8,128)(2,1)S(1)}, bf16[8,32,128]{2,1,0:T(8,128)(2,1)S(1)}, u32[]{:S(2)}, u32[]{:S(2)}) collective-permute-start(bf16[8,32,128]{2,1,0:T(8,128)(2,1)S(1)} %get-tuple-element.24), channel_id=1, source_target_pairs={{0,1},{1,2},{2,3},{3,0},{4,5},{5,6},{6,7},{7,4},{8,9},{9,10},{10,1... | collective-permute-start | bytes 196616 | tf_op jit(solution)/shard_map/ppermute | solution.py:333
  108.5 15.8 %all-to-all-start.2 = ((bf16[8,192,128]{2,1,0:T(8,128)(2,1)}), bf16[8,192,128]{2,1,0:T(8,128)(2,1)S(1)}, u32[]{:S(2)}, u32[]{:S(2)}) async-start(bf16[8,192,128]{2,1,0:T(8,128)(2,1)} %get-tuple-element.18), calls=%async_computation.2 | async-start | bytes 786432 | tf_op jit(solution)/shard_map/all_to_all | solution.py:364
  133.3 26.4 %collective-permute-start.4 = (bf16[2048,1024]{1,0:T(8,128)(2,1)}, bf16[2048,1024]{1,0:T(8,128)(2,1)}, u32[]{:S(2)}, u32[]{:S(2)}) collective-permute-start(bf16[2048,1024]{1,0:T(8,128)(2,1)} %all-gather.2.cloned.1.call-done.own_ref), channel_id=1, source_target_pairs={{0,64},{64,0},{1,65},{65,1},{2,66},{66,2},{3,67},{67,3},{4,68},{68... | collective-permute-start | bytes 12582920 | tf_op jit(solution)/shard_map/ppermute | solution.py:333
  136.0 23.6 %all-to-all-start.3 = ((bf16[8,192,256]{2,1,0:T(8,128)(2,1)}), bf16[8,192,256]{2,1,0:T(8,128)(2,1)S(1)}, u32[]{:S(2)}, u32[]{:S(2)}) async-start(bf16[8,192,256]{2,1,0:T(8,128)(2,1)} %bitcast.13), calls=%async_computation.3 | async-start | bytes 1572864 | tf_op jit(solution)/shard_map/all_to_all | solution.py:369
  159.6 2.2 %copy-start.1 = (bf16[2048,1024]{1,0:T(8,128)(2,1)S(1)}, bf16[2048,1024]{1,0:T(8,128)(2,1)}, u32[]{:S(2)}) copy-start(bf16[2048,1024]{1,0:T(8,128)(2,1)} %all-gather.2.cloned.1.call-done.own_ref) | copy-start | bytes 12582916
Sparse Core Ops, SparseCore 0:
  24.7 84.8 all-gather.1

commit v6 on v5

--- a/solution.py
+++ b/solution.py
@@ -29,7 +29,7 @@
 BLOCK = 512
 PART = 256
 BULK = PAIR + 2 * WIDTH
-PER_STEP = 2
+PER_STEP = 4
 SCALE2 = HD**-0.5 * math.log2(math.e)
 VMEM_LIMIT = 28 * 2**20
 GROUP = ("zl", "core")
@@ -198,7 +198,7 @@
     )(place, got, far)
 
 
-def dense_kernel(pair, scalar_ref, q_ref, bulk_ref, back_ref, done_ref, out_ref, acc, top, aug, scores, few):
+def dense_kernel(pair, scalar_ref, q_ref, bulk_ref, back_ref, out_ref, acc, top, aug, scores, few):
     zero, one = jnp.zeros((), BF16), jnp.ones((), BF16)
     blocks, parts = SEG1 // BLOCK, SEG1 // PART
 
@@ -260,19 +260,14 @@
             few[g * LOCAL3 : (g + 1) * LOCAL3, :] = back[g, LOCAL2 : LOCAL2 + LOCAL3]
         merge(pl.ds(scalar_ref[1 + OWN + head], SEG1 // R3, stride=R3), few[...])
     result = [acc[parity] / pltpu.roll(acc[parity], HD, 1) for parity in range(2)]
-    result = jnp.where(mine(0, SEG1), result[0], result[1]).astype(BF16)
-    if pair:
-        out_ref[:, :PAIR] = done_ref[...]
-        out_ref[:, PAIR:] = result
-    else:
-        out_ref[...] = result
-
-
-def dense_level(pair, scalars, q, bulk, back, done):
+    out_ref[...] = jnp.where(mine(0, SEG1), result[0], result[1]).astype(BF16)
+
+
+def dense_level(pair, scalars, q, bulk, back):
     return pl.pallas_call(
         functools.partial(dense_kernel, pair),
-        in_specs=[pl.BlockSpec(memory_space=pltpu.SMEM)] + [pl.BlockSpec(memory_space=pltpu.VMEM)] * 4,
-        out_shape=jax.ShapeDtypeStruct((SEG1, PAIR * (pair + 1)), BF16),
+        in_specs=[pl.BlockSpec(memory_space=pltpu.SMEM)] + [pl.BlockSpec(memory_space=pltpu.VMEM)] * 3,
+        out_shape=jax.ShapeDtypeStruct((SEG1, PAIR), BF16),
         scratch_shapes=[
             pltpu.VMEM((2, SEG1, PAIR), F32),
             pltpu.VMEM((2, SEG1, PAIR), F32),
@@ -283,49 +278,36 @@
         compiler_params=params(),
         cost_estimate=cost(10 * 10**9, 2 * 10**6, 5 * 10**6),
         name="dense_level",
-    )(scalars, q, bulk, back, done)
-
-
-def project_kernel(place_ref, att_ref, own_ref, other_ref, out_ref):
-    upper = place_ref[1] == 1
+    )(scalars, q, bulk, back)
+
+
+def project_kernel(place_ref, first_ref, second_ref, w_ref, out_ref):
+    upper = place_ref[0] == 1
     part = WIDTH // (XS * ZH)
-
-    def write(w_ref):
+    columns = 512
+    att = []
+    for g in range(GRP):
+        low, high = first_ref[g], second_ref[g]
+        att.append(jnp.concatenate([jnp.where(upper, high, low), jnp.where(upper, low, high)], 1))
+    for start in range(0, D, columns):
         total = None
         for g in range(GRP):
-            starts = [g * WIDTH + (x * ZH + far) * part for far in range(ZH) for x in range(XS)]
-            weights = jnp.concatenate([w_ref[start : start + part, :] for start in starts], 0)
-            low, high = att_ref[g, :, :PAIR], att_ref[g, :, PAIR:]
-            att = jnp.concatenate([jnp.where(upper, high, low), jnp.where(upper, low, high)], 1)
-            term = jnp.dot(att, weights, preferred_element_type=F32)
+            rows = [g * WIDTH + (x * ZH + far) * part for far in range(ZH) for x in range(XS)]
+            weights = jnp.concatenate([w_ref[row : row + part, start : start + columns] for row in rows], 0)
+            term = jnp.dot(att[g], weights, preferred_element_type=F32)
             total = term if total is None else total + term
-        out_ref[...] = total.astype(BF16)
-
-    is_own = pl.program_id(0) < pl.num_programs(0) // 2
-    pl.when(is_own)(lambda: write(own_ref))
-    pl.when(jnp.logical_not(is_own))(lambda: write(other_ref))
-
-
-def project(place, att, own, other):
-    columns = 256
-    half = D // 2 // columns
+        out_ref[:, start : start + columns] = total.astype(BF16)
+
+
+def project(zh, first, second, weights):
     return pl.pallas_call(
         project_kernel,
-        grid_spec=pltpu.PrefetchScalarGridSpec(
-            num_scalar_prefetch=1,
-            grid=(2 * half,),
-            in_specs=[
-                pl.BlockSpec((GRP, ROWS, WIDTH), lambda j, place: (0, 0, 0)),
-                pl.BlockSpec((D, columns), lambda j, place: (0, jnp.minimum(j, half - 1))),
-                pl.BlockSpec((D, columns), lambda j, place: (0, jnp.maximum(j - half, 0))),
-            ],
-            out_specs=pl.BlockSpec((ROWS, columns), lambda j, place: (0, (j + place[0] * half) % (2 * half))),
-        ),
+        in_specs=[pl.BlockSpec(memory_space=pltpu.SMEM)] + [pl.BlockSpec(memory_space=pltpu.VMEM)] * 3,
         out_shape=jax.ShapeDtypeStruct((ROWS, D), BF16),
-        compiler_params=pltpu.CompilerParams(vmem_limit_bytes=24 * 2**20),
+        compiler_params=params(),
         cost_estimate=cost(2 * ROWS * D * D, 10 * 10**6),
         name="project",
-    )(place, att, own, other)
+    )(zh, first, second, weights)
 
 
 def shift(value, axis, step):
@@ -338,21 +320,17 @@
 
 
 def local(queries, keys, values, offsets_two, offsets_three, w_out):
-    half = D // 2
     exchange = functools.partial(lax.all_to_all, axis_name=GROUP, split_axis=0, concat_axis=0, tiled=True)
-    x = lax.axis_index("x")
+    x, zh = lax.axis_index("x"), lax.axis_index("zh")
     first_head = lax.axis_index(GROUP) * OWN
     own_two = lax.dynamic_slice_in_dim(offsets_two, first_head, OWN)
     own_three = lax.dynamic_slice_in_dim(offsets_three, first_head, OWN)
 
-    core, zh = lax.axis_index("core"), lax.axis_index("zh")
-
-    w_rows = lax.dynamic_slice_in_dim(w_out, core * half, half, axis=1)
-    far_rows = shift(w_rows, "zh", 1)
+    far_rows = shift(w_out, "zh", 1)
     small = pick(offsets_two, offsets_three, queries, keys, values)
     bulk, rest = pack(after(queries, small), keys, values)
-    w_rows = jnp.concatenate([after(w_rows, small), far_rows], 0)
-    w_own = lax.all_gather(w_rows, ("y", "x"), axis=0, tiled=True)
+    weights = jnp.concatenate([after(w_out, small), far_rows], 0)
+    weights = lax.all_gather(weights, ("y", "x"), axis=0, tiled=True)
     got = lax.all_to_all(
         after(small, far_rows).reshape(H * ZH, SENT, PAIR), ("zl", "core", "x", "zh"), split_axis=0, concat_axis=0, tiled=True
     ).reshape(H, ZH, SENT, PAIR)
@@ -363,11 +341,11 @@
     back = jnp.stack([parts[0]] + [shift(parts[step], "x", step) for step in range(1, XS)])
     rest = exchange(after(rest, bulk, back)).reshape(SEG1, PAIR)
     scalars = jnp.concatenate([x.reshape(1), own_two, own_three])
-    att = dense_level(0, scalars, bulk, bulk, back, back)
-    att = dense_level(1, scalars, rest, bulk, back, att)
-    w_other = shift(after(w_own, att), "core", 1)
-    att = exchange(att.reshape(GRP, ROWS, WIDTH))
-    return project(jnp.stack([core, zh]), att, w_own, w_other)
+    first = dense_level(0, scalars, bulk, bulk, back)
+    first = exchange(after(first, rest).reshape(GRP, ROWS, PAIR))
+    second = dense_level(1, scalars, rest, bulk, back)
+    second = exchange(after(second, weights).reshape(GRP, ROWS, PAIR))
+    return project(zh.reshape(1), first, second, weights)
 
 
 def solution(mesh):

time: 178 us -> 173 us (0.972)
  waiting for transfers between devices: 52.6 us -> 35.9 us
  blocking collectives: 21.6 us -> 36.8 us
  Pallas kernels: 40.2 us -> 33.3 us
  starting transfers between devices: 44.6 us -> 47.7 us
    all_to_all x1, waiting for transfers between devices: 20 us -> 3.68 us  [local(): first = exchange(after(first, rest).reshape(GRP, ROWS, PAIR))]
    all_to_all x0 -> x1, blocking collectives: none -> 14.9 us  [local(): second = exchange(after(second, weights).reshape(GRP, ROWS, PAIR))]
    pallas_call x1, Pallas kernels: 8.05 us -> 2.7 us  [project(): pl.pallas_call(project_kernel, in_specs=[pl.BlockSpec(memory_space=pltpu....]
    all_to_all x1, starting transfers between devices: 9.72 us -> 13.2 us  [local(): lax.all_to_all(after(small, far_rows).reshape(H * ZH, SENT, PAIR), ('zl',...]
    ppermute x5 -> x4, starting transfers between devices: 21.4 us -> 18.8 us  [shift(): lax.ppermute(value, axis, [(i, (i + step) % size) for i in range(size)])]
    ppermute x5 -> x4, waiting for transfers between devices: 5.37 us -> 6.36 us  [shift(): lax.ppermute(value, axis, [(i, (i + step) % size) for i in range(size)])]
  transfers between devices with their start and end apart: 10 -> 9, of which waited for: 6 -> 7; matrix products, arithmetic and copies ran while one was open for 0% -> 0% of each run, Pallas kernels for 18% -> 18%
where the time goes in v6:
time: 173 us; the launch traced here: 172 us
  starting transfers between devices  47.7 us (28%)
  blocking collectives  36.8 us (21%)
  waiting for transfers between devices  35.9 us (21%)
  Pallas kernels  33.3 us (19%)
  between operations  13.5 us (8%)
  local copies, waits for them, and re-layouts  3.56 us (2%)
    all_gather x1, blocking collectives, local(): far = lax.all_gather(compact(got), 'y', axis=0, tiled=True)  21.9 us
    ppermute x4, starting transfers between devices, shift(): lax.ppermute(value, axis, [(i, (i + step) % size) for i in range(size)])  18.8 us
    all_to_all x1, waiting for transfers between devices, local(): lax.all_to_all(after(small, far_rows).reshape(H * ZH, SENT, PAIR), ('zl',...  16.9 us
    pallas_call x2, Pallas kernels, dense_level(): pl.pallas_call(functools.partial(dense_kernel, pair), in_specs=[pl.BlockS...  16.7 us
    all_to_all x1, blocking collectives, local(): second = exchange(after(second, weights).reshape(GRP, ROWS, PAIR))  14.9 us
    all_to_all x1, starting transfers between devices, local(): lax.all_to_all(after(small, far_rows).reshape(H * ZH, SENT, PAIR), ('zl',...  13.2 us
    ppermute x4, waiting for transfers between devices, shift(): lax.ppermute(value, axis, [(i, (i + step) % size) for i in range(size)])  6.36 us
    pallas_call x1, Pallas kernels, pack(): pl.pallas_call(pack_kernel, grid=(GRP,), in_specs=[block] * 3, out_specs=...  5.98 us
  transfers between devices with their start and end apart: 9, of which 7 were waited for; matrix products, arithmetic and copies ran while one was open for 0% of the time, Pallas kernels for 18%

profile of v6, /device:TPU:1, one launch (start us, length us, event | category | flops | bytes accessed | tf_op | source)
XLA Modules:
  0.0 171.7 jit_solution(11204743408652072433)
XLA Ops:
  6.5 11.6 %collective-permute-start = (bf16[32,2048]{1,0:T(8,128)(2,1)}, bf16[32,2048]{1,0:T(8,128)(2,1)S(1)}, u32[]{:S(2)}, u32[]{:S(2)}) collective-permute-start(bf16[32,2048]{1,0:T(8,128)(2,1)} %param.11), channel_id=1, source_target_pairs={{0,4},{4,0},{1,5},{5,1},{2,6},{6,2},{3,7},{7,3},{8,12},{12,8},{9,1... | collective-permute-start | bytes 393224 | tf_op jit(solution)/shard_map/ppermute | solution.py:315
  18.1 3.6 %pick.1 = bf16[32,2,48,128]{3,2,1,0:T(8,128)(2,1)} custom-call(s32[32]{0:T(128)} %two_ref.1, s32[32]{0:T(128)} %three_ref.1, bf16[192,2048]{1,0:T(8,128)(2,1)} %q_ref.2, bf16[192,2048]{1,0:T(8,128)(2,1)} %k_ref.3, bf16[192,2048]{1,0:T(8,128)(2,1)} %v_ref.3), custom_call_target="tpu_custom_call" | custom-call | flops 1000000000 | bytes 4000000 | tf_op jit(solution)/shard_map/pick/pallas_call | solution.py:94
  21.7 0.6 collective-permute-done
  22.3 0.7 pad_maximum_fusion.1
  23.1 0.0 all-gather.2.cloned.1.call-update
  23.1 13.2 %all-to-all-start = ((bf16[64,48,128]{2,1,0:T(8,128)(2,1)}), bf16[64,48,128]{2,1,0:T(8,128)(2,1)S(1)}, u32[]{:S(2)}, u32[]{:S(2)}) async-start(bf16[64,48,128]{2,1,0:T(8,128)(2,1)} %bitcast.24), calls=%async_computation | async-start | bytes 1572864 | tf_op jit(solution)/shard_map/all_to_all | solution.py:334
  36.3 6.0 %pack.1 = (bf16[8,192,640]{2,1,0:T(8,128)(2,1)}, bf16[8,192,128]{2,1,0:T(8,128)(2,1)}) custom-call(bf16[192,2048]{1,0:T(8,128)(2,1)} %q_ref.2, bf16[192,2048]{1,0:T(8,128)(2,1)} %k_ref.3, bf16[192,2048]{1,0:T(8,128)(2,1)} %v_ref.3), custom_call_target="tpu_custom_call" | custom-call | bytes 5000000 | tf_op jit(solution)/shard_map/pack/pallas_call | solution.py:118
  42.3 16.9 %all-to-all-done = bf16[64,48,128]{2,1,0:T(8,128)(2,1)S(1)} async-done(((bf16[64,48,128]{2,1,0:T(8,128)(2,1)}), bf16[64,48,128]{2,1,0:T(8,128)(2,1)S(1)}, u32[]{:S(2)}, u32[]{:S(2)}) %all-to-all-start) | async-done | bytes 786464 | tf_op jit(solution)/shard_map/all_to_all | solution.py:334
  59.2 5.9 %all-to-all-start.1 = ((bf16[8,192,640]{2,1,0:T(8,128)(2,1)}), bf16[8,192,640]{2,1,0:T(8,128)(2,1)S(1)}, u32[]{:S(2)}, u32[]{:S(2)}) async-start(bf16[8,192,640]{2,1,0:T(8,128)(2,1)} %get-tuple-element.17), calls=%async_computation.1 | async-start | bytes 3932160 | tf_op jit(solution)/shard_map/all_to_all | solution.py:338
  65.1 0.1 dynamic_slice.7
  65.2 0.1 dynamic_slice.6
  65.3 0.1 pad_add_fusion.1.place_ref
  65.4 0.4 compact_three.1
  65.7 21.9 %all_gather.6.far_ref = bf16[1536,128]{1,0:T(8,128)(2,1)S(1)} all-gather(bf16[192,128]{1,0:T(8,128)(2,1)S(1)} %compact_three.1), channel_id=1, replica_groups=mesh['zl'=4,'core'=2,'y'=8,'zh'=2,'x'=4] {'y'}, dimensions={0}, use_global_device_ids=true | all-gather | bytes 442368 | tf_op jit(solution)/shard_map/all_gather | solution.py:339
  87.6 4.0 %sparse_levels.1 = bf16[4,8,32,128]{3,2,1,0:T(8,128)(2,1)S(1)} custom-call(s32[2]{0:T(128)S(1)} %pad_add_fusion.1.place_ref, bf16[32,2,48,128]{3,2,1,0:T(8,128)(2,1)S(1)} %bitcast.18, bf16[1536,128]{1,0:T(8,128)(2,1)S(1)} %all_gather.6.far_ref), custom_call_target="tpu_custom_call" | custom-call | flops 4000000000 | bytes 2000000 | tf_op jit(solution)/shard_map/sparse_levels/pallas_call | solution.py:191
  91.6 1.9 %collective-permute-start.3 = (bf16[8,32,128]{2,1,0:T(8,128)(2,1)S(1)}, bf16[8,32,128]{2,1,0:T(8,128)(2,1)S(1)}, u32[]{:S(2)}, u32[]{:S(2)}) collective-permute-start(bf16[8,32,128]{2,1,0:T(8,128)(2,1)S(1)} %get-tuple-element.24), channel_id=1, source_target_pairs={{0,3},{1,0},{2,1},{3,2},{4,7},{5,4},{6,5},{7,6},{8,11},{9,8},{10,9... | collective-permute-start | bytes 196616 | tf_op jit(solution)/shard_map/ppermute | solution.py:315
  93.6 2.1 %collective-permute-start.2 = (bf16[8,32,128]{2,1,0:T(8,128)(2,1)S(1)}, bf16[8,32,128]{2,1,0:T(8,128)(2,1)S(1)}, u32[]{:S(2)}, u32[]{:S(2)}) collective-permute-start(bf16[8,32,128]{2,1,0:T(8,128)(2,1)S(1)} %get-tuple-element.25), channel_id=1, source_target_pairs={{0,2},{1,3},{2,0},{3,1},{4,6},{5,7},{6,4},{7,5},{8,10},{9,11},{10,... | collective-permute-start | bytes 196616 | tf_op jit(solution)/shard_map/ppermute | solution.py:315
  95.7 3.1 %collective-permute-start.1 = (bf16[8,32,128]{2,1,0:T(8,128)(2,1)S(1)}, bf16[8,32,128]{2,1,0:T(8,128)(2,1)S(1)}, u32[]{:S(2)}, u32[]{:S(2)}) collective-permute-start(bf16[8,32,128]{2,1,0:T(8,128)(2,1)S(1)} %get-tuple-element.26), channel_id=1, source_target_pairs={{0,1},{1,2},{2,3},{3,0},{4,5},{5,6},{6,7},{7,4},{8,9},{9,10},{10,1... | collective-permute-start | bytes 196616 | tf_op jit(solution)/shard_map/ppermute | solution.py:315
  98.9 0.1 pad_add_fusion.scalar_ref
  99.0 2.6 %collective-permute-done.2 = bf16[8,32,128]{2,1,0:T(8,128)(2,1)S(1)} collective-permute-done((bf16[8,32,128]{2,1,0:T(8,128)(2,1)S(1)}, bf16[8,32,128]{2,1,0:T(8,128)(2,1)S(1)}, u32[]{:S(2)}, u32[]{:S(2)}) %collective-permute-start.2) | collective-permute-done | bytes 65568 | tf_op jit(solution)/shard_map/ppermute | solution.py:315
  101.5 3.2 %collective-permute-done.1 = bf16[8,32,128]{2,1,0:T(8,128)(2,1)S(1)} collective-permute-done((bf16[8,32,128]{2,1,0:T(8,128)(2,1)S(1)}, bf16[8,32,128]{2,1,0:T(8,128)(2,1)S(1)}, u32[]{:S(2)}, u32[]{:S(2)}) %collective-permute-start.1) | collective-permute-done | bytes 65568 | tf_op jit(solution)/shard_map/ppermute | solution.py:315
  104.7 6.0 %all-to-all-done.1 = bf16[8,192,640]{2,1,0:T(8,128)(2,1)S(1)} async-done(((bf16[8,192,640]{2,1,0:T(8,128)(2,1)}), bf16[8,192,640]{2,1,0:T(8,128)(2,1)S(1)}, u32[]{:S(2)}, u32[]{:S(2)}) %all-to-all-start.1) | async-done | bytes 1966112 | tf_op jit(solution)/shard_map/all_to_all | solution.py:338
  110.7 5.5 %all-to-all-start.2 = ((bf16[8,192,128]{2,1,0:T(8,128)(2,1)}), bf16[8,192,128]{2,1,0:T(8,128)(2,1)S(1)}, u32[]{:S(2)}, u32[]{:S(2)}) async-start(bf16[8,192,128]{2,1,0:T(8,128)(2,1)} %get-tuple-element.19), calls=%async_computation.2 | async-start | bytes 786432 | tf_op jit(solution)/shard_map/all_to_all | solution.py:342
  116.2 8.7 %dense_level.2 = bf16[1536,128]{1,0:T(8,128)(2,1)} custom-call(s32[9]{0:T(128)S(1)} %pad_add_fusion.scalar_ref, bf16[1536,640]{1,0:T(8,128)(2,1)S(1)} %bitcast.19, bf16[1536,640]{1,0:T(8,128)(2,1)S(1)} %bitcast.20, bf16[4,8,32,128]{3,2,1,0:T(8,128)(2,1)S(1)} %pad_maximum_fusion.back_ref), custom_call_target="tpu_custom_call" | custom-call | flops 10000000000 | bytes 2000000 | tf_op jit(solution)/shard_map/dense_level/pallas_call | solution.py:267
  124.9 3.0 %all-to-all-done.2 = bf16[8,192,128]{2,1,0:T(8,128)(2,1)S(1)} async-done(((bf16[8,192,128]{2,1,0:T(8,128)(2,1)}), bf16[8,192,128]{2,1,0:T(8,128)(2,1)S(1)}, u32[]{:S(2)}, u32[]{:S(2)}) %all-to-all-start.2) | async-done | bytes 393248 | tf_op jit(solution)/shard_map/all_to_all | solution.py:342
  127.9 4.2 %all-to-all-start.3 = ((bf16[8,192,128]{2,1,0:T(8,128)(2,1)}), bf16[8,192,128]{2,1,0:T(8,128)(2,1)S(1)}, u32[]{:S(2)}, u32[]{:S(2)}) async-start(bf16[8,192,128]{2,1,0:T(8,128)(2,1)} %bitcast.12), calls=%async_computation.3 | async-start | bytes 786432 | tf_op jit(solution)/shard_map/all_to_all | solution.py:345
  132.1 8.0 %dense_level.3 = bf16[1536,128]{1,0:T(8,128)(2,1)S(1)} custom-call(s32[9]{0:T(128)S(1)} %pad_add_fusion.scalar_ref, bf16[1536,128]{1,0:T(8,128)(2,1)S(1)} %bitcast.22, bf16[1536,640]{1,0:T(8,128)(2,1)S(1)} %bitcast.21, bf16[4,8,32,128]{3,2,1,0:T(8,128)(2,1)S(1)} %pad_maximum_fusion.back_ref), custom_call_target="tpu_custom_call" | custom-call | flops 10000000000 | bytes 2000000 | tf_op jit(solution)/shard_map/dense_level/pallas_call | solution.py:267
  140.1 0.0 all-gather.2.cloned.1.call-done.w_ref
  140.1 3.7 %all-to-all-done.3.first_ref = bf16[8,192,128]{2,1,0:T(8,128)(2,1)S(1)} async-done(((bf16[8,192,128]{2,1,0:T(8,128)(2,1)}), bf16[8,192,128]{2,1,0:T(8,128)(2,1)S(1)}, u32[]{:S(2)}, u32[]{:S(2)}) %all-to-all-start.3) | async-done | bytes 393248 | tf_op jit(solution)/shard_map/all_to_all | solution.py:345
  143.8 14.9 %all_to_all.25.second_ref = bf16[8,192,128]{2,1,0:T(8,128)(2,1)S(1)} all-to-all(bf16[8,192,128]{2,1,0:T(8,128)(2,1)S(1)} %bitcast.23), channel_id=1, replica_groups=mesh['zl'=4,'core'=2,'y'=8,'zh'=2,'x'=4] {'zl','core'}, dimensions={0} | all-to-all | bytes 786432 | tf_op jit(solution)/shard_map/all_to_all | solution.py:347
  158.8 3.4 %copy-done = bf16[2048,2048]{1,0:T(8,128)(2,1)S(1)} copy-done((bf16[2048,2048]{1,0:T(8,128)(2,1)S(1)}, bf16[2048,2048]{1,0:T(8,128)(2,1)}, u32[]{:S(2)}) %copy-start) | copy-done | bytes 8388632
  162.1 2.7 %project.1 = bf16[192,2048]{1,0:T(8,128)(2,1)} custom-call(s32[1]{0:T(128)} %bitcast.place_ref, bf16[8,192,128]{2,1,0:T(8,128)(2,1)S(1)} %all-to-all-done.3.first_ref, bf16[8,192,128]{2,1,0:T(8,128)(2,1)S(1)} %all_to_all.25.second_ref, bf16[2048,2048]{1,0:T(8,128)(2,1)S(1)} %copy-done), custom_call_target="tpu_custom_call" | custom-call | flops 1610612736 | bytes 10000000 | tf_op jit(solution)/shard_map/project/pallas_call | solution.py:303
  (11 shorter events, 0.1 us)
Async XLA Ops:
  6.5 15.8 %copy-start.1 = (bf16[32,2048]{1,0:T(8,128)(2,1)S(1)}, bf16[32,2048]{1,0:T(8,128)(2,1)}, u32[]{:S(2)}) copy-start(bf16[32,2048]{1,0:T(8,128)(2,1)} %param.11) | copy-start | bytes 393220
  6.5 133.6 %all-gather.2.cloned.1.call-start = ((), (), s32[]{:S(2)}) async-start(), calls=%async_computation.5 | async-start | bytes 8650752 | tf_op jit(solution)/shard_map/all_gather | solution.py:333
  6.5 15.8 %collective-permute-start = (bf16[32,2048]{1,0:T(8,128)(2,1)}, bf16[32,2048]{1,0:T(8,128)(2,1)S(1)}, u32[]{:S(2)}, u32[]{:S(2)}) collective-permute-start(bf16[32,2048]{1,0:T(8,128)(2,1)} %param.11), channel_id=1, source_target_pairs={{0,4},{4,0},{1,5},{5,1},{2,6},{6,2},{3,7},{7,3},{8,12},{12,8},{9,1... | collective-permute-start | bytes 393224 | tf_op jit(solution)/shard_map/ppermute | solution.py:315
  23.1 36.1 %all-to-all-start = ((bf16[64,48,128]{2,1,0:T(8,128)(2,1)}), bf16[64,48,128]{2,1,0:T(8,128)(2,1)S(1)}, u32[]{:S(2)}, u32[]{:S(2)}) async-start(bf16[64,48,128]{2,1,0:T(8,128)(2,1)} %bitcast.24), calls=%async_computation | async-start | bytes 1572864 | tf_op jit(solution)/shard_map/all_to_all | solution.py:334
  59.2 5.9 %copy-start.2 = (s32[32]{0:T(128)S(1)}, s32[32]{0:T(128)}, u32[]{:S(2)}) copy-start(s32[32]{0:T(128)} %three_ref.1) | copy-start | bytes 388
  59.2 6.0 %copy-start.3 = (s32[32]{0:T(128)S(1)}, s32[32]{0:T(128)}, u32[]{:S(2)}) copy-start(s32[32]{0:T(128)} %two_ref.1) | copy-start | bytes 388
  59.2 51.5 %all-to-all-start.1 = ((bf16[8,192,640]{2,1,0:T(8,128)(2,1)}), bf16[8,192,640]{2,1,0:T(8,128)(2,1)S(1)}, u32[]{:S(2)}, u32[]{:S(2)}) async-start(bf16[8,192,640]{2,1,0:T(8,128)(2,1)} %get-tuple-element.17), calls=%async_computation.1 | async-start | bytes 3932160 | tf_op jit(solution)/shard_map/all_to_all | solution.py:338
  91.6 7.3 %collective-permute-start.3 = (bf16[8,32,128]{2,1,0:T(8,128)(2,1)S(1)}, bf16[8,32,128]{2,1,0:T(8,128)(2,1)S(1)}, u32[]{:S(2)}, u32[]{:S(2)}) collective-permute-start(bf16[8,32,128]{2,1,0:T(8,128)(2,1)S(1)} %get-tuple-element.24), channel_id=1, source_target_pairs={{0,3},{1,0},{2,1},{3,2},{4,7},{5,4},{6,5},{7,6},{8,11},{9,8},{10,9... | collective-permute-start | bytes 196616 | tf_op jit(solution)/shard_map/ppermute | solution.py:315
  93.6 7.9 %collective-permute-start.2 = (bf16[8,32,128]{2,1,0:T(8,128)(2,1)S(1)}, bf16[8,32,128]{2,1,0:T(8,128)(2,1)S(1)}, u32[]{:S(2)}, u32[]{:S(2)}) collective-permute-start(bf16[8,32,128]{2,1,0:T(8,128)(2,1)S(1)} %get-tuple-element.25), channel_id=1, source_target_pairs={{0,2},{1,3},{2,0},{3,1},{4,6},{5,7},{6,4},{7,5},{8,10},{9,11},{10,... | collective-permute-start | bytes 196616 | tf_op jit(solution)/shard_map/ppermute | solution.py:315
  95.7 8.9 %collective-permute-start.1 = (bf16[8,32,128]{2,1,0:T(8,128)(2,1)S(1)}, bf16[8,32,128]{2,1,0:T(8,128)(2,1)S(1)}, u32[]{:S(2)}, u32[]{:S(2)}) collective-permute-start(bf16[8,32,128]{2,1,0:T(8,128)(2,1)S(1)} %get-tuple-element.26), channel_id=1, source_target_pairs={{0,1},{1,2},{2,3},{3,0},{4,5},{5,6},{6,7},{7,4},{8,9},{9,10},{10,1... | collective-permute-start | bytes 196616 | tf_op jit(solution)/shard_map/ppermute | solution.py:315
  110.7 17.2 %all-to-all-start.2 = ((bf16[8,192,128]{2,1,0:T(8,128)(2,1)}), bf16[8,192,128]{2,1,0:T(8,128)(2,1)S(1)}, u32[]{:S(2)}, u32[]{:S(2)}) async-start(bf16[8,192,128]{2,1,0:T(8,128)(2,1)} %get-tuple-element.19), calls=%async_computation.2 | async-start | bytes 786432 | tf_op jit(solution)/shard_map/all_to_all | solution.py:342
  127.9 15.9 %all-to-all-start.3 = ((bf16[8,192,128]{2,1,0:T(8,128)(2,1)}), bf16[8,192,128]{2,1,0:T(8,128)(2,1)S(1)}, u32[]{:S(2)}, u32[]{:S(2)}) async-start(bf16[8,192,128]{2,1,0:T(8,128)(2,1)} %bitcast.12), calls=%async_computation.3 | async-start | bytes 786432 | tf_op jit(solution)/shard_map/all_to_all | solution.py:345
  158.8 3.4 %copy-start = (bf16[2048,2048]{1,0:T(8,128)(2,1)S(1)}, bf16[2048,2048]{1,0:T(8,128)(2,1)}, u32[]{:S(2)}) copy-start(bf16[2048,2048]{1,0:T(8,128)(2,1)} %all-gather.2.cloned.1.call-done.w_ref) | copy-start | bytes 25165828
Sparse Core Ops, SparseCore 0:
  23.2 109.5 all-gather.1

commit v7 on v6

--- a/solution.py
+++ b/solution.py
@@ -106,11 +106,25 @@
     )(offsets_two, offsets_three, queries, keys, values)
 
 
-def pack_kernel(q_ref, k_ref, v_ref, bulk_ref, rest_ref):
-    bulk_ref[0, :, :PAIR] = q_ref[:, :PAIR]
-    bulk_ref[0, :, PAIR : PAIR + WIDTH] = k_ref[...]
-    bulk_ref[0, :, PAIR + WIDTH :] = v_ref[...]
-    rest_ref[0] = q_ref[:, PAIR:]
+def pack_queries_kernel(q_ref, out_ref):
+    for g in range(GRP):
+        out_ref[g] = q_ref[:, g * WIDTH + PAIR : (g + 1) * WIDTH]
+
+
+def pack_queries(queries):
+    return pl.pallas_call(
+        pack_queries_kernel,
+        out_shape=jax.ShapeDtypeStruct((GRP, ROWS, PAIR), BF16),
+        compiler_params=pltpu.CompilerParams(vmem_limit_bytes=56 * 2**20),
+        cost_estimate=cost(0, 10**6),
+        name="pack_queries",
+    )(queries)
+
+
+def pack_kernel(q_ref, k_ref, v_ref, out_ref):
+    out_ref[0, :, :PAIR] = q_ref[:, :PAIR]
+    out_ref[0, :, PAIR : PAIR + WIDTH] = k_ref[...]
+    out_ref[0, :, PAIR + WIDTH :] = v_ref[...]
 
 
 def pack(queries, keys, values):
@@ -119,10 +133,10 @@
         pack_kernel,
         grid=(GRP,),
         in_specs=[block] * 3,
-        out_specs=[pl.BlockSpec((1, ROWS, columns), lambda j: (j, 0, 0)) for columns in (BULK, PAIR)],
-        out_shape=[jax.ShapeDtypeStruct((GRP, ROWS, columns), BF16) for columns in (BULK, PAIR)],
+        out_specs=pl.BlockSpec((1, ROWS, BULK), lambda j: (j, 0, 0)),
+        out_shape=jax.ShapeDtypeStruct((GRP, ROWS, BULK), BF16),
         compiler_params=pltpu.CompilerParams(vmem_limit_bytes=56 * 2**20),
-        cost_estimate=cost(0, 5 * 10**6),
+        cost_estimate=cost(0, 4 * 10**6),
         name="pack",
     )(queries, keys, values)
 
@@ -281,33 +295,33 @@
     )(scalars, q, bulk, back)
 
 
-def project_kernel(place_ref, first_ref, second_ref, w_ref, out_ref):
-    upper = place_ref[0] == 1
+def project_kernel(pair, place_ref, att_ref, w_ref, *refs):
+    out_ref = refs[-1]
+    far = (place_ref[0] + pair) % ZH
     part = WIDTH // (XS * ZH)
     columns = 512
-    att = []
-    for g in range(GRP):
-        low, high = first_ref[g], second_ref[g]
-        att.append(jnp.concatenate([jnp.where(upper, high, low), jnp.where(upper, low, high)], 1))
     for start in range(0, D, columns):
-        total = None
-        for g in range(GRP):
-            rows = [g * WIDTH + (x * ZH + far) * part for far in range(ZH) for x in range(XS)]
-            weights = jnp.concatenate([w_ref[row : row + part, start : start + columns] for row in rows], 0)
-            term = jnp.dot(att[g], weights, preferred_element_type=F32)
+        lanes = slice(start, start + columns)
+        total = refs[0][:, lanes] if pair else None
+        for first in range(0, GRP, 2):
+            both = (first, first + 1)
+            rows = [pl.multiple_of(g * WIDTH + x * ZH * part + far * part, part) for g in both for x in range(XS)]
+            weights = jnp.concatenate([w_ref[pl.ds(row, part), lanes] for row in rows], 0)
+            att = jnp.concatenate([att_ref[g] for g in both], 1)
+            term = jnp.dot(att, weights, preferred_element_type=F32)
             total = term if total is None else total + term
-        out_ref[:, start : start + columns] = total.astype(BF16)
-
-
-def project(zh, first, second, weights):
-    return pl.pallas_call(
-        project_kernel,
-        in_specs=[pl.BlockSpec(memory_space=pltpu.SMEM)] + [pl.BlockSpec(memory_space=pltpu.VMEM)] * 3,
-        out_shape=jax.ShapeDtypeStruct((ROWS, D), BF16),
+        out_ref[:, lanes] = total.astype(out_ref.dtype)
+
+
+def project(pair, zh, att, weights, *before):
+    return pl.pallas_call(
+        functools.partial(project_kernel, pair),
+        in_specs=[pl.BlockSpec(memory_space=pltpu.SMEM)] + [pl.BlockSpec(memory_space=pltpu.VMEM)] * (2 + pair),
+        out_shape=jax.ShapeDtypeStruct((ROWS, D), BF16 if pair else F32),
         compiler_params=params(),
-        cost_estimate=cost(2 * ROWS * D * D, 10 * 10**6),
+        cost_estimate=cost(ROWS * D * D, 6 * 10**6),
         name="project",
-    )(zh, first, second, weights)
+    )(zh, att, weights, *before)
 
 
 def shift(value, axis, step):
@@ -326,26 +340,32 @@
     own_two = lax.dynamic_slice_in_dim(offsets_two, first_head, OWN)
     own_three = lax.dynamic_slice_in_dim(offsets_three, first_head, OWN)
 
-    far_rows = shift(w_out, "zh", 1)
-    small = pick(offsets_two, offsets_three, queries, keys, values)
-    bulk, rest = pack(after(queries, small), keys, values)
+    rest = pack_queries(queries)
+    far_rows = shift(after(w_out, rest), "zh", 1)
+    small = pick(offsets_two, offsets_three, after(queries, rest), keys, values)
     weights = jnp.concatenate([after(w_out, small), far_rows], 0)
     weights = lax.all_gather(weights, ("y", "x"), axis=0, tiled=True)
+    rest = exchange(rest).reshape(SEG1, PAIR)
     got = lax.all_to_all(
-        after(small, far_rows).reshape(H * ZH, SENT, PAIR), ("zl", "core", "x", "zh"), split_axis=0, concat_axis=0, tiled=True
+        after(small, far_rows, rest).reshape(H * ZH, SENT, PAIR),
+        ("zl", "core", "x", "zh"),
+        split_axis=0,
+        concat_axis=0,
+        tiled=True,
     ).reshape(H, ZH, SENT, PAIR)
+    bulk = pack(after(queries, small), keys, values)
 
     bulk = exchange(after(bulk, got)).reshape(SEG1, BULK)
     far = lax.all_gather(compact(got), "y", axis=0, tiled=True)
     parts = sparse_levels(jnp.stack([x, zh]), got, far)
     back = jnp.stack([parts[0]] + [shift(parts[step], "x", step) for step in range(1, XS)])
-    rest = exchange(after(rest, bulk, back)).reshape(SEG1, PAIR)
     scalars = jnp.concatenate([x.reshape(1), own_two, own_three])
     first = dense_level(0, scalars, bulk, bulk, back)
-    first = exchange(after(first, rest).reshape(GRP, ROWS, PAIR))
+    first = exchange(first.reshape(GRP, ROWS, PAIR))
     second = dense_level(1, scalars, rest, bulk, back)
-    second = exchange(after(second, weights).reshape(GRP, ROWS, PAIR))
-    return project(zh.reshape(1), first, second, weights)
+    second = exchange(second.reshape(GRP, ROWS, PAIR))
+    place = zh.reshape(1)
+    return project(1, place, second, weights, project(0, place, first, weights))
 
 
 def solution(mesh):

time: 173 us -> 182 us (1.052)
  blocking collectives: 36.8 us -> 42.5 us
  starting transfers between devices: 47.7 us -> 44.1 us
  local copies, waits for them, and re-layouts: 3.56 us -> 6.95 us
  Pallas kernels: 33.3 us -> 36.1 us
    all_to_all x3, waiting for transfers between devices: 23.6 us -> 27.3 us  [the longest x1 17 us: local(): lax.all_to_all(after(small, far_rows, rest).reshape(H * ZH, SENT, PAIR),...]
    all_to_all x3, starting transfers between devices: 23 us -> 19.3 us  [the longest x1 10.5 us: local(): lax.all_to_all(after(small, far_rows, rest).reshape(H * ZH, SENT, PAIR),...]
    all_to_all x1, blocking collectives: 14.9 us -> 18.5 us  [local(): rest = exchange(rest).reshape(SEG1, PAIR)]
    unnamed x8 -> x12, local copies, waits for them, and re-layouts: 3.39 us -> 6.78 us
    pallas_call x1 -> x3, Pallas kernels: 2.7 us -> 4.87 us  [the longest x2 2.89 us: project(): pl.pallas_call(functools.partial(project_kernel, pair), in_specs=[pl.Bloc...]
    all_gather x1, blocking collectives: 21.9 us -> 23.9 us  [local(): far = lax.all_gather(compact(got), 'y', axis=0, tiled=True)]
where the time goes in v7:
time: 182 us; the launch traced here: 181 us
  starting transfers between devices  44.1 us (24%)
  blocking collectives  42.5 us (23%)
  waiting for transfers between devices  37.5 us (21%)
  Pallas kernels  36.1 us (20%)
  between operations  13.5 us (7%)
  local copies, waits for them, and re-layouts  6.95 us (4%)
    all_gather x1, blocking collectives, local(): far = lax.all_gather(compact(got), 'y', axis=0, tiled=True)  23.9 us
    ppermute x4, starting transfers between devices, shift(): lax.ppermute(value, axis, [(i, (i + step) % size) for i in range(size)])  18.8 us
    all_to_all x1, blocking collectives, local(): rest = exchange(rest).reshape(SEG1, PAIR)  18.5 us
    pallas_call x2, Pallas kernels, dense_level(): pl.pallas_call(functools.partial(dense_kernel, pair), in_specs=[pl.BlockS...  17.4 us
    all_to_all x1, waiting for transfers between devices, local(): lax.all_to_all(after(small, far_rows, rest).reshape(H * ZH, SENT, PAIR),...  17 us
    all_to_all x1, starting transfers between devices, local(): lax.all_to_all(after(small, far_rows, rest).reshape(H * ZH, SENT, PAIR),...  10.5 us
    all_to_all x1, waiting for transfers between devices, local(): second = exchange(second.reshape(GRP, ROWS, PAIR))  7.3 us
    unnamed x12, local copies, waits for them, and re-layouts  6.78 us
  transfers between devices with their start and end apart: 9, of which 7 were waited for; matrix products, arithmetic and copies ran while one was open for 0% of the time, Pallas kernels for 18%

profile of v7, /device:TPU:1, one launch (start us, length us, event | category | flops | bytes accessed | tf_op | source)
XLA Modules:
  0.0 181.5 jit_solution(15413945664926846431)
XLA Ops:
  6.5 2.0 %pack_queries.1 = bf16[8,192,128]{2,1,0:T(8,128)(2,1)} custom-call(bf16[192,2048]{1,0:T(8,128)(2,1)} %q_ref.3), custom_call_target="tpu_custom_call" | custom-call | bytes 1000000 | tf_op jit(solution)/shard_map/pack_queries/pallas_call | solution.py:115
  8.5 11.6 %collective-permute-start = (bf16[32,2048]{1,0:T(8,128)(2,1)}, bf16[32,2048]{1,0:T(8,128)(2,1)S(1)}, u32[]{:S(2)}, u32[]{:S(2)}) collective-permute-start(bf16[32,2048]{1,0:T(8,128)(2,1)} %param.11), channel_id=1, source_target_pairs={{0,4},{4,0},{1,5},{5,1},{2,6},{6,2},{3,7},{7,3},{8,12},{12,8},{9,1... | collective-permute-start | bytes 393224 | tf_op jit(solution)/shard_map/ppermute | solution.py:329
  20.1 3.6 %pick.1 = bf16[32,2,48,128]{3,2,1,0:T(8,128)(2,1)} custom-call(s32[32]{0:T(128)} %two_ref.1, s32[32]{0:T(128)} %three_ref.1, bf16[192,2048]{1,0:T(8,128)(2,1)} %q_ref.3, bf16[192,2048]{1,0:T(8,128)(2,1)} %k_ref.3, bf16[192,2048]{1,0:T(8,128)(2,1)} %v_ref.3), custom_call_target="tpu_custom_call" | custom-call | flops 1000000000 | bytes 4000000 | tf_op jit(solution)/shard_map/pick/pallas_call | solution.py:94
  23.7 0.6 collective-permute-done
  24.3 0.7 pad_maximum_fusion.1
  25.1 18.5 %all_to_all.25 = bf16[8,192,128]{2,1,0:T(8,128)(2,1)S(1)} all-to-all(bf16[8,192,128]{2,1,0:T(8,128)(2,1)S(1)} %copy-done.2), channel_id=1, replica_groups=mesh['zl'=4,'core'=2,'y'=8,'zh'=2,'x'=4] {'zl','core'}, dimensions={0} | all-to-all | bytes 786432 | tf_op jit(solution)/shard_map/all_to_all | solution.py:348
  43.6 10.5 %all-to-all-start.1 = ((bf16[64,48,128]{2,1,0:T(8,128)(2,1)}), bf16[64,48,128]{2,1,0:T(8,128)(2,1)S(1)}, u32[]{:S(2)}, u32[]{:S(2)}) async-start(bf16[64,48,128]{2,1,0:T(8,128)(2,1)} %bitcast.23), calls=%async_computation.1 | async-start | bytes 1572864 | tf_op jit(solution)/shard_map/all_to_all | solution.py:349
  54.1 5.9 %pack.1 = bf16[8,192,640]{2,1,0:T(8,128)(2,1)} custom-call(bf16[192,2048]{1,0:T(8,128)(2,1)} %q_ref.3, bf16[192,2048]{1,0:T(8,128)(2,1)} %k_ref.3, bf16[192,2048]{1,0:T(8,128)(2,1)} %v_ref.3), custom_call_target="tpu_custom_call" | custom-call | bytes 4000000 | tf_op jit(solution)/shard_map/pack/pallas_call | solution.py:132
  60.0 17.0 %all-to-all-done.1 = bf16[64,48,128]{2,1,0:T(8,128)(2,1)S(1)} async-done(((bf16[64,48,128]{2,1,0:T(8,128)(2,1)}), bf16[64,48,128]{2,1,0:T(8,128)(2,1)S(1)}, u32[]{:S(2)}, u32[]{:S(2)}) %all-to-all-start.1) | async-done | bytes 786464 | tf_op jit(solution)/shard_map/all_to_all | solution.py:349
  77.0 5.9 %all-to-all-start.2 = ((bf16[8,192,640]{2,1,0:T(8,128)(2,1)}), bf16[8,192,640]{2,1,0:T(8,128)(2,1)S(1)}, u32[]{:S(2)}, u32[]{:S(2)}) async-start(bf16[8,192,640]{2,1,0:T(8,128)(2,1)} %pack.1), calls=%async_computation.2 | async-start | bytes 3932160 | tf_op jit(solution)/shard_map/all_to_all | solution.py:358
  83.0 0.1 dynamic_slice.7
  83.1 0.1 pad_add_fusion.1.place_ref
  83.2 0.4 compact_three.1
  83.6 23.9 %all_gather.6.far_ref = bf16[1536,128]{1,0:T(8,128)(2,1)S(1)} all-gather(bf16[192,128]{1,0:T(8,128)(2,1)S(1)} %compact_three.1), channel_id=1, replica_groups=mesh['zl'=4,'core'=2,'y'=8,'zh'=2,'x'=4] {'y'}, dimensions={0}, use_global_device_ids=true | all-gather | bytes 442368 | tf_op jit(solution)/shard_map/all_gather | solution.py:359
  107.5 4.0 %sparse_levels.1 = bf16[4,8,32,128]{3,2,1,0:T(8,128)(2,1)S(1)} custom-call(s32[2]{0:T(128)S(1)} %pad_add_fusion.1.place_ref, bf16[32,2,48,128]{3,2,1,0:T(8,128)(2,1)S(1)} %bitcast.18, bf16[1536,128]{1,0:T(8,128)(2,1)S(1)} %all_gather.6.far_ref), custom_call_target="tpu_custom_call" | custom-call | flops 4000000000 | bytes 2000000 | tf_op jit(solution)/shard_map/sparse_levels/pallas_call | solution.py:205
  111.5 2.1 %collective-permute-start.3 = (bf16[8,32,128]{2,1,0:T(8,128)(2,1)S(1)}, bf16[8,32,128]{2,1,0:T(8,128)(2,1)S(1)}, u32[]{:S(2)}, u32[]{:S(2)}) collective-permute-start(bf16[8,32,128]{2,1,0:T(8,128)(2,1)S(1)} %get-tuple-element.18), channel_id=1, source_target_pairs={{0,3},{1,0},{2,1},{3,2},{4,7},{5,4},{6,5},{7,6},{8,11},{9,8},{10,9... | collective-permute-start | bytes 196616 | tf_op jit(solution)/shard_map/ppermute | solution.py:329
  113.6 1.9 %collective-permute-start.2 = (bf16[8,32,128]{2,1,0:T(8,128)(2,1)S(1)}, bf16[8,32,128]{2,1,0:T(8,128)(2,1)S(1)}, u32[]{:S(2)}, u32[]{:S(2)}) collective-permute-start(bf16[8,32,128]{2,1,0:T(8,128)(2,1)S(1)} %get-tuple-element.19), channel_id=1, source_target_pairs={{0,2},{1,3},{2,0},{3,1},{4,6},{5,7},{6,4},{7,5},{8,10},{9,11},{10,... | collective-permute-start | bytes 196616 | tf_op jit(solution)/shard_map/ppermute | solution.py:329
  115.6 3.2 %collective-permute-start.1 = (bf16[8,32,128]{2,1,0:T(8,128)(2,1)S(1)}, bf16[8,32,128]{2,1,0:T(8,128)(2,1)S(1)}, u32[]{:S(2)}, u32[]{:S(2)}) collective-permute-start(bf16[8,32,128]{2,1,0:T(8,128)(2,1)S(1)} %get-tuple-element.20), channel_id=1, source_target_pairs={{0,1},{1,2},{2,3},{3,0},{4,5},{5,6},{6,7},{7,4},{8,9},{9,10},{10,1... | collective-permute-start | bytes 196616 | tf_op jit(solution)/shard_map/ppermute | solution.py:329
  118.7 0.1 pad_add_fusion.scalar_ref
  118.8 2.7 %collective-permute-done.2 = bf16[8,32,128]{2,1,0:T(8,128)(2,1)S(1)} collective-permute-done((bf16[8,32,128]{2,1,0:T(8,128)(2,1)S(1)}, bf16[8,32,128]{2,1,0:T(8,128)(2,1)S(1)}, u32[]{:S(2)}, u32[]{:S(2)}) %collective-permute-start.2) | collective-permute-done | bytes 65568 | tf_op jit(solution)/shard_map/ppermute | solution.py:329
  121.5 2.3 %collective-permute-done.1 = bf16[8,32,128]{2,1,0:T(8,128)(2,1)S(1)} collective-permute-done((bf16[8,32,128]{2,1,0:T(8,128)(2,1)S(1)}, bf16[8,32,128]{2,1,0:T(8,128)(2,1)S(1)}, u32[]{:S(2)}, u32[]{:S(2)}) %collective-permute-start.1) | collective-permute-done | bytes 65568 | tf_op jit(solution)/shard_map/ppermute | solution.py:329
  123.9 4.5 %all-to-all-done.2 = bf16[8,192,640]{2,1,0:T(8,128)(2,1)S(1)} async-done(((bf16[8,192,640]{2,1,0:T(8,128)(2,1)}), bf16[8,192,640]{2,1,0:T(8,128)(2,1)S(1)}, u32[]{:S(2)}, u32[]{:S(2)}) %all-to-all-start.2) | async-done | bytes 1966112 | tf_op jit(solution)/shard_map/all_to_all | solution.py:358
  128.4 8.7 %dense_level.3 = bf16[1536,128]{1,0:T(8,128)(2,1)} custom-call(s32[9]{0:T(128)S(1)} %pad_add_fusion.scalar_ref, bf16[1536,640]{1,0:T(8,128)(2,1)S(1)} %bitcast.19, bf16[1536,640]{1,0:T(8,128)(2,1)S(1)} %bitcast.20, bf16[4,8,32,128]{3,2,1,0:T(8,128)(2,1)S(1)} %pad_maximum_fusion.back_ref), custom_call_target="tpu_custom_call" | custom-call | flops 10000000000 | bytes 2000000 | tf_op jit(solution)/shard_map/dense_level/pallas_call | solution.py:281
  137.1 4.6 %all-to-all-start.4 = ((bf16[8,192,128]{2,1,0:T(8,128)(2,1)}), bf16[8,192,128]{2,1,0:T(8,128)(2,1)S(1)}, u32[]{:S(2)}, u32[]{:S(2)}) async-start(bf16[8,192,128]{2,1,0:T(8,128)(2,1)} %bitcast.13), calls=%async_computation.4 | async-start | bytes 786432 | tf_op jit(solution)/shard_map/all_to_all | solution.py:364
  141.8 8.7 %dense_level.2 = bf16[1536,128]{1,0:T(8,128)(2,1)} custom-call(s32[9]{0:T(128)S(1)} %pad_add_fusion.scalar_ref, bf16[1536,128]{1,0:T(8,128)(2,1)S(1)} %bitcast.22, bf16[1536,640]{1,0:T(8,128)(2,1)S(1)} %bitcast.21, bf16[4,8,32,128]{3,2,1,0:T(8,128)(2,1)S(1)} %pad_maximum_fusion.back_ref), custom_call_target="tpu_custom_call" | custom-call | flops 10000000000 | bytes 2000000 | tf_op jit(solution)/shard_map/dense_level/pallas_call | solution.py:281
  150.5 3.0 %all-to-all-done.4.att_ref = bf16[8,192,128]{2,1,0:T(8,128)(2,1)S(1)} async-done(((bf16[8,192,128]{2,1,0:T(8,128)(2,1)}), bf16[8,192,128]{2,1,0:T(8,128)(2,1)S(1)}, u32[]{:S(2)}, u32[]{:S(2)}) %all-to-all-start.4) | async-done | bytes 393248 | tf_op jit(solution)/shard_map/all_to_all | solution.py:364
  153.4 4.2 %all-to-all-start.3 = ((bf16[8,192,128]{2,1,0:T(8,128)(2,1)}), bf16[8,192,128]{2,1,0:T(8,128)(2,1)S(1)}, u32[]{:S(2)}, u32[]{:S(2)}) async-start(bf16[8,192,128]{2,1,0:T(8,128)(2,1)} %bitcast.12), calls=%async_computation.3 | async-start | bytes 786432 | tf_op jit(solution)/shard_map/all_to_all | solution.py:366
  157.7 3.4 %copy-done = bf16[2048,2048]{1,0:T(8,128)(2,1)S(1)} copy-done((bf16[2048,2048]{1,0:T(8,128)(2,1)S(1)}, bf16[2048,2048]{1,0:T(8,128)(2,1)}, u32[]{:S(2)}) %copy-start) | copy-done | bytes 8388632
  161.0 1.0 project.2.refs_0_
  162.1 7.3 %all-to-all-done.3.att_ref = bf16[8,192,128]{2,1,0:T(8,128)(2,1)S(1)} async-done(((bf16[8,192,128]{2,1,0:T(8,128)(2,1)}), bf16[8,192,128]{2,1,0:T(8,128)(2,1)S(1)}, u32[]{:S(2)}, u32[]{:S(2)}) %all-to-all-start.3) | async-done | bytes 393248 | tf_op jit(solution)/shard_map/all_to_all | solution.py:366
  169.4 3.4 %copy-done.1 = bf16[2048,2048]{1,0:T(8,128)(2,1)S(1)} copy-done((bf16[2048,2048]{1,0:T(8,128)(2,1)S(1)}, bf16[2048,2048]{1,0:T(8,128)(2,1)}, u32[]{:S(2)}) %copy-start.1) | copy-done | bytes 8388632
  172.8 1.9 %project.3 = bf16[192,2048]{1,0:T(8,128)(2,1)} custom-call(s32[1]{0:T(128)} %bitcast.place_ref, bf16[8,192,128]{2,1,0:T(8,128)(2,1)S(1)} %all-to-all-done.3.att_ref, bf16[2048,2048]{1,0:T(8,128)(2,1)S(1)} %copy-done.1, f32[192,2048]{1,0:T(8,128)S(1)} %project.2.refs_0_), custom_call_target="tpu_custom_call" | custom-call | flops 805306368 | bytes 6000000 | tf_op jit(solution)/shard_map/project/pallas_call | solution.py:317
  (17 shorter events, 0.2 us)
Async XLA Ops:
  6.5 151.1 %all-gather.2.cloned.1.call-start = ((), (), s32[]{:S(2)}) async-start(), calls=%async_computation.5 | async-start | bytes 8650752 | tf_op jit(solution)/shard_map/all_gather | solution.py:347
  8.5 15.8 %copy-start.3 = (bf16[32,2048]{1,0:T(8,128)(2,1)S(1)}, bf16[32,2048]{1,0:T(8,128)(2,1)}, u32[]{:S(2)}) copy-start(bf16[32,2048]{1,0:T(8,128)(2,1)} %param.11) | copy-start | bytes 393220
  8.5 16.6 %copy-start.2 = (bf16[8,192,128]{2,1,0:T(8,128)(2,1)S(1)}, bf16[8,192,128]{2,1,0:T(8,128)(2,1)}, u32[]{:S(2)}) copy-start(bf16[8,192,128]{2,1,0:T(8,128)(2,1)} %pack_queries.1) | copy-start | bytes 1179652
  8.5 15.8 %collective-permute-start = (bf16[32,2048]{1,0:T(8,128)(2,1)}, bf16[32,2048]{1,0:T(8,128)(2,1)S(1)}, u32[]{:S(2)}, u32[]{:S(2)}) collective-permute-start(bf16[32,2048]{1,0:T(8,128)(2,1)} %param.11), channel_id=1, source_target_pairs={{0,4},{4,0},{1,5},{5,1},{2,6},{6,2},{3,7},{7,3},{8,12},{12,8},{9,1... | collective-permute-start | bytes 393224 | tf_op jit(solution)/shard_map/ppermute | solution.py:329
  43.6 33.4 %all-to-all-start.1 = ((bf16[64,48,128]{2,1,0:T(8,128)(2,1)}), bf16[64,48,128]{2,1,0:T(8,128)(2,1)S(1)}, u32[]{:S(2)}, u32[]{:S(2)}) async-start(bf16[64,48,128]{2,1,0:T(8,128)(2,1)} %bitcast.23), calls=%async_computation.1 | async-start | bytes 1572864 | tf_op jit(solution)/shard_map/all_to_all | solution.py:349
  77.0 5.9 %copy-start.4 = (s32[32]{0:T(128)S(1)}, s32[32]{0:T(128)}, u32[]{:S(2)}) copy-start(s32[32]{0:T(128)} %three_ref.1) | copy-start | bytes 388
  77.0 6.0 %copy-start.5 = (s32[32]{0:T(128)S(1)}, s32[32]{0:T(128)}, u32[]{:S(2)}) copy-start(s32[32]{0:T(128)} %two_ref.1) | copy-start | bytes 388
  77.0 51.3 %all-to-all-start.2 = ((bf16[8,192,640]{2,1,0:T(8,128)(2,1)}), bf16[8,192,640]{2,1,0:T(8,128)(2,1)S(1)}, u32[]{:S(2)}, u32[]{:S(2)}) async-start(bf16[8,192,640]{2,1,0:T(8,128)(2,1)} %pack.1), calls=%async_computation.2 | async-start | bytes 3932160 | tf_op jit(solution)/shard_map/all_to_all | solution.py:358
  111.5 7.3 %collective-permute-start.3 = (bf16[8,32,128]{2,1,0:T(8,128)(2,1)S(1)}, bf16[8,32,128]{2,1,0:T(8,128)(2,1)S(1)}, u32[]{:S(2)}, u32[]{:S(2)}) collective-permute-start(bf16[8,32,128]{2,1,0:T(8,128)(2,1)S(1)} %get-tuple-element.18), channel_id=1, source_target_pairs={{0,3},{1,0},{2,1},{3,2},{4,7},{5,4},{6,5},{7,6},{8,11},{9,8},{10,9... | collective-permute-start | bytes 196616 | tf_op jit(solution)/shard_map/ppermute | solution.py:329
  113.6 7.9 %collective-permute-start.2 = (bf16[8,32,128]{2,1,0:T(8,128)(2,1)S(1)}, bf16[8,32,128]{2,1,0:T(8,128)(2,1)S(1)}, u32[]{:S(2)}, u32[]{:S(2)}) collective-permute-start(bf16[8,32,128]{2,1,0:T(8,128)(2,1)S(1)} %get-tuple-element.19), channel_id=1, source_target_pairs={{0,2},{1,3},{2,0},{3,1},{4,6},{5,7},{6,4},{7,5},{8,10},{9,11},{10,... | collective-permute-start | bytes 196616 | tf_op jit(solution)/shard_map/ppermute | solution.py:329
  115.6 8.3 %collective-permute-start.1 = (bf16[8,32,128]{2,1,0:T(8,128)(2,1)S(1)}, bf16[8,32,128]{2,1,0:T(8,128)(2,1)S(1)}, u32[]{:S(2)}, u32[]{:S(2)}) collective-permute-start(bf16[8,32,128]{2,1,0:T(8,128)(2,1)S(1)} %get-tuple-element.20), channel_id=1, source_target_pairs={{0,1},{1,2},{2,3},{3,0},{4,5},{5,6},{6,7},{7,4},{8,9},{9,10},{10,1... | collective-permute-start | bytes 196616 | tf_op jit(solution)/shard_map/ppermute | solution.py:329
  137.1 16.3 %all-to-all-start.4 = ((bf16[8,192,128]{2,1,0:T(8,128)(2,1)}), bf16[8,192,128]{2,1,0:T(8,128)(2,1)S(1)}, u32[]{:S(2)}, u32[]{:S(2)}) async-start(bf16[8,192,128]{2,1,0:T(8,128)(2,1)} %bitcast.13), calls=%async_computation.4 | async-start | bytes 786432 | tf_op jit(solution)/shard_map/all_to_all | solution.py:364
  153.4 15.9 %all-to-all-start.3 = ((bf16[8,192,128]{2,1,0:T(8,128)(2,1)}), bf16[8,192,128]{2,1,0:T(8,128)(2,1)S(1)}, u32[]{:S(2)}, u32[]{:S(2)}) async-start(bf16[8,192,128]{2,1,0:T(8,128)(2,1)} %bitcast.12), calls=%async_computation.3 | async-start | bytes 786432 | tf_op jit(solution)/shard_map/all_to_all | solution.py:366
  157.7 3.4 %copy-start = (bf16[2048,2048]{1,0:T(8,128)(2,1)S(1)}, bf16[2048,2048]{1,0:T(8,128)(2,1)}, u32[]{:S(2)}) copy-start(bf16[2048,2048]{1,0:T(8,128)(2,1)} %all-gather.2.cloned.1.call-done.w_ref) | copy-start | bytes 25165828
  169.4 3.4 %copy-start.1 = (bf16[2048,2048]{1,0:T(8,128)(2,1)S(1)}, bf16[2048,2048]{1,0:T(8,128)(2,1)}, u32[]{:S(2)}) copy-start(bf16[2048,2048]{1,0:T(8,128)(2,1)} %all-gather.2.cloned.1.call-done.w_ref) | copy-start | bytes 25165828
Sparse Core Ops, SparseCore 0:
  25.2 108.3 all-gather.1

commit v8 on v6

--- a/solution.py
+++ b/solution.py
@@ -281,33 +281,63 @@
     )(scalars, q, bulk, back)
 
 
-def project_kernel(place_ref, first_ref, second_ref, w_ref, out_ref):
-    upper = place_ref[0] == 1
-    part = WIDTH // (XS * ZH)
-    columns = 512
-    att = []
-    for g in range(GRP):
-        low, high = first_ref[g], second_ref[g]
-        att.append(jnp.concatenate([jnp.where(upper, high, low), jnp.where(upper, low, high)], 1))
-    for start in range(0, D, columns):
+COLUMNS = 512
+PART_ROWS = WIDTH // (XS * ZH)
+
+
+def pairs_of_groups(att_ref):
+    for first in range(0, GRP, 2):
+        yield first, jnp.concatenate([att_ref[first], att_ref[first + 1]], 1)
+
+
+def project_first_kernel(place_ref, att_ref, w_ref, out_ref, later_ref):
+    def weights_of(first, half, lanes):
+        far = (place_ref[0] + half) % ZH
+        both = (first, first + 1)
+        rows = [pl.multiple_of(g * WIDTH + (x * ZH + far) * PART_ROWS, PART_ROWS) for g in both for x in range(XS)]
+        return jnp.concatenate([w_ref[pl.ds(row, PART_ROWS), lanes] for row in rows], 0)
+
+    for start in range(0, D, COLUMNS):
+        lanes = slice(start, start + COLUMNS)
         total = None
-        for g in range(GRP):
-            rows = [g * WIDTH + (x * ZH + far) * part for far in range(ZH) for x in range(XS)]
-            weights = jnp.concatenate([w_ref[row : row + part, start : start + columns] for row in rows], 0)
-            term = jnp.dot(att[g], weights, preferred_element_type=F32)
+        for first, att in pairs_of_groups(att_ref):
+            term = jnp.dot(att, weights_of(first, 0, lanes), preferred_element_type=F32)
             total = term if total is None else total + term
-        out_ref[:, start : start + columns] = total.astype(BF16)
-
-
-def project(zh, first, second, weights):
-    return pl.pallas_call(
-        project_kernel,
-        in_specs=[pl.BlockSpec(memory_space=pltpu.SMEM)] + [pl.BlockSpec(memory_space=pltpu.VMEM)] * 3,
+            later_ref[first * PAIR : (first + 2) * PAIR, lanes] = weights_of(first, 1, lanes)
+        out_ref[:, lanes] = total
+
+
+def project_first(zh, att, weights):
+    return pl.pallas_call(
+        project_first_kernel,
+        in_specs=[pl.BlockSpec(memory_space=pltpu.SMEM)] + [pl.BlockSpec(memory_space=pltpu.VMEM)] * 2,
+        out_specs=[pl.BlockSpec(memory_space=pltpu.VMEM)] * 2,
+        out_shape=[jax.ShapeDtypeStruct((ROWS, D), F32), jax.ShapeDtypeStruct((D // 2, D), BF16)],
+        compiler_params=params(),
+        cost_estimate=cost(ROWS * D * D, 12 * 10**6),
+        name="project_first",
+    )(zh, att, weights)
+
+
+def project_second_kernel(before_ref, att_ref, w_ref, out_ref):
+    for start in range(0, D, COLUMNS):
+        lanes = slice(start, start + COLUMNS)
+        total = before_ref[:, lanes]
+        for first, att in pairs_of_groups(att_ref):
+            total += jnp.dot(att, w_ref[first * PAIR : (first + 2) * PAIR, lanes], preferred_element_type=F32)
+        out_ref[:, lanes] = total.astype(BF16)
+
+
+def project_second(before, att, weights):
+    return pl.pallas_call(
+        project_second_kernel,
+        in_specs=[pl.BlockSpec(memory_space=pltpu.VMEM)] * 3,
+        out_specs=pl.BlockSpec(memory_space=pltpu.VMEM),
         out_shape=jax.ShapeDtypeStruct((ROWS, D), BF16),
         compiler_params=params(),
-        cost_estimate=cost(2 * ROWS * D * D, 10 * 10**6),
-        name="project",
-    )(zh, first, second, weights)
+        cost_estimate=cost(ROWS * D * D, 6 * 10**6),
+        name="project_second",
+    )(before, att, weights)
 
 
 def shift(value, axis, step):
@@ -344,8 +374,9 @@
     first = dense_level(0, scalars, bulk, bulk, back)
     first = exchange(after(first, rest).reshape(GRP, ROWS, PAIR))
     second = dense_level(1, scalars, rest, bulk, back)
-    second = exchange(after(second, weights).reshape(GRP, ROWS, PAIR))
-    return project(zh.reshape(1), first, second, weights)
+    second = exchange(after(second, first).reshape(GRP, ROWS, PAIR))
+    partial, weights = project_first(zh.reshape(1), first, weights)
+    return project_second(partial, second, weights)
 
 
 def solution(mesh):

time: 173 us -> 172 us (level)
  blocking collectives: 36.8 us -> 21.9 us
  starting transfers between devices: 47.7 us -> 51.9 us
  local copies, waits for them, and re-layouts: 3.56 us -> 7.68 us
  waiting for transfers between devices: 35.9 us -> 40 us
    all_to_all x1 -> x0, blocking collectives: 14.9 us -> none  [local(): second = exchange(after(second, weights).reshape(GRP, ROWS, PAIR))]
    all_to_all x0 -> x1, waiting for transfers between devices: none -> 4.84 us  [local(): second = exchange(after(second, first).reshape(GRP, ROWS, PAIR))]
    all_to_all x0 -> x1, starting transfers between devices: none -> 4.23 us  [local(): second = exchange(after(second, first).reshape(GRP, ROWS, PAIR))]
    unnamed x8 -> x12, local copies, waits for them, and re-layouts: 3.39 us -> 7.52 us
  transfers between devices with their start and end apart: 9 -> 10, of which waited for: 7 -> 8; matrix products, arithmetic and copies ran while one was open for 0% -> 0% of each run, Pallas kernels for 18% -> 19%
where the time goes in v8:
time: 172 us; the launch traced here: 171 us
  starting transfers between devices  51.9 us (30%)
  waiting for transfers between devices  40 us (23%)
  Pallas kernels  34.8 us (20%)
  blocking collectives  21.9 us (13%)
  between operations  13.5 us (8%)
  local copies, waits for them, and re-layouts  7.68 us (4%)
    all_gather x1, blocking collectives, local(): far = lax.all_gather(compact(got), 'y', axis=0, tiled=True)  21.9 us
    ppermute x4, starting transfers between devices, shift(): lax.ppermute(value, axis, [(i, (i + step) % size) for i in range(size)])  18.8 us
    pallas_call x2, Pallas kernels, dense_level(): pl.pallas_call(functools.partial(dense_kernel, pair), in_specs=[pl.BlockS...  17.5 us
    all_to_all x1, waiting for transfers between devices, local(): lax.all_to_all(after(small, far_rows).reshape(H * ZH, SENT, PAIR), ('zl',...  16.9 us
    all_to_all x1, starting transfers between devices, local(): lax.all_to_all(after(small, far_rows).reshape(H * ZH, SENT, PAIR), ('zl',...  13.2 us
    unnamed x12, local copies, waits for them, and re-layouts  7.52 us
    ppermute x4, waiting for transfers between devices, shift(): lax.ppermute(value, axis, [(i, (i + step) % size) for i in range(size)])  6.36 us
    pallas_call x1, Pallas kernels, pack(): pl.pallas_call(pack_kernel, grid=(GRP,), in_specs=[block] * 3, out_specs=...  6.01 us
  transfers between devices with their start and end apart: 10, of which 8 were waited for; matrix products, arithmetic and copies ran while one was open for 0% of the time, Pallas kernels for 19%

profile of v8, /device:TPU:1, one launch (start us, length us, event | category | flops | bytes accessed | tf_op | source)
XLA Modules:
  0.0 170.7 jit_solution(3716579960838661072)
XLA Ops:
  6.5 11.6 %collective-permute-start = (bf16[32,2048]{1,0:T(8,128)(2,1)}, bf16[32,2048]{1,0:T(8,128)(2,1)S(1)}, u32[]{:S(2)}, u32[]{:S(2)}) collective-permute-start(bf16[32,2048]{1,0:T(8,128)(2,1)} %param.11), channel_id=1, source_target_pairs={{0,4},{4,0},{1,5},{5,1},{2,6},{6,2},{3,7},{7,3},{8,12},{12,8},{9,1... | collective-permute-start | bytes 393224 | tf_op jit(solution)/shard_map/ppermute | solution.py:345
  18.1 3.6 %pick.1 = bf16[32,2,48,128]{3,2,1,0:T(8,128)(2,1)} custom-call(s32[32]{0:T(128)} %two_ref.1, s32[32]{0:T(128)} %three_ref.1, bf16[192,2048]{1,0:T(8,128)(2,1)} %q_ref.2, bf16[192,2048]{1,0:T(8,128)(2,1)} %k_ref.3, bf16[192,2048]{1,0:T(8,128)(2,1)} %v_ref.3), custom_call_target="tpu_custom_call" | custom-call | flops 1000000000 | bytes 4000000 | tf_op jit(solution)/shard_map/pick/pallas_call | solution.py:94
  21.7 0.6 collective-permute-done
  22.3 0.7 pad_maximum_fusion.1
  23.1 13.2 %all-to-all-start = ((bf16[64,48,128]{2,1,0:T(8,128)(2,1)}), bf16[64,48,128]{2,1,0:T(8,128)(2,1)S(1)}, u32[]{:S(2)}, u32[]{:S(2)}) async-start(bf16[64,48,128]{2,1,0:T(8,128)(2,1)} %bitcast.23), calls=%async_computation | async-start | bytes 1572864 | tf_op jit(solution)/shard_map/all_to_all | solution.py:364
  36.3 6.0 %pack.1 = (bf16[8,192,640]{2,1,0:T(8,128)(2,1)}, bf16[8,192,128]{2,1,0:T(8,128)(2,1)}) custom-call(bf16[192,2048]{1,0:T(8,128)(2,1)} %q_ref.2, bf16[192,2048]{1,0:T(8,128)(2,1)} %k_ref.3, bf16[192,2048]{1,0:T(8,128)(2,1)} %v_ref.3), custom_call_target="tpu_custom_call" | custom-call | bytes 5000000 | tf_op jit(solution)/shard_map/pack/pallas_call | solution.py:118
  42.3 16.9 %all-to-all-done = bf16[64,48,128]{2,1,0:T(8,128)(2,1)S(1)} async-done(((bf16[64,48,128]{2,1,0:T(8,128)(2,1)}), bf16[64,48,128]{2,1,0:T(8,128)(2,1)S(1)}, u32[]{:S(2)}, u32[]{:S(2)}) %all-to-all-start) | async-done | bytes 786464 | tf_op jit(solution)/shard_map/all_to_all | solution.py:364
  59.2 5.9 %all-to-all-start.1 = ((bf16[8,192,640]{2,1,0:T(8,128)(2,1)}), bf16[8,192,640]{2,1,0:T(8,128)(2,1)S(1)}, u32[]{:S(2)}, u32[]{:S(2)}) async-start(bf16[8,192,640]{2,1,0:T(8,128)(2,1)} %get-tuple-element.19), calls=%async_computation.1 | async-start | bytes 3932160 | tf_op jit(solution)/shard_map/all_to_all | solution.py:368
  65.3 0.1 pad_add_fusion.1.place_ref
  65.4 0.4 compact_three.1
  65.7 21.9 %all_gather.6.far_ref = bf16[1536,128]{1,0:T(8,128)(2,1)S(1)} all-gather(bf16[192,128]{1,0:T(8,128)(2,1)S(1)} %compact_three.1), channel_id=1, replica_groups=mesh['zl'=4,'core'=2,'y'=8,'zh'=2,'x'=4] {'y'}, dimensions={0}, use_global_device_ids=true | all-gather | bytes 442368 | tf_op jit(solution)/shard_map/all_gather | solution.py:369
  87.6 4.0 %sparse_levels.1 = bf16[4,8,32,128]{3,2,1,0:T(8,128)(2,1)S(1)} custom-call(s32[2]{0:T(128)S(1)} %pad_add_fusion.1.place_ref, bf16[32,2,48,128]{3,2,1,0:T(8,128)(2,1)S(1)} %bitcast.18, bf16[1536,128]{1,0:T(8,128)(2,1)S(1)} %all_gather.6.far_ref), custom_call_target="tpu_custom_call" | custom-call | flops 4000000000 | bytes 2000000 | tf_op jit(solution)/shard_map/sparse_levels/pallas_call | solution.py:191
  91.6 1.9 %collective-permute-start.3 = (bf16[8,32,128]{2,1,0:T(8,128)(2,1)S(1)}, bf16[8,32,128]{2,1,0:T(8,128)(2,1)S(1)}, u32[]{:S(2)}, u32[]{:S(2)}) collective-permute-start(bf16[8,32,128]{2,1,0:T(8,128)(2,1)S(1)} %get-tuple-element.28), channel_id=1, source_target_pairs={{0,3},{1,0},{2,1},{3,2},{4,7},{5,4},{6,5},{7,6},{8,11},{9,8},{10,9... | collective-permute-start | bytes 196616 | tf_op jit(solution)/shard_map/ppermute | solution.py:345
  93.6 2.1 %collective-permute-start.2 = (bf16[8,32,128]{2,1,0:T(8,128)(2,1)S(1)}, bf16[8,32,128]{2,1,0:T(8,128)(2,1)S(1)}, u32[]{:S(2)}, u32[]{:S(2)}) collective-permute-start(bf16[8,32,128]{2,1,0:T(8,128)(2,1)S(1)} %get-tuple-element.29), channel_id=1, source_target_pairs={{0,2},{1,3},{2,0},{3,1},{4,6},{5,7},{6,4},{7,5},{8,10},{9,11},{10,... | collective-permute-start | bytes 196616 | tf_op jit(solution)/shard_map/ppermute | solution.py:345
  95.7 3.1 %collective-permute-start.1 = (bf16[8,32,128]{2,1,0:T(8,128)(2,1)S(1)}, bf16[8,32,128]{2,1,0:T(8,128)(2,1)S(1)}, u32[]{:S(2)}, u32[]{:S(2)}) collective-permute-start(bf16[8,32,128]{2,1,0:T(8,128)(2,1)S(1)} %get-tuple-element.30), channel_id=1, source_target_pairs={{0,1},{1,2},{2,3},{3,0},{4,5},{5,6},{6,7},{7,4},{8,9},{9,10},{10,1... | collective-permute-start | bytes 196616 | tf_op jit(solution)/shard_map/ppermute | solution.py:345
  98.9 0.1 pad_add_fusion.scalar_ref
  98.9 2.6 %collective-permute-done.2 = bf16[8,32,128]{2,1,0:T(8,128)(2,1)S(1)} collective-permute-done((bf16[8,32,128]{2,1,0:T(8,128)(2,1)S(1)}, bf16[8,32,128]{2,1,0:T(8,128)(2,1)S(1)}, u32[]{:S(2)}, u32[]{:S(2)}) %collective-permute-start.2) | collective-permute-done | bytes 65568 | tf_op jit(solution)/shard_map/ppermute | solution.py:345
  101.5 3.2 %collective-permute-done.1 = bf16[8,32,128]{2,1,0:T(8,128)(2,1)S(1)} collective-permute-done((bf16[8,32,128]{2,1,0:T(8,128)(2,1)S(1)}, bf16[8,32,128]{2,1,0:T(8,128)(2,1)S(1)}, u32[]{:S(2)}, u32[]{:S(2)}) %collective-permute-start.1) | collective-permute-done | bytes 65568 | tf_op jit(solution)/shard_map/ppermute | solution.py:345
  104.7 6.0 %all-to-all-done.1 = bf16[8,192,640]{2,1,0:T(8,128)(2,1)S(1)} async-done(((bf16[8,192,640]{2,1,0:T(8,128)(2,1)}), bf16[8,192,640]{2,1,0:T(8,128)(2,1)S(1)}, u32[]{:S(2)}, u32[]{:S(2)}) %all-to-all-start.1) | async-done | bytes 1966112 | tf_op jit(solution)/shard_map/all_to_all | solution.py:368
  110.7 5.5 %all-to-all-start.2 = ((bf16[8,192,128]{2,1,0:T(8,128)(2,1)}), bf16[8,192,128]{2,1,0:T(8,128)(2,1)S(1)}, u32[]{:S(2)}, u32[]{:S(2)}) async-start(bf16[8,192,128]{2,1,0:T(8,128)(2,1)} %get-tuple-element.21), calls=%async_computation.2 | async-start | bytes 786432 | tf_op jit(solution)/shard_map/all_to_all | solution.py:372
  116.2 8.7 %dense_level.2 = bf16[1536,128]{1,0:T(8,128)(2,1)} custom-call(s32[9]{0:T(128)S(1)} %pad_add_fusion.scalar_ref, bf16[1536,640]{1,0:T(8,128)(2,1)S(1)} %bitcast.19, bf16[1536,640]{1,0:T(8,128)(2,1)S(1)} %bitcast.20, bf16[4,8,32,128]{3,2,1,0:T(8,128)(2,1)S(1)} %pad_maximum_fusion.back_ref), custom_call_target="tpu_custom_call" | custom-call | flops 10000000000 | bytes 2000000 | tf_op jit(solution)/shard_map/dense_level/pallas_call | solution.py:267
  124.9 3.0 %all-to-all-done.2 = bf16[8,192,128]{2,1,0:T(8,128)(2,1)S(1)} async-done(((bf16[8,192,128]{2,1,0:T(8,128)(2,1)}), bf16[8,192,128]{2,1,0:T(8,128)(2,1)S(1)}, u32[]{:S(2)}, u32[]{:S(2)}) %all-to-all-start.2) | async-done | bytes 393248 | tf_op jit(solution)/shard_map/all_to_all | solution.py:372
  127.9 4.2 %all-to-all-start.3 = ((bf16[8,192,128]{2,1,0:T(8,128)(2,1)}), bf16[8,192,128]{2,1,0:T(8,128)(2,1)S(1)}, u32[]{:S(2)}, u32[]{:S(2)}) async-start(bf16[8,192,128]{2,1,0:T(8,128)(2,1)} %bitcast.12), calls=%async_computation.3 | async-start | bytes 786432 | tf_op jit(solution)/shard_map/all_to_all | solution.py:375
  132.1 8.8 %dense_level.3 = bf16[1536,128]{1,0:T(8,128)(2,1)} custom-call(s32[9]{0:T(128)S(1)} %pad_add_fusion.scalar_ref, bf16[1536,128]{1,0:T(8,128)(2,1)S(1)} %bitcast.22, bf16[1536,640]{1,0:T(8,128)(2,1)S(1)} %bitcast.21, bf16[4,8,32,128]{3,2,1,0:T(8,128)(2,1)S(1)} %pad_maximum_fusion.back_ref), custom_call_target="tpu_custom_call" | custom-call | flops 10000000000 | bytes 2000000 | tf_op jit(solution)/shard_map/dense_level/pallas_call | solution.py:267
  140.9 2.9 %all-to-all-done.3.att_ref = bf16[8,192,128]{2,1,0:T(8,128)(2,1)S(1)} async-done(((bf16[8,192,128]{2,1,0:T(8,128)(2,1)}), bf16[8,192,128]{2,1,0:T(8,128)(2,1)S(1)}, u32[]{:S(2)}, u32[]{:S(2)}) %all-to-all-start.3) | async-done | bytes 393248 | tf_op jit(solution)/shard_map/all_to_all | solution.py:375
  143.8 4.2 %all-to-all-start.4 = ((bf16[8,192,128]{2,1,0:T(8,128)(2,1)}), bf16[8,192,128]{2,1,0:T(8,128)(2,1)S(1)}, u32[]{:S(2)}, u32[]{:S(2)}) async-start(bf16[8,192,128]{2,1,0:T(8,128)(2,1)} %bitcast.13), calls=%async_computation.4 | async-start | bytes 786432 | tf_op jit(solution)/shard_map/all_to_all | solution.py:377
  148.0 3.4 %copy-done = bf16[2048,2048]{1,0:T(8,128)(2,1)S(1)} copy-done((bf16[2048,2048]{1,0:T(8,128)(2,1)S(1)}, bf16[2048,2048]{1,0:T(8,128)(2,1)}, u32[]{:S(2)}) %copy-start) | copy-done | bytes 8388632
  151.4 1.5 project_first.1
  153.0 1.9 %copy-done.1 = bf16[1024,2048]{1,0:T(8,128)(2,1)} copy-done((bf16[1024,2048]{1,0:T(8,128)(2,1)}, bf16[1024,2048]{1,0:T(8,128)(2,1)S(1)}, u32[]{:S(2)}) %copy-start.1) | copy-done | bytes 4194328
  154.9 4.8 %all-to-all-done.4.att_ref = bf16[8,192,128]{2,1,0:T(8,128)(2,1)S(1)} async-done(((bf16[8,192,128]{2,1,0:T(8,128)(2,1)}), bf16[8,192,128]{2,1,0:T(8,128)(2,1)S(1)}, u32[]{:S(2)}, u32[]{:S(2)}) %all-to-all-start.4) | async-done | bytes 393248 | tf_op jit(solution)/shard_map/all_to_all | solution.py:377
  159.7 2.2 %copy-done.2 = bf16[1024,2048]{1,0:T(8,128)(2,1)S(1)} copy-done((bf16[1024,2048]{1,0:T(8,128)(2,1)S(1)}, bf16[1024,2048]{1,0:T(8,128)(2,1)}, u32[]{:S(2)}) %copy-start.2) | copy-done | bytes 4194328
  161.9 1.9 %project_second.1 = bf16[192,2048]{1,0:T(8,128)(2,1)} custom-call(f32[192,2048]{1,0:T(8,128)S(1)} %get-tuple-element.24.before_ref, bf16[8,192,128]{2,1,0:T(8,128)(2,1)S(1)} %all-to-all-done.4.att_ref, bf16[1024,2048]{1,0:T(8,128)(2,1)S(1)} %copy-done.2), custom_call_target="tpu_custom_call" | custom-call | flops 805306368 | bytes 6000000 | tf_op jit(solution)/shard_map/project_second/pallas_call | solution.py:332
  (17 shorter events, 0.2 us)
Async XLA Ops:
  6.5 15.8 %copy-start.3 = (bf16[32,2048]{1,0:T(8,128)(2,1)S(1)}, bf16[32,2048]{1,0:T(8,128)(2,1)}, u32[]{:S(2)}) copy-start(bf16[32,2048]{1,0:T(8,128)(2,1)} %param.11) | copy-start | bytes 393220
  6.5 141.5 %all-gather.2.cloned.1.call-start = ((), (), s32[]{:S(2)}) async-start(), calls=%async_computation.5 | async-start | bytes 8650752 | tf_op jit(solution)/shard_map/all_gather | solution.py:363
  6.5 15.8 %collective-permute-start = (bf16[32,2048]{1,0:T(8,128)(2,1)}, bf16[32,2048]{1,0:T(8,128)(2,1)S(1)}, u32[]{:S(2)}, u32[]{:S(2)}) collective-permute-start(bf16[32,2048]{1,0:T(8,128)(2,1)} %param.11), channel_id=1, source_target_pairs={{0,4},{4,0},{1,5},{5,1},{2,6},{6,2},{3,7},{7,3},{8,12},{12,8},{9,1... | collective-permute-start | bytes 393224 | tf_op jit(solution)/shard_map/ppermute | solution.py:345
  23.1 36.1 %all-to-all-start = ((bf16[64,48,128]{2,1,0:T(8,128)(2,1)}), bf16[64,48,128]{2,1,0:T(8,128)(2,1)S(1)}, u32[]{:S(2)}, u32[]{:S(2)}) async-start(bf16[64,48,128]{2,1,0:T(8,128)(2,1)} %bitcast.23), calls=%async_computation | async-start | bytes 1572864 | tf_op jit(solution)/shard_map/all_to_all | solution.py:364
  59.2 5.9 %copy-start.4 = (s32[32]{0:T(128)S(1)}, s32[32]{0:T(128)}, u32[]{:S(2)}) copy-start(s32[32]{0:T(128)} %two_ref.1) | copy-start | bytes 388
  59.2 6.0 %copy-start.5 = (s32[32]{0:T(128)S(1)}, s32[32]{0:T(128)}, u32[]{:S(2)}) copy-start(s32[32]{0:T(128)} %three_ref.1) | copy-start | bytes 388
  59.2 51.5 %all-to-all-start.1 = ((bf16[8,192,640]{2,1,0:T(8,128)(2,1)}), bf16[8,192,640]{2,1,0:T(8,128)(2,1)S(1)}, u32[]{:S(2)}, u32[]{:S(2)}) async-start(bf16[8,192,640]{2,1,0:T(8,128)(2,1)} %get-tuple-element.19), calls=%async_computation.1 | async-start | bytes 3932160 | tf_op jit(solution)/shard_map/all_to_all | solution.py:368
  91.6 7.3 %collective-permute-start.3 = (bf16[8,32,128]{2,1,0:T(8,128)(2,1)S(1)}, bf16[8,32,128]{2,1,0:T(8,128)(2,1)S(1)}, u32[]{:S(2)}, u32[]{:S(2)}) collective-permute-start(bf16[8,32,128]{2,1,0:T(8,128)(2,1)S(1)} %get-tuple-element.28), channel_id=1, source_target_pairs={{0,3},{1,0},{2,1},{3,2},{4,7},{5,4},{6,5},{7,6},{8,11},{9,8},{10,9... | collective-permute-start | bytes 196616 | tf_op jit(solution)/shard_map/ppermute | solution.py:345
  93.6 7.9 %collective-permute-start.2 = (bf16[8,32,128]{2,1,0:T(8,128)(2,1)S(1)}, bf16[8,32,128]{2,1,0:T(8,128)(2,1)S(1)}, u32[]{:S(2)}, u32[]{:S(2)}) collective-permute-start(bf16[8,32,128]{2,1,0:T(8,128)(2,1)S(1)} %get-tuple-element.29), channel_id=1, source_target_pairs={{0,2},{1,3},{2,0},{3,1},{4,6},{5,7},{6,4},{7,5},{8,10},{9,11},{10,... | collective-permute-start | bytes 196616 | tf_op jit(solution)/shard_map/ppermute | solution.py:345
  95.7 8.9 %collective-permute-start.1 = (bf16[8,32,128]{2,1,0:T(8,128)(2,1)S(1)}, bf16[8,32,128]{2,1,0:T(8,128)(2,1)S(1)}, u32[]{:S(2)}, u32[]{:S(2)}) collective-permute-start(bf16[8,32,128]{2,1,0:T(8,128)(2,1)S(1)} %get-tuple-element.30), channel_id=1, source_target_pairs={{0,1},{1,2},{2,3},{3,0},{4,5},{5,6},{6,7},{7,4},{8,9},{9,10},{10,1... | collective-permute-start | bytes 196616 | tf_op jit(solution)/shard_map/ppermute | solution.py:345
  110.7 17.2 %all-to-all-start.2 = ((bf16[8,192,128]{2,1,0:T(8,128)(2,1)}), bf16[8,192,128]{2,1,0:T(8,128)(2,1)S(1)}, u32[]{:S(2)}, u32[]{:S(2)}) async-start(bf16[8,192,128]{2,1,0:T(8,128)(2,1)} %get-tuple-element.21), calls=%async_computation.2 | async-start | bytes 786432 | tf_op jit(solution)/shard_map/all_to_all | solution.py:372
  127.9 15.9 %all-to-all-start.3 = ((bf16[8,192,128]{2,1,0:T(8,128)(2,1)}), bf16[8,192,128]{2,1,0:T(8,128)(2,1)S(1)}, u32[]{:S(2)}, u32[]{:S(2)}) async-start(bf16[8,192,128]{2,1,0:T(8,128)(2,1)} %bitcast.12), calls=%async_computation.3 | async-start | bytes 786432 | tf_op jit(solution)/shard_map/all_to_all | solution.py:375
  143.8 15.9 %all-to-all-start.4 = ((bf16[8,192,128]{2,1,0:T(8,128)(2,1)}), bf16[8,192,128]{2,1,0:T(8,128)(2,1)S(1)}, u32[]{:S(2)}, u32[]{:S(2)}) async-start(bf16[8,192,128]{2,1,0:T(8,128)(2,1)} %bitcast.13), calls=%async_computation.4 | async-start | bytes 786432 | tf_op jit(solution)/shard_map/all_to_all | solution.py:377
  148.0 3.4 %copy-start = (bf16[2048,2048]{1,0:T(8,128)(2,1)S(1)}, bf16[2048,2048]{1,0:T(8,128)(2,1)}, u32[]{:S(2)}) copy-start(bf16[2048,2048]{1,0:T(8,128)(2,1)} %all-gather.2.cloned.1.call-done.w_ref) | copy-start | bytes 25165828
  153.0 1.9 %copy-start.1 = (bf16[1024,2048]{1,0:T(8,128)(2,1)}, bf16[1024,2048]{1,0:T(8,128)(2,1)S(1)}, u32[]{:S(2)}) copy-start(bf16[1024,2048]{1,0:T(8,128)(2,1)S(1)} %get-tuple-element.26.w_ref) | copy-start | bytes 12582916
  159.7 2.2 %copy-start.2 = (bf16[1024,2048]{1,0:T(8,128)(2,1)S(1)}, bf16[1024,2048]{1,0:T(8,128)(2,1)}, u32[]{:S(2)}) copy-start(bf16[1024,2048]{1,0:T(8,128)(2,1)} %copy-done.1) | copy-start | bytes 12582916
Sparse Core Ops, SparseCore 0:
  23.2 109.5 all-gather.1

commit v9 on v8

--- a/solution.py
+++ b/solution.py
@@ -319,22 +319,36 @@
     )(zh, att, weights)
 
 
-def project_second_kernel(before_ref, att_ref, w_ref, out_ref):
+def project_second_kernel(before_ref, att_ref, w_ref, out_ref, total):
+    step = pl.program_id(0)
+
+    @pl.when(step == 0)
+    def _():
+        total[...] = before_ref[...]
+
+    att = jnp.concatenate([att_ref[0], att_ref[1]], 1)
     for start in range(0, D, COLUMNS):
         lanes = slice(start, start + COLUMNS)
-        total = before_ref[:, lanes]
-        for first, att in pairs_of_groups(att_ref):
-            total += jnp.dot(att, w_ref[first * PAIR : (first + 2) * PAIR, lanes], preferred_element_type=F32)
-        out_ref[:, lanes] = total.astype(BF16)
+        total[:, lanes] += jnp.dot(att, w_ref[:, lanes], preferred_element_type=F32)
+
+    @pl.when(step == pl.num_programs(0) - 1)
+    def _():
+        out_ref[...] = total[...].astype(BF16)
 
 
 def project_second(before, att, weights):
     return pl.pallas_call(
         project_second_kernel,
-        in_specs=[pl.BlockSpec(memory_space=pltpu.VMEM)] * 3,
-        out_specs=pl.BlockSpec(memory_space=pltpu.VMEM),
+        grid=(GRP // 2,),
+        in_specs=[
+            pl.BlockSpec((ROWS, D), lambda j: (0, 0)),
+            pl.BlockSpec((2, ROWS, PAIR), lambda j: (j, 0, 0)),
+            pl.BlockSpec((2 * PAIR, D), lambda j: (j, 0)),
+        ],
+        out_specs=pl.BlockSpec((ROWS, D), lambda j: (0, 0)),
         out_shape=jax.ShapeDtypeStruct((ROWS, D), BF16),
-        compiler_params=params(),
+        scratch_shapes=[pltpu.VMEM((ROWS, D), F32)],
+        compiler_params=pltpu.CompilerParams(vmem_limit_bytes=56 * 2**20),
         cost_estimate=cost(ROWS * D * D, 6 * 10**6),
         name="project_second",
     )(before, att, weights)

time: 172 us -> 174 us (1.012)
  Pallas kernels: 34.8 us -> 38.2 us
    pallas_call x1, Pallas kernels: 1.87 us -> 5.37 us  [project_second(): pl.pallas_call(project_second_kernel, grid=(GRP // 2,), in_specs=[pl.Bloc...]
    unnamed x12 -> x14, local copies, waits for them, and re-layouts: 7.52 us -> 7.28 us
where the time goes in v9:
time: 174 us; the launch traced here: 173 us
  starting transfers between devices  51.9 us (30%)
  waiting for transfers between devices  38.8 us (22%)
  Pallas kernels  38.2 us (22%)
  blocking collectives  21.9 us (13%)
  between operations  13.5 us (8%)
  local copies, waits for them, and re-layouts  7.45 us (4%)
    all_gather x1, blocking collectives, local(): far = lax.all_gather(compact(got), 'y', axis=0, tiled=True)  21.9 us
    ppermute x4, starting transfers between devices, shift(): lax.ppermute(value, axis, [(i, (i + step) % size) for i in range(size)])  18.8 us
    pallas_call x2, Pallas kernels, dense_level(): pl.pallas_call(functools.partial(dense_kernel, pair), in_specs=[pl.BlockS...  17.5 us
    all_to_all x1, waiting for transfers between devices, local(): lax.all_to_all(after(small, far_rows).reshape(H * ZH, SENT, PAIR), ('zl',...  16.9 us
    all_to_all x1, starting transfers between devices, local(): lax.all_to_all(after(small, far_rows).reshape(H * ZH, SENT, PAIR), ('zl',...  13.2 us
    unnamed x14, local copies, waits for them, and re-layouts  7.28 us
    ppermute x4, waiting for transfers between devices, shift(): lax.ppermute(value, axis, [(i, (i + step) % size) for i in range(size)])  6.36 us
    pallas_call x1, Pallas kernels, pack(): pl.pallas_call(pack_kernel, grid=(GRP,), in_specs=[block] * 3, out_specs=...  5.97 us
  transfers between devices with their start and end apart: 10, of which 8 were waited for; matrix products, arithmetic and copies ran while one was open for 0% of the time, Pallas kernels for 19%

profile of v9, /device:TPU:1, one launch (start us, length us, event | category | flops | bytes accessed | tf_op | source)
XLA Modules:
  0.0 172.7 jit_solution(8593446034605080797)
XLA Ops:
  6.5 11.6 %collective-permute-start = (bf16[32,2048]{1,0:T(8,128)(2,1)}, bf16[32,2048]{1,0:T(8,128)(2,1)S(1)}, u32[]{:S(2)}, u32[]{:S(2)}) collective-permute-start(bf16[32,2048]{1,0:T(8,128)(2,1)} %param.11), channel_id=1, source_target_pairs={{0,4},{4,0},{1,5},{5,1},{2,6},{6,2},{3,7},{7,3},{8,12},{12,8},{9,1... | collective-permute-start | bytes 393224 | tf_op jit(solution)/shard_map/ppermute | solution.py:359
  18.1 3.6 %pick.1 = bf16[32,2,48,128]{3,2,1,0:T(8,128)(2,1)} custom-call(s32[32]{0:T(128)} %two_ref.1, s32[32]{0:T(128)} %three_ref.1, bf16[192,2048]{1,0:T(8,128)(2,1)} %q_ref.2, bf16[192,2048]{1,0:T(8,128)(2,1)} %k_ref.3, bf16[192,2048]{1,0:T(8,128)(2,1)} %v_ref.3), custom_call_target="tpu_custom_call" | custom-call | flops 1000000000 | bytes 4000000 | tf_op jit(solution)/shard_map/pick/pallas_call | solution.py:94
  21.7 0.6 collective-permute-done
  22.3 0.7 pad_maximum_fusion.1
  23.1 13.2 %all-to-all-start = ((bf16[64,48,128]{2,1,0:T(8,128)(2,1)}), bf16[64,48,128]{2,1,0:T(8,128)(2,1)S(1)}, u32[]{:S(2)}, u32[]{:S(2)}) async-start(bf16[64,48,128]{2,1,0:T(8,128)(2,1)} %bitcast.23), calls=%async_computation | async-start | bytes 1572864 | tf_op jit(solution)/shard_map/all_to_all | solution.py:378
  36.3 6.0 %pack.1 = (bf16[8,192,640]{2,1,0:T(8,128)(2,1)}, bf16[8,192,128]{2,1,0:T(8,128)(2,1)}) custom-call(bf16[192,2048]{1,0:T(8,128)(2,1)} %q_ref.2, bf16[192,2048]{1,0:T(8,128)(2,1)} %k_ref.3, bf16[192,2048]{1,0:T(8,128)(2,1)} %v_ref.3), custom_call_target="tpu_custom_call" | custom-call | bytes 5000000 | tf_op jit(solution)/shard_map/pack/pallas_call | solution.py:118
  42.3 16.9 %all-to-all-done = bf16[64,48,128]{2,1,0:T(8,128)(2,1)S(1)} async-done(((bf16[64,48,128]{2,1,0:T(8,128)(2,1)}), bf16[64,48,128]{2,1,0:T(8,128)(2,1)S(1)}, u32[]{:S(2)}, u32[]{:S(2)}) %all-to-all-start) | async-done | bytes 786464 | tf_op jit(solution)/shard_map/all_to_all | solution.py:378
  59.2 5.9 %all-to-all-start.1 = ((bf16[8,192,640]{2,1,0:T(8,128)(2,1)}), bf16[8,192,640]{2,1,0:T(8,128)(2,1)S(1)}, u32[]{:S(2)}, u32[]{:S(2)}) async-start(bf16[8,192,640]{2,1,0:T(8,128)(2,1)} %get-tuple-element.19), calls=%async_computation.1 | async-start | bytes 3932160 | tf_op jit(solution)/shard_map/all_to_all | solution.py:382
  65.4 0.4 compact_three.1
  65.8 21.9 %all_gather.6.far_ref = bf16[1536,128]{1,0:T(8,128)(2,1)S(1)} all-gather(bf16[192,128]{1,0:T(8,128)(2,1)S(1)} %compact_three.1), channel_id=1, replica_groups=mesh['zl'=4,'core'=2,'y'=8,'zh'=2,'x'=4] {'y'}, dimensions={0}, use_global_device_ids=true | all-gather | bytes 442368 | tf_op jit(solution)/shard_map/all_gather | solution.py:383
  87.7 4.0 %sparse_levels.1 = bf16[4,8,32,128]{3,2,1,0:T(8,128)(2,1)S(1)} custom-call(s32[2]{0:T(128)S(1)} %pad_add_fusion.1.place_ref, bf16[32,2,48,128]{3,2,1,0:T(8,128)(2,1)S(1)} %bitcast.18, bf16[1536,128]{1,0:T(8,128)(2,1)S(1)} %all_gather.6.far_ref), custom_call_target="tpu_custom_call" | custom-call | flops 4000000000 | bytes 2000000 | tf_op jit(solution)/shard_map/sparse_levels/pallas_call | solution.py:191
  91.7 1.9 %collective-permute-start.3 = (bf16[8,32,128]{2,1,0:T(8,128)(2,1)S(1)}, bf16[8,32,128]{2,1,0:T(8,128)(2,1)S(1)}, u32[]{:S(2)}, u32[]{:S(2)}) collective-permute-start(bf16[8,32,128]{2,1,0:T(8,128)(2,1)S(1)} %get-tuple-element.28), channel_id=1, source_target_pairs={{0,3},{1,0},{2,1},{3,2},{4,7},{5,4},{6,5},{7,6},{8,11},{9,8},{10,9... | collective-permute-start | bytes 196616 | tf_op jit(solution)/shard_map/ppermute | solution.py:359
  93.6 2.1 %collective-permute-start.2 = (bf16[8,32,128]{2,1,0:T(8,128)(2,1)S(1)}, bf16[8,32,128]{2,1,0:T(8,128)(2,1)S(1)}, u32[]{:S(2)}, u32[]{:S(2)}) collective-permute-start(bf16[8,32,128]{2,1,0:T(8,128)(2,1)S(1)} %get-tuple-element.29), channel_id=1, source_target_pairs={{0,2},{1,3},{2,0},{3,1},{4,6},{5,7},{6,4},{7,5},{8,10},{9,11},{10,... | collective-permute-start | bytes 196616 | tf_op jit(solution)/shard_map/ppermute | solution.py:359
  95.7 3.1 %collective-permute-start.1 = (bf16[8,32,128]{2,1,0:T(8,128)(2,1)S(1)}, bf16[8,32,128]{2,1,0:T(8,128)(2,1)S(1)}, u32[]{:S(2)}, u32[]{:S(2)}) collective-permute-start(bf16[8,32,128]{2,1,0:T(8,128)(2,1)S(1)} %get-tuple-element.30), channel_id=1, source_target_pairs={{0,1},{1,2},{2,3},{3,0},{4,5},{5,6},{6,7},{7,4},{8,9},{9,10},{10,1... | collective-permute-start | bytes 196616 | tf_op jit(solution)/shard_map/ppermute | solution.py:359
  98.9 0.1 pad_add_fusion.scalar_ref
  99.0 2.6 %collective-permute-done.2 = bf16[8,32,128]{2,1,0:T(8,128)(2,1)S(1)} collective-permute-done((bf16[8,32,128]{2,1,0:T(8,128)(2,1)S(1)}, bf16[8,32,128]{2,1,0:T(8,128)(2,1)S(1)}, u32[]{:S(2)}, u32[]{:S(2)}) %collective-permute-start.2) | collective-permute-done | bytes 65568 | tf_op jit(solution)/shard_map/ppermute | solution.py:359
  101.5 3.2 %collective-permute-done.1 = bf16[8,32,128]{2,1,0:T(8,128)(2,1)S(1)} collective-permute-done((bf16[8,32,128]{2,1,0:T(8,128)(2,1)S(1)}, bf16[8,32,128]{2,1,0:T(8,128)(2,1)S(1)}, u32[]{:S(2)}, u32[]{:S(2)}) %collective-permute-start.1) | collective-permute-done | bytes 65568 | tf_op jit(solution)/shard_map/ppermute | solution.py:359
  104.7 6.0 %all-to-all-done.1 = bf16[8,192,640]{2,1,0:T(8,128)(2,1)S(1)} async-done(((bf16[8,192,640]{2,1,0:T(8,128)(2,1)}), bf16[8,192,640]{2,1,0:T(8,128)(2,1)S(1)}, u32[]{:S(2)}, u32[]{:S(2)}) %all-to-all-start.1) | async-done | bytes 1966112 | tf_op jit(solution)/shard_map/all_to_all | solution.py:382
  110.7 5.5 %all-to-all-start.2 = ((bf16[8,192,128]{2,1,0:T(8,128)(2,1)}), bf16[8,192,128]{2,1,0:T(8,128)(2,1)S(1)}, u32[]{:S(2)}, u32[]{:S(2)}) async-start(bf16[8,192,128]{2,1,0:T(8,128)(2,1)} %get-tuple-element.21), calls=%async_computation.2 | async-start | bytes 786432 | tf_op jit(solution)/shard_map/all_to_all | solution.py:386
  116.2 8.7 %dense_level.2 = bf16[1536,128]{1,0:T(8,128)(2,1)} custom-call(s32[9]{0:T(128)S(1)} %pad_add_fusion.scalar_ref, bf16[1536,640]{1,0:T(8,128)(2,1)S(1)} %bitcast.19, bf16[1536,640]{1,0:T(8,128)(2,1)S(1)} %bitcast.20, bf16[4,8,32,128]{3,2,1,0:T(8,128)(2,1)S(1)} %pad_maximum_fusion.back_ref), custom_call_target="tpu_custom_call" | custom-call | flops 10000000000 | bytes 2000000 | tf_op jit(solution)/shard_map/dense_level/pallas_call | solution.py:267
  124.9 3.0 %all-to-all-done.2 = bf16[8,192,128]{2,1,0:T(8,128)(2,1)S(1)} async-done(((bf16[8,192,128]{2,1,0:T(8,128)(2,1)}), bf16[8,192,128]{2,1,0:T(8,128)(2,1)S(1)}, u32[]{:S(2)}, u32[]{:S(2)}) %all-to-all-start.2) | async-done | bytes 393248 | tf_op jit(solution)/shard_map/all_to_all | solution.py:386
  127.9 4.2 %all-to-all-start.3 = ((bf16[8,192,128]{2,1,0:T(8,128)(2,1)}), bf16[8,192,128]{2,1,0:T(8,128)(2,1)S(1)}, u32[]{:S(2)}, u32[]{:S(2)}) async-start(bf16[8,192,128]{2,1,0:T(8,128)(2,1)} %bitcast.12), calls=%async_computation.3 | async-start | bytes 786432 | tf_op jit(solution)/shard_map/all_to_all | solution.py:389
  132.1 8.8 %dense_level.3 = bf16[1536,128]{1,0:T(8,128)(2,1)} custom-call(s32[9]{0:T(128)S(1)} %pad_add_fusion.scalar_ref, bf16[1536,128]{1,0:T(8,128)(2,1)S(1)} %bitcast.22, bf16[1536,640]{1,0:T(8,128)(2,1)S(1)} %bitcast.21, bf16[4,8,32,128]{3,2,1,0:T(8,128)(2,1)S(1)} %pad_maximum_fusion.back_ref), custom_call_target="tpu_custom_call" | custom-call | flops 10000000000 | bytes 2000000 | tf_op jit(solution)/shard_map/dense_level/pallas_call | solution.py:267
  140.9 2.9 %all-to-all-done.3.att_ref = bf16[8,192,128]{2,1,0:T(8,128)(2,1)S(1)} async-done(((bf16[8,192,128]{2,1,0:T(8,128)(2,1)}), bf16[8,192,128]{2,1,0:T(8,128)(2,1)S(1)}, u32[]{:S(2)}, u32[]{:S(2)}) %all-to-all-start.3) | async-done | bytes 393248 | tf_op jit(solution)/shard_map/all_to_all | solution.py:389
  143.8 4.2 %all-to-all-start.4 = ((bf16[8,192,128]{2,1,0:T(8,128)(2,1)}), bf16[8,192,128]{2,1,0:T(8,128)(2,1)S(1)}, u32[]{:S(2)}, u32[]{:S(2)}) async-start(bf16[8,192,128]{2,1,0:T(8,128)(2,1)} %bitcast.13), calls=%async_computation.4 | async-start | bytes 786432 | tf_op jit(solution)/shard_map/all_to_all | solution.py:391
  148.1 3.4 %copy-done = bf16[2048,2048]{1,0:T(8,128)(2,1)S(1)} copy-done((bf16[2048,2048]{1,0:T(8,128)(2,1)S(1)}, bf16[2048,2048]{1,0:T(8,128)(2,1)}, u32[]{:S(2)}) %copy-start) | copy-done | bytes 8388632
  151.4 1.5 project_first.1
  153.0 1.9 %copy-done.1 = bf16[1024,2048]{1,0:T(8,128)(2,1)} copy-done((bf16[1024,2048]{1,0:T(8,128)(2,1)}, bf16[1024,2048]{1,0:T(8,128)(2,1)S(1)}, u32[]{:S(2)}) %copy-start.1) | copy-done | bytes 4194328
  154.9 1.2 copy-done.2
  156.1 3.7 %all-to-all-done.4.att_ref = bf16[8,192,128]{2,1,0:T(8,128)(2,1)S(1)} async-done(((bf16[8,192,128]{2,1,0:T(8,128)(2,1)}), bf16[8,192,128]{2,1,0:T(8,128)(2,1)S(1)}, u32[]{:S(2)}, u32[]{:S(2)}) %all-to-all-start.4) | async-done | bytes 393248 | tf_op jit(solution)/shard_map/all_to_all | solution.py:391
  159.8 0.8 copy-done.3
  160.5 5.4 %project_second.1 = bf16[192,2048]{1,0:T(8,128)(2,1)} custom-call(f32[192,2048]{1,0:T(8,128)} %copy-done.2, bf16[8,192,128]{2,1,0:T(8,128)(2,1)} %copy-done.3, bf16[1024,2048]{1,0:T(8,128)(2,1)} %copy-done.1), custom_call_target="tpu_custom_call" | custom-call | flops 805306368 | bytes 6000000 | tf_op jit(solution)/shard_map/project_second/pallas_call | solution.py:340
  (19 shorter events, 0.3 us)
Async XLA Ops:
  6.5 15.8 %copy-start.4 = (bf16[32,2048]{1,0:T(8,128)(2,1)S(1)}, bf16[32,2048]{1,0:T(8,128)(2,1)}, u32[]{:S(2)}) copy-start(bf16[32,2048]{1,0:T(8,128)(2,1)} %param.11) | copy-start | bytes 393220
  6.5 141.5 %all-gather.2.cloned.1.call-start = ((), (), s32[]{:S(2)}) async-start(), calls=%async_computation.5 | async-start | bytes 8650752 | tf_op jit(solution)/shard_map/all_gather | solution.py:377
  6.5 15.8 %collective-permute-start = (bf16[32,2048]{1,0:T(8,128)(2,1)}, bf16[32,2048]{1,0:T(8,128)(2,1)S(1)}, u32[]{:S(2)}, u32[]{:S(2)}) collective-permute-start(bf16[32,2048]{1,0:T(8,128)(2,1)} %param.11), channel_id=1, source_target_pairs={{0,4},{4,0},{1,5},{5,1},{2,6},{6,2},{3,7},{7,3},{8,12},{12,8},{9,1... | collective-permute-start | bytes 393224 | tf_op jit(solution)/shard_map/ppermute | solution.py:359
  23.1 36.1 %all-to-all-start = ((bf16[64,48,128]{2,1,0:T(8,128)(2,1)}), bf16[64,48,128]{2,1,0:T(8,128)(2,1)S(1)}, u32[]{:S(2)}, u32[]{:S(2)}) async-start(bf16[64,48,128]{2,1,0:T(8,128)(2,1)} %bitcast.23), calls=%async_computation | async-start | bytes 1572864 | tf_op jit(solution)/shard_map/all_to_all | solution.py:378
  59.2 5.9 %copy-start.5 = (s32[32]{0:T(128)S(1)}, s32[32]{0:T(128)}, u32[]{:S(2)}) copy-start(s32[32]{0:T(128)} %two_ref.1) | copy-start | bytes 388
  59.2 6.0 %copy-start.6 = (s32[32]{0:T(128)S(1)}, s32[32]{0:T(128)}, u32[]{:S(2)}) copy-start(s32[32]{0:T(128)} %three_ref.1) | copy-start | bytes 388
  59.2 51.5 %all-to-all-start.1 = ((bf16[8,192,640]{2,1,0:T(8,128)(2,1)}), bf16[8,192,640]{2,1,0:T(8,128)(2,1)S(1)}, u32[]{:S(2)}, u32[]{:S(2)}) async-start(bf16[8,192,640]{2,1,0:T(8,128)(2,1)} %get-tuple-element.19), calls=%async_computation.1 | async-start | bytes 3932160 | tf_op jit(solution)/shard_map/all_to_all | solution.py:382
  91.7 7.3 %collective-permute-start.3 = (bf16[8,32,128]{2,1,0:T(8,128)(2,1)S(1)}, bf16[8,32,128]{2,1,0:T(8,128)(2,1)S(1)}, u32[]{:S(2)}, u32[]{:S(2)}) collective-permute-start(bf16[8,32,128]{2,1,0:T(8,128)(2,1)S(1)} %get-tuple-element.28), channel_id=1, source_target_pairs={{0,3},{1,0},{2,1},{3,2},{4,7},{5,4},{6,5},{7,6},{8,11},{9,8},{10,9... | collective-permute-start | bytes 196616 | tf_op jit(solution)/shard_map/ppermute | solution.py:359
  93.6 7.9 %collective-permute-start.2 = (bf16[8,32,128]{2,1,0:T(8,128)(2,1)S(1)}, bf16[8,32,128]{2,1,0:T(8,128)(2,1)S(1)}, u32[]{:S(2)}, u32[]{:S(2)}) collective-permute-start(bf16[8,32,128]{2,1,0:T(8,128)(2,1)S(1)} %get-tuple-element.29), channel_id=1, source_target_pairs={{0,2},{1,3},{2,0},{3,1},{4,6},{5,7},{6,4},{7,5},{8,10},{9,11},{10,... | collective-permute-start | bytes 196616 | tf_op jit(solution)/shard_map/ppermute | solution.py:359
  95.7 8.9 %collective-permute-start.1 = (bf16[8,32,128]{2,1,0:T(8,128)(2,1)S(1)}, bf16[8,32,128]{2,1,0:T(8,128)(2,1)S(1)}, u32[]{:S(2)}, u32[]{:S(2)}) collective-permute-start(bf16[8,32,128]{2,1,0:T(8,128)(2,1)S(1)} %get-tuple-element.30), channel_id=1, source_target_pairs={{0,1},{1,2},{2,3},{3,0},{4,5},{5,6},{6,7},{7,4},{8,9},{9,10},{10,1... | collective-permute-start | bytes 196616 | tf_op jit(solution)/shard_map/ppermute | solution.py:359
  110.7 17.2 %all-to-all-start.2 = ((bf16[8,192,128]{2,1,0:T(8,128)(2,1)}), bf16[8,192,128]{2,1,0:T(8,128)(2,1)S(1)}, u32[]{:S(2)}, u32[]{:S(2)}) async-start(bf16[8,192,128]{2,1,0:T(8,128)(2,1)} %get-tuple-element.21), calls=%async_computation.2 | async-start | bytes 786432 | tf_op jit(solution)/shard_map/all_to_all | solution.py:386
  127.9 15.9 %all-to-all-start.3 = ((bf16[8,192,128]{2,1,0:T(8,128)(2,1)}), bf16[8,192,128]{2,1,0:T(8,128)(2,1)S(1)}, u32[]{:S(2)}, u32[]{:S(2)}) async-start(bf16[8,192,128]{2,1,0:T(8,128)(2,1)} %bitcast.12), calls=%async_computation.3 | async-start | bytes 786432 | tf_op jit(solution)/shard_map/all_to_all | solution.py:389
  143.8 15.9 %all-to-all-start.4 = ((bf16[8,192,128]{2,1,0:T(8,128)(2,1)}), bf16[8,192,128]{2,1,0:T(8,128)(2,1)S(1)}, u32[]{:S(2)}, u32[]{:S(2)}) async-start(bf16[8,192,128]{2,1,0:T(8,128)(2,1)} %bitcast.13), calls=%async_computation.4 | async-start | bytes 786432 | tf_op jit(solution)/shard_map/all_to_all | solution.py:391
  148.1 3.4 %copy-start = (bf16[2048,2048]{1,0:T(8,128)(2,1)S(1)}, bf16[2048,2048]{1,0:T(8,128)(2,1)}, u32[]{:S(2)}) copy-start(bf16[2048,2048]{1,0:T(8,128)(2,1)} %all-gather.2.cloned.1.call-done.w_ref) | copy-start | bytes 25165828
  153.0 1.9 %copy-start.1 = (bf16[1024,2048]{1,0:T(8,128)(2,1)}, bf16[1024,2048]{1,0:T(8,128)(2,1)S(1)}, u32[]{:S(2)}) copy-start(bf16[1024,2048]{1,0:T(8,128)(2,1)S(1)} %get-tuple-element.26.w_ref) | copy-start | bytes 12582916
  154.9 1.2 copy-start.2
  159.8 0.8 copy-start.3
Sparse Core Ops, SparseCore 0:
  23.2 109.5 all-gather.1

commit v10 on v8

--- a/solution.py
+++ b/solution.py
@@ -320,21 +320,25 @@
 
 
 def project_second_kernel(before_ref, att_ref, w_ref, out_ref):
-    for start in range(0, D, COLUMNS):
-        lanes = slice(start, start + COLUMNS)
-        total = before_ref[:, lanes]
-        for first, att in pairs_of_groups(att_ref):
-            total += jnp.dot(att, w_ref[first * PAIR : (first + 2) * PAIR, lanes], preferred_element_type=F32)
-        out_ref[:, lanes] = total.astype(BF16)
+    total = before_ref[...]
+    for first, att in pairs_of_groups(att_ref):
+        total += jnp.dot(att, w_ref[first * PAIR : (first + 2) * PAIR, :], preferred_element_type=F32)
+    out_ref[...] = total.astype(BF16)
 
 
 def project_second(before, att, weights):
+    columns = pl.BlockSpec((ROWS, COLUMNS), lambda j: (0, j))
     return pl.pallas_call(
         project_second_kernel,
-        in_specs=[pl.BlockSpec(memory_space=pltpu.VMEM)] * 3,
-        out_specs=pl.BlockSpec(memory_space=pltpu.VMEM),
+        grid=(D // COLUMNS,),
+        in_specs=[
+            columns,
+            pl.BlockSpec((GRP, ROWS, PAIR), lambda j: (0, 0, 0)),
+            pl.BlockSpec((D // 2, COLUMNS), lambda j: (0, j)),
+        ],
+        out_specs=columns,
         out_shape=jax.ShapeDtypeStruct((ROWS, D), BF16),
-        compiler_params=params(),
+        compiler_params=pltpu.CompilerParams(vmem_limit_bytes=56 * 2**20),
         cost_estimate=cost(ROWS * D * D, 6 * 10**6),
         name="project_second",
     )(before, att, weights)

time: 172 us -> 173 us (level)
  Pallas kernels: 34.8 us -> 37.9 us
    pallas_call x1, Pallas kernels: 1.87 us -> 5.01 us  [project_second(): pl.pallas_call(project_second_kernel, grid=(D // COLUMNS,), in_specs=[col...]
    unnamed x12 -> x14, local copies, waits for them, and re-layouts: 7.52 us -> 7.28 us
where the time goes in v10:
time: 173 us; the launch traced here: 172 us
  starting transfers between devices  51.9 us (30%)
  waiting for transfers between devices  38.8 us (22%)
  Pallas kernels  37.9 us (22%)
  blocking collectives  21.9 us (13%)
  between operations  13.5 us (8%)
  local copies, waits for them, and re-layouts  7.45 us (4%)
    all_gather x1, blocking collectives, local(): far = lax.all_gather(compact(got), 'y', axis=0, tiled=True)  21.9 us
    ppermute x4, starting transfers between devices, shift(): lax.ppermute(value, axis, [(i, (i + step) % size) for i in range(size)])  18.8 us
    pallas_call x2, Pallas kernels, dense_level(): pl.pallas_call(functools.partial(dense_kernel, pair), in_specs=[pl.BlockS...  17.5 us
    all_to_all x1, waiting for transfers between devices, local(): lax.all_to_all(after(small, far_rows).reshape(H * ZH, SENT, PAIR), ('zl',...  16.9 us
    all_to_all x1, starting transfers between devices, local(): lax.all_to_all(after(small, far_rows).reshape(H * ZH, SENT, PAIR), ('zl',...  13.2 us
    unnamed x14, local copies, waits for them, and re-layouts  7.28 us
    ppermute x4, waiting for transfers between devices, shift(): lax.ppermute(value, axis, [(i, (i + step) % size) for i in range(size)])  6.36 us
    pallas_call x1, Pallas kernels, pack(): pl.pallas_call(pack_kernel, grid=(GRP,), in_specs=[block] * 3, out_specs=...  5.97 us
  transfers between devices with their start and end apart: 10, of which 8 were waited for; matrix products, arithmetic and copies ran while one was open for 0% of the time, Pallas kernels for 19%

profile of v10, /device:TPU:1, one launch (start us, length us, event | category | flops | bytes accessed | tf_op | source)
XLA Modules:
  0.0 172.4 jit_solution(7030835282295227764)
XLA Ops:
  6.5 11.6 %collective-permute-start = (bf16[32,2048]{1,0:T(8,128)(2,1)}, bf16[32,2048]{1,0:T(8,128)(2,1)S(1)}, u32[]{:S(2)}, u32[]{:S(2)}) collective-permute-start(bf16[32,2048]{1,0:T(8,128)(2,1)} %param.11), channel_id=1, source_target_pairs={{0,4},{4,0},{1,5},{5,1},{2,6},{6,2},{3,7},{7,3},{8,12},{12,8},{9,1... | collective-permute-start | bytes 393224 | tf_op jit(solution)/shard_map/ppermute | solution.py:349
  18.1 3.6 %pick.1 = bf16[32,2,48,128]{3,2,1,0:T(8,128)(2,1)} custom-call(s32[32]{0:T(128)} %two_ref.1, s32[32]{0:T(128)} %three_ref.1, bf16[192,2048]{1,0:T(8,128)(2,1)} %q_ref.2, bf16[192,2048]{1,0:T(8,128)(2,1)} %k_ref.3, bf16[192,2048]{1,0:T(8,128)(2,1)} %v_ref.3), custom_call_target="tpu_custom_call" | custom-call | flops 1000000000 | bytes 4000000 | tf_op jit(solution)/shard_map/pick/pallas_call | solution.py:94
  21.7 0.6 collective-permute-done
  22.3 0.7 pad_maximum_fusion.1
  23.1 13.2 %all-to-all-start = ((bf16[64,48,128]{2,1,0:T(8,128)(2,1)}), bf16[64,48,128]{2,1,0:T(8,128)(2,1)S(1)}, u32[]{:S(2)}, u32[]{:S(2)}) async-start(bf16[64,48,128]{2,1,0:T(8,128)(2,1)} %bitcast.23), calls=%async_computation | async-start | bytes 1572864 | tf_op jit(solution)/shard_map/all_to_all | solution.py:368
  36.3 6.0 %pack.1 = (bf16[8,192,640]{2,1,0:T(8,128)(2,1)}, bf16[8,192,128]{2,1,0:T(8,128)(2,1)}) custom-call(bf16[192,2048]{1,0:T(8,128)(2,1)} %q_ref.2, bf16[192,2048]{1,0:T(8,128)(2,1)} %k_ref.3, bf16[192,2048]{1,0:T(8,128)(2,1)} %v_ref.3), custom_call_target="tpu_custom_call" | custom-call | bytes 5000000 | tf_op jit(solution)/shard_map/pack/pallas_call | solution.py:118
  42.3 16.9 %all-to-all-done = bf16[64,48,128]{2,1,0:T(8,128)(2,1)S(1)} async-done(((bf16[64,48,128]{2,1,0:T(8,128)(2,1)}), bf16[64,48,128]{2,1,0:T(8,128)(2,1)S(1)}, u32[]{:S(2)}, u32[]{:S(2)}) %all-to-all-start) | async-done | bytes 786464 | tf_op jit(solution)/shard_map/all_to_all | solution.py:368
  59.2 5.9 %all-to-all-start.1 = ((bf16[8,192,640]{2,1,0:T(8,128)(2,1)}), bf16[8,192,640]{2,1,0:T(8,128)(2,1)S(1)}, u32[]{:S(2)}, u32[]{:S(2)}) async-start(bf16[8,192,640]{2,1,0:T(8,128)(2,1)} %get-tuple-element.19), calls=%async_computation.1 | async-start | bytes 3932160 | tf_op jit(solution)/shard_map/all_to_all | solution.py:372
  65.4 0.4 compact_three.1
  65.8 21.9 %all_gather.6.far_ref = bf16[1536,128]{1,0:T(8,128)(2,1)S(1)} all-gather(bf16[192,128]{1,0:T(8,128)(2,1)S(1)} %compact_three.1), channel_id=1, replica_groups=mesh['zl'=4,'core'=2,'y'=8,'zh'=2,'x'=4] {'y'}, dimensions={0}, use_global_device_ids=true | all-gather | bytes 442368 | tf_op jit(solution)/shard_map/all_gather | solution.py:373
  87.7 4.0 %sparse_levels.1 = bf16[4,8,32,128]{3,2,1,0:T(8,128)(2,1)S(1)} custom-call(s32[2]{0:T(128)S(1)} %pad_add_fusion.1.place_ref, bf16[32,2,48,128]{3,2,1,0:T(8,128)(2,1)S(1)} %bitcast.18, bf16[1536,128]{1,0:T(8,128)(2,1)S(1)} %all_gather.6.far_ref), custom_call_target="tpu_custom_call" | custom-call | flops 4000000000 | bytes 2000000 | tf_op jit(solution)/shard_map/sparse_levels/pallas_call | solution.py:191
  91.7 1.9 %collective-permute-start.3 = (bf16[8,32,128]{2,1,0:T(8,128)(2,1)S(1)}, bf16[8,32,128]{2,1,0:T(8,128)(2,1)S(1)}, u32[]{:S(2)}, u32[]{:S(2)}) collective-permute-start(bf16[8,32,128]{2,1,0:T(8,128)(2,1)S(1)} %get-tuple-element.28), channel_id=1, source_target_pairs={{0,3},{1,0},{2,1},{3,2},{4,7},{5,4},{6,5},{7,6},{8,11},{9,8},{10,9... | collective-permute-start | bytes 196616 | tf_op jit(solution)/shard_map/ppermute | solution.py:349
  93.6 2.1 %collective-permute-start.2 = (bf16[8,32,128]{2,1,0:T(8,128)(2,1)S(1)}, bf16[8,32,128]{2,1,0:T(8,128)(2,1)S(1)}, u32[]{:S(2)}, u32[]{:S(2)}) collective-permute-start(bf16[8,32,128]{2,1,0:T(8,128)(2,1)S(1)} %get-tuple-element.29), channel_id=1, source_target_pairs={{0,2},{1,3},{2,0},{3,1},{4,6},{5,7},{6,4},{7,5},{8,10},{9,11},{10,... | collective-permute-start | bytes 196616 | tf_op jit(solution)/shard_map/ppermute | solution.py:349
  95.7 3.1 %collective-permute-start.1 = (bf16[8,32,128]{2,1,0:T(8,128)(2,1)S(1)}, bf16[8,32,128]{2,1,0:T(8,128)(2,1)S(1)}, u32[]{:S(2)}, u32[]{:S(2)}) collective-permute-start(bf16[8,32,128]{2,1,0:T(8,128)(2,1)S(1)} %get-tuple-element.30), channel_id=1, source_target_pairs={{0,1},{1,2},{2,3},{3,0},{4,5},{5,6},{6,7},{7,4},{8,9},{9,10},{10,1... | collective-permute-start | bytes 196616 | tf_op jit(solution)/shard_map/ppermute | solution.py:349
  98.9 0.1 pad_add_fusion.scalar_ref
  99.0 2.6 %collective-permute-done.2 = bf16[8,32,128]{2,1,0:T(8,128)(2,1)S(1)} collective-permute-done((bf16[8,32,128]{2,1,0:T(8,128)(2,1)S(1)}, bf16[8,32,128]{2,1,0:T(8,128)(2,1)S(1)}, u32[]{:S(2)}, u32[]{:S(2)}) %collective-permute-start.2) | collective-permute-done | bytes 65568 | tf_op jit(solution)/shard_map/ppermute | solution.py:349
  101.5 3.2 %collective-permute-done.1 = bf16[8,32,128]{2,1,0:T(8,128)(2,1)S(1)} collective-permute-done((bf16[8,32,128]{2,1,0:T(8,128)(2,1)S(1)}, bf16[8,32,128]{2,1,0:T(8,128)(2,1)S(1)}, u32[]{:S(2)}, u32[]{:S(2)}) %collective-permute-start.1) | collective-permute-done | bytes 65568 | tf_op jit(solution)/shard_map/ppermute | solution.py:349
  104.7 6.0 %all-to-all-done.1 = bf16[8,192,640]{2,1,0:T(8,128)(2,1)S(1)} async-done(((bf16[8,192,640]{2,1,0:T(8,128)(2,1)}), bf16[8,192,640]{2,1,0:T(8,128)(2,1)S(1)}, u32[]{:S(2)}, u32[]{:S(2)}) %all-to-all-start.1) | async-done | bytes 1966112 | tf_op jit(solution)/shard_map/all_to_all | solution.py:372
  110.7 5.5 %all-to-all-start.2 = ((bf16[8,192,128]{2,1,0:T(8,128)(2,1)}), bf16[8,192,128]{2,1,0:T(8,128)(2,1)S(1)}, u32[]{:S(2)}, u32[]{:S(2)}) async-start(bf16[8,192,128]{2,1,0:T(8,128)(2,1)} %get-tuple-element.21), calls=%async_computation.2 | async-start | bytes 786432 | tf_op jit(solution)/shard_map/all_to_all | solution.py:376
  116.2 8.7 %dense_level.2 = bf16[1536,128]{1,0:T(8,128)(2,1)} custom-call(s32[9]{0:T(128)S(1)} %pad_add_fusion.scalar_ref, bf16[1536,640]{1,0:T(8,128)(2,1)S(1)} %bitcast.19, bf16[1536,640]{1,0:T(8,128)(2,1)S(1)} %bitcast.20, bf16[4,8,32,128]{3,2,1,0:T(8,128)(2,1)S(1)} %pad_maximum_fusion.back_ref), custom_call_target="tpu_custom_call" | custom-call | flops 10000000000 | bytes 2000000 | tf_op jit(solution)/shard_map/dense_level/pallas_call | solution.py:267
  124.9 3.0 %all-to-all-done.2 = bf16[8,192,128]{2,1,0:T(8,128)(2,1)S(1)} async-done(((bf16[8,192,128]{2,1,0:T(8,128)(2,1)}), bf16[8,192,128]{2,1,0:T(8,128)(2,1)S(1)}, u32[]{:S(2)}, u32[]{:S(2)}) %all-to-all-start.2) | async-done | bytes 393248 | tf_op jit(solution)/shard_map/all_to_all | solution.py:376
  127.9 4.2 %all-to-all-start.3 = ((bf16[8,192,128]{2,1,0:T(8,128)(2,1)}), bf16[8,192,128]{2,1,0:T(8,128)(2,1)S(1)}, u32[]{:S(2)}, u32[]{:S(2)}) async-start(bf16[8,192,128]{2,1,0:T(8,128)(2,1)} %bitcast.12), calls=%async_computation.3 | async-start | bytes 786432 | tf_op jit(solution)/shard_map/all_to_all | solution.py:379
  132.1 8.8 %dense_level.3 = bf16[1536,128]{1,0:T(8,128)(2,1)} custom-call(s32[9]{0:T(128)S(1)} %pad_add_fusion.scalar_ref, bf16[1536,128]{1,0:T(8,128)(2,1)S(1)} %bitcast.22, bf16[1536,640]{1,0:T(8,128)(2,1)S(1)} %bitcast.21, bf16[4,8,32,128]{3,2,1,0:T(8,128)(2,1)S(1)} %pad_maximum_fusion.back_ref), custom_call_target="tpu_custom_call" | custom-call | flops 10000000000 | bytes 2000000 | tf_op jit(solution)/shard_map/dense_level/pallas_call | solution.py:267
  140.9 2.9 %all-to-all-done.3.att_ref = bf16[8,192,128]{2,1,0:T(8,128)(2,1)S(1)} async-done(((bf16[8,192,128]{2,1,0:T(8,128)(2,1)}), bf16[8,192,128]{2,1,0:T(8,128)(2,1)S(1)}, u32[]{:S(2)}, u32[]{:S(2)}) %all-to-all-start.3) | async-done | bytes 393248 | tf_op jit(solution)/shard_map/all_to_all | solution.py:379
  143.8 4.2 %all-to-all-start.4 = ((bf16[8,192,128]{2,1,0:T(8,128)(2,1)}), bf16[8,192,128]{2,1,0:T(8,128)(2,1)S(1)}, u32[]{:S(2)}, u32[]{:S(2)}) async-start(bf16[8,192,128]{2,1,0:T(8,128)(2,1)} %bitcast.13), calls=%async_computation.4 | async-start | bytes 786432 | tf_op jit(solution)/shard_map/all_to_all | solution.py:381
  148.1 3.4 %copy-done = bf16[2048,2048]{1,0:T(8,128)(2,1)S(1)} copy-done((bf16[2048,2048]{1,0:T(8,128)(2,1)S(1)}, bf16[2048,2048]{1,0:T(8,128)(2,1)}, u32[]{:S(2)}) %copy-start) | copy-done | bytes 8388632
  151.4 1.5 project_first.1
  153.0 1.9 %copy-done.1 = bf16[1024,2048]{1,0:T(8,128)(2,1)} copy-done((bf16[1024,2048]{1,0:T(8,128)(2,1)}, bf16[1024,2048]{1,0:T(8,128)(2,1)S(1)}, u32[]{:S(2)}) %copy-start.1) | copy-done | bytes 4194328
  154.9 1.2 copy-done.2
  156.1 3.7 %all-to-all-done.4.att_ref = bf16[8,192,128]{2,1,0:T(8,128)(2,1)S(1)} async-done(((bf16[8,192,128]{2,1,0:T(8,128)(2,1)}), bf16[8,192,128]{2,1,0:T(8,128)(2,1)S(1)}, u32[]{:S(2)}, u32[]{:S(2)}) %all-to-all-start.4) | async-done | bytes 393248 | tf_op jit(solution)/shard_map/all_to_all | solution.py:381
  159.8 0.8 copy-done.3
  160.5 5.0 %project_second.1 = bf16[192,2048]{1,0:T(8,128)(2,1)} custom-call(f32[192,2048]{1,0:T(8,128)} %copy-done.2, bf16[8,192,128]{2,1,0:T(8,128)(2,1)} %copy-done.3, bf16[1024,2048]{1,0:T(8,128)(2,1)} %copy-done.1), custom_call_target="tpu_custom_call" | custom-call | flops 805306368 | bytes 6000000 | tf_op jit(solution)/shard_map/project_second/pallas_call | solution.py:331
  (19 shorter events, 0.3 us)
Async XLA Ops:
  6.5 15.8 %copy-start.4 = (bf16[32,2048]{1,0:T(8,128)(2,1)S(1)}, bf16[32,2048]{1,0:T(8,128)(2,1)}, u32[]{:S(2)}) copy-start(bf16[32,2048]{1,0:T(8,128)(2,1)} %param.11) | copy-start | bytes 393220
  6.5 141.5 %all-gather.2.cloned.1.call-start = ((), (), s32[]{:S(2)}) async-start(), calls=%async_computation.5 | async-start | bytes 8650752 | tf_op jit(solution)/shard_map/all_gather | solution.py:367
  6.5 15.8 %collective-permute-start = (bf16[32,2048]{1,0:T(8,128)(2,1)}, bf16[32,2048]{1,0:T(8,128)(2,1)S(1)}, u32[]{:S(2)}, u32[]{:S(2)}) collective-permute-start(bf16[32,2048]{1,0:T(8,128)(2,1)} %param.11), channel_id=1, source_target_pairs={{0,4},{4,0},{1,5},{5,1},{2,6},{6,2},{3,7},{7,3},{8,12},{12,8},{9,1... | collective-permute-start | bytes 393224 | tf_op jit(solution)/shard_map/ppermute | solution.py:349
  23.1 36.1 %all-to-all-start = ((bf16[64,48,128]{2,1,0:T(8,128)(2,1)}), bf16[64,48,128]{2,1,0:T(8,128)(2,1)S(1)}, u32[]{:S(2)}, u32[]{:S(2)}) async-start(bf16[64,48,128]{2,1,0:T(8,128)(2,1)} %bitcast.23), calls=%async_computation | async-start | bytes 1572864 | tf_op jit(solution)/shard_map/all_to_all | solution.py:368
  59.2 5.9 %copy-start.5 = (s32[32]{0:T(128)S(1)}, s32[32]{0:T(128)}, u32[]{:S(2)}) copy-start(s32[32]{0:T(128)} %two_ref.1) | copy-start | bytes 388
  59.2 6.0 %copy-start.6 = (s32[32]{0:T(128)S(1)}, s32[32]{0:T(128)}, u32[]{:S(2)}) copy-start(s32[32]{0:T(128)} %three_ref.1) | copy-start | bytes 388
  59.2 51.5 %all-to-all-start.1 = ((bf16[8,192,640]{2,1,0:T(8,128)(2,1)}), bf16[8,192,640]{2,1,0:T(8,128)(2,1)S(1)}, u32[]{:S(2)}, u32[]{:S(2)}) async-start(bf16[8,192,640]{2,1,0:T(8,128)(2,1)} %get-tuple-element.19), calls=%async_computation.1 | async-start | bytes 3932160 | tf_op jit(solution)/shard_map/all_to_all | solution.py:372
  91.7 7.3 %collective-permute-start.3 = (bf16[8,32,128]{2,1,0:T(8,128)(2,1)S(1)}, bf16[8,32,128]{2,1,0:T(8,128)(2,1)S(1)}, u32[]{:S(2)}, u32[]{:S(2)}) collective-permute-start(bf16[8,32,128]{2,1,0:T(8,128)(2,1)S(1)} %get-tuple-element.28), channel_id=1, source_target_pairs={{0,3},{1,0},{2,1},{3,2},{4,7},{5,4},{6,5},{7,6},{8,11},{9,8},{10,9... | collective-permute-start | bytes 196616 | tf_op jit(solution)/shard_map/ppermute | solution.py:349
  93.6 7.9 %collective-permute-start.2 = (bf16[8,32,128]{2,1,0:T(8,128)(2,1)S(1)}, bf16[8,32,128]{2,1,0:T(8,128)(2,1)S(1)}, u32[]{:S(2)}, u32[]{:S(2)}) collective-permute-start(bf16[8,32,128]{2,1,0:T(8,128)(2,1)S(1)} %get-tuple-element.29), channel_id=1, source_target_pairs={{0,2},{1,3},{2,0},{3,1},{4,6},{5,7},{6,4},{7,5},{8,10},{9,11},{10,... | collective-permute-start | bytes 196616 | tf_op jit(solution)/shard_map/ppermute | solution.py:349
  95.7 8.9 %collective-permute-start.1 = (bf16[8,32,128]{2,1,0:T(8,128)(2,1)S(1)}, bf16[8,32,128]{2,1,0:T(8,128)(2,1)S(1)}, u32[]{:S(2)}, u32[]{:S(2)}) collective-permute-start(bf16[8,32,128]{2,1,0:T(8,128)(2,1)S(1)} %get-tuple-element.30), channel_id=1, source_target_pairs={{0,1},{1,2},{2,3},{3,0},{4,5},{5,6},{6,7},{7,4},{8,9},{9,10},{10,1... | collective-permute-start | bytes 196616 | tf_op jit(solution)/shard_map/ppermute | solution.py:349
  110.7 17.2 %all-to-all-start.2 = ((bf16[8,192,128]{2,1,0:T(8,128)(2,1)}), bf16[8,192,128]{2,1,0:T(8,128)(2,1)S(1)}, u32[]{:S(2)}, u32[]{:S(2)}) async-start(bf16[8,192,128]{2,1,0:T(8,128)(2,1)} %get-tuple-element.21), calls=%async_computation.2 | async-start | bytes 786432 | tf_op jit(solution)/shard_map/all_to_all | solution.py:376
  127.9 15.9 %all-to-all-start.3 = ((bf16[8,192,128]{2,1,0:T(8,128)(2,1)}), bf16[8,192,128]{2,1,0:T(8,128)(2,1)S(1)}, u32[]{:S(2)}, u32[]{:S(2)}) async-start(bf16[8,192,128]{2,1,0:T(8,128)(2,1)} %bitcast.12), calls=%async_computation.3 | async-start | bytes 786432 | tf_op jit(solution)/shard_map/all_to_all | solution.py:379
  143.8 15.9 %all-to-all-start.4 = ((bf16[8,192,128]{2,1,0:T(8,128)(2,1)}), bf16[8,192,128]{2,1,0:T(8,128)(2,1)S(1)}, u32[]{:S(2)}, u32[]{:S(2)}) async-start(bf16[8,192,128]{2,1,0:T(8,128)(2,1)} %bitcast.13), calls=%async_computation.4 | async-start | bytes 786432 | tf_op jit(solution)/shard_map/all_to_all | solution.py:381
  148.1 3.4 %copy-start = (bf16[2048,2048]{1,0:T(8,128)(2,1)S(1)}, bf16[2048,2048]{1,0:T(8,128)(2,1)}, u32[]{:S(2)}) copy-start(bf16[2048,2048]{1,0:T(8,128)(2,1)} %all-gather.2.cloned.1.call-done.w_ref) | copy-start | bytes 25165828
  153.0 1.9 %copy-start.1 = (bf16[1024,2048]{1,0:T(8,128)(2,1)}, bf16[1024,2048]{1,0:T(8,128)(2,1)S(1)}, u32[]{:S(2)}) copy-start(bf16[1024,2048]{1,0:T(8,128)(2,1)S(1)} %get-tuple-element.26.w_ref) | copy-start | bytes 12582916
  154.9 1.2 copy-start.2
  159.8 0.8 copy-start.3
Sparse Core Ops, SparseCore 0:
  23.2 109.5 all-gather.1
